TPU v7x, 128 devices: a whole 4x4x4 slice. The times are simulated.
128 devices in a mesh: cmp: 32 (over y, x, core), off: 4 (over z).
Axes of the slice: x: 4, y: 4, z: 4, core: 2. Of those that a mesh axis runs over, the one named last changes fastest.
Arguments:
- traces: bfloat16 [32768, 2048], P(('cmp', 'off')), may hold values from -6 to 6
- shot_id: int32 [32768], P(('cmp', 'off')), may hold values from 0 to 255, as said below
- receiver_id: int32 [32768], P(('cmp', 'off')), may hold values from 0 to 1023
- cmp_bin: int32 [32768], P(('cmp', 'off')), may hold values from 0 to 511, as said below
- offset_class: int32 [32768], P(('cmp', 'off')), may hold values from 0 to 3, as said below
- shift_int: int32 [32768], P(('cmp', 'off')), may hold values from -8 to 8
- frac_index: int32 [32768], P(('cmp', 'off')), may hold values from 0 to 31
- damping_table: float32 [8], replicated, may hold values from 0.1 to 3
- damping_index: int32 [2], replicated, may hold values from 0 to 7
Outputs:
- shot_static: float32 [256], replicated
- receiver_static: float32 [1024], replicated
- pilot: bfloat16 [512, 2048], P('cmp')
Inputs may be any that keep to these rules, and one draw needn't show every extreme that they name: Each device holds the traces of its own shots: shot_id // 2 equals the trace's row // 256. Call the owner of a trace the pair (cmp_bin // 16, offset_class). Among the 256 traces of one device, at most 4 have the same owner; on every device some owners have exactly 4, and some owners receive exactly 4 traces from every device. See the promise above on owners, which ties cmp_bin and offset_class together.
All inputs are finite; a program needn't handle non-finite values.
Results may differ from a plain program's by a relative error of at most 0.0054.
Values may be sent and summed in bfloat16 or wider, within the bound.
No kernel may reach another device: no remote copies, remote signals or barrier semaphores. Data moves between devices by JAX's collectives and lax.ppermute only.
A program may use at most 64 MiB of HBM per device.

v0:
```python
import jax
import jax.numpy as jnp
from jax import lax
from jax.sharding import PartitionSpec as P

LAGS = 101
TAPS = 16
NPHASE = 32
SHIFT_MAX = 8
ITERS = 2
NTAB = 8
FOLD = 64
SHOT_DEV = 2
REC_DEV = 8


BETA = 24.0
EPS = 1e-06


def fir_taps(frac_total):
    tap_pos = jnp.arange(TAPS, dtype=jnp.float32) - (TAPS // 2 - 1)
    offset = tap_pos - frac_total[..., None]
    return jnp.sinc(offset) * (0.5 + 0.5 * jnp.cos(jnp.pi * offset / (TAPS // 2)))


def spread_taps(taps_now, shifts):
    reach_all = TAPS + 2 * SHIFT_MAX
    targets = jnp.arange(reach_all, dtype=jnp.int32) - (TAPS // 2 - 1) - SHIFT_MAX
    landing = shifts[..., None] + jnp.arange(TAPS, dtype=jnp.int32) - (TAPS // 2 - 1)
    matches = landing[..., None, :] == targets[:, None]
    return jnp.sum(jnp.where(matches, taps_now[..., None, :], 0.0), axis=-1)


def shift_traces(raw_rows, shifts, frac_total):
    kernel = spread_taps(fir_taps(frac_total), shifts)
    samples = raw_rows.shape[-1]
    widths = [(0, 0)] * (raw_rows.ndim - 1) + [(TAPS // 2 - 1 + SHIFT_MAX, TAPS // 2 + SHIFT_MAX)]
    padded = jnp.pad(raw_rows, widths)
    accumulated = jnp.zeros(raw_rows.shape, jnp.float32)
    for offset in range(TAPS + 2 * SHIFT_MAX):
        accumulated = accumulated + kernel[..., offset, None] * padded[
            ..., offset : offset + samples
        ].astype(jnp.float32)
    return accumulated.astype(jnp.bfloat16)


def on_device(
    traces,
    shot_id,
    receiver_id,
    cmp_bin,
    offset_class,
    shift_int,
    frac_index,
    damping_table,
    damping_index,
):
    cmp_count = lax.axis_size("cmp")
    off_count = lax.axis_size("off")
    devices = cmp_count * off_count
    tr_dev, samples = traces.shape
    capacity = 2 * tr_dev // devices
    total_slot_count = devices * capacity
    bins_dev = tr_dev * off_count // FOLD
    shot_total = SHOT_DEV * devices
    rec_total = REC_DEV * devices
    half_lag = LAGS // 2
    highest = lax.Precision.HIGHEST
    unit_rows = jnp.ones((tr_dev,), jnp.float32)
    shot_fold, rec_fold = lax.psum(
        (
            jax.ops.segment_sum(unit_rows, shot_id, shot_total),
            jax.ops.segment_sum(unit_rows, receiver_id, rec_total),
        ),
        ("cmp", "off"),
    )
    destination = cmp_bin // bins_dev * off_count + offset_class
    sort_order = jnp.argsort(destination, stable=True)
    dest_sorted = destination[sort_order]
    starts = jnp.searchsorted(dest_sorted, jnp.arange(devices, dtype=jnp.int32))
    slot_place = dest_sorted * capacity + jnp.arange(tr_dev, dtype=jnp.int32) - starts[dest_sorted]
    source_row = jnp.full((total_slot_count,), tr_dev, jnp.int32).at[slot_place].set(sort_order)
    filled = source_row < tr_dev
    picked = jnp.minimum(source_row, tr_dev - 1)
    outgoing = jnp.where(filled[:, None], traces[picked], jnp.zeros((), traces.dtype)).reshape(
        devices, capacity, samples
    )
    header = jnp.stack(
        [
            shot_id[picked],
            receiver_id[picked],
            (cmp_bin % bins_dev)[picked],
            shift_int[picked],
            frac_index[picked],
            filled.astype(jnp.int32),
        ],
        axis=-1,
    ).reshape(devices, capacity, 6)
    first_pass = None
    arrived, header_in = (
        lax.all_to_all(outgoing, ("cmp", "off"), split_axis=0, concat_axis=0, tiled=True),
        lax.all_to_all(header, ("cmp", "off"), split_axis=0, concat_axis=0, tiled=True),
    )
    raw_slots = arrived.reshape(total_slot_count, samples)
    header_rows = header_in.reshape(total_slot_count, 6)
    slot_shot = header_rows[:, 0]
    slot_rec = header_rows[:, 1]
    slot_bin = header_rows[:, 2]
    slot_shift = header_rows[:, 3]
    slot_frac = header_rows[:, 4]
    live_mask = header_rows[:, 5].astype(jnp.float32)
    bin_mask = jnp.where(
        slot_bin[:, None] == jnp.arange(bins_dev, dtype=jnp.int32), live_mask[:, None], 0.0
    )
    bin_mask_half = bin_mask.astype(jnp.bfloat16)
    shot_table = (slot_shot[:, None] == jnp.arange(shot_total, dtype=jnp.int32)).astype(jnp.float32)
    rec_table = (slot_rec[:, None] == jnp.arange(rec_total, dtype=jnp.int32)).astype(jnp.float32)
    off_weight = 1.0 / (1.0 + lax.axis_index("off").astype(jnp.float32))
    frac_base = slot_frac.astype(jnp.float32) / NPHASE
    lag_values = jnp.arange(LAGS, dtype=jnp.float32) - half_lag
    shot_static = jnp.zeros((shot_total,), jnp.float32)
    receiver_static = jnp.zeros((rec_total,), jnp.float32)
    pilot = None
    for iteration in range(ITERS):
        damping = jnp.sum(
            jnp.where(
                jnp.arange(NTAB, dtype=jnp.int32) == damping_index[iteration], damping_table, 0.0
            )
        )
        frac_total = (
            frac_base
            + jnp.dot(shot_table, shot_static, precision=highest)
            + jnp.dot(rec_table, receiver_static, precision=highest)
        )
        shifted = shift_traces(raw_slots, slot_shift, frac_total)
        partial_value = off_weight * jnp.einsum(
            "tb,tn->bn", bin_mask_half, shifted, preferred_element_type=jnp.float32
        )
        weight_part = off_weight * jnp.sum(bin_mask, axis=0)
        stacked, weight_sum = lax.psum((partial_value, weight_part), "off")
        pilot = (stacked * lax.rsqrt(weight_sum + 1.0)[:, None]).astype(jnp.bfloat16)
        pilot_wide = pilot.astype(jnp.float32)
        pilot_scale = lax.rsqrt(jnp.sum(pilot_wide * pilot_wide, axis=1) + EPS)
        slot_pilot_scale = jnp.dot(bin_mask, pilot_scale, precision=highest)
        pilot_padded = jnp.pad(pilot, ((0, 0), (half_lag, half_lag)))
        lag_table = jnp.stack(
            [pilot_padded[:, lag_index : lag_index + samples] for lag_index in range(LAGS)], axis=1
        )
        every_bin = jnp.einsum(
            "tn,bln->tbl", shifted, lag_table, preferred_element_type=jnp.float32
        )
        correlation = jnp.einsum("tb,tbl->tl", bin_mask, every_bin)
        shifted_wide = shifted.astype(jnp.float32)
        trace_scale = lax.rsqrt(jnp.sum(shifted_wide * shifted_wide, axis=1) + EPS)
        ncorr = correlation * (trace_scale * slot_pilot_scale)[:, None]
        exponent = jnp.exp(BETA * ncorr)
        delay_est = jnp.sum(exponent * lag_values, axis=1) / jnp.sum(exponent, axis=1)
        misfit = -delay_est * live_mask
        shot_grad, receiver_grad = lax.psum(
            (
                jnp.dot(misfit, shot_table, precision=highest),
                jnp.dot(misfit, rec_table, precision=highest),
            ),
            ("cmp", "off"),
        )
        shot_static = shot_static + shot_grad / ((1.0 + damping) * shot_fold + damping)
        receiver_static = receiver_static + receiver_grad / ((1.0 + damping) * rec_fold + damping)
    return (shot_static, receiver_static, pilot)


def solution(mesh):
    placed = (
        P(("cmp", "off"), None),
        P(("cmp", "off")),
        P(("cmp", "off")),
        P(("cmp", "off")),
        P(("cmp", "off")),
        P(("cmp", "off")),
        P(("cmp", "off")),
        P(),
        P(),
    )
    return jax.shard_map(
        on_device, mesh=mesh, in_specs=placed, out_specs=(P(), P(), P("cmp", None)), check_vma=False
    )
```

profile of v0, /device:TPU:1, one launch (start us, length us, event | category | flops | bytes accessed | tf_op | source)
XLA Modules:
  0.0 444.4 jit_solution(5811955369952620026)
XLA Ops:
  8.0 3.2 sort.17
  13.2 12.0 %while.24 = (s32[]{:T(128)}, u32[128]{0:T(128)S(1)}, u32[128]{0:T(128)S(1)}, s32[256]{0:T(256)S(1)}, s32[]{:T(128)}, /*index=5*/s32[]{:T(128)}, s32[]{}) while((s32[]{:T(128)}, u32[128]{0:T(128)S(1)}, u32[128]{0:T(128)S(1)}, s32[256]{0:T(256)S(1)}, s32[]{:T(128)}, /*index=5*/s32[]{:T(128)}, s32[]{}) %tuple.113), condition=%wide.region_2.0_spmd.clone, body=%wide.region_1.0_spmd.clone.sunk | while | flops 2692 | bytes 10348 | solution.py:81
  28.5 3.6 gather_fusion.3
  32.3 3.5 gather_fusion.4
  35.9 3.5 gather_fusion.5
  39.6 3.5 gather_fusion.6
  43.2 3.5 gather_fusion.7
  48.6 11.5 %all-to-all-start = ((s32[128,4,6]{2,1,0:T(4,128)}), s32[128,4,6]{2,1,0:T(4,128)S(1)}, u32[]{:S(2)}, u32[]{:S(2)}) async-start(s32[128,4,6]{2,1,0:T(4,128)} %copy.24), calls=%async_computation | async-start | bytes 524288 | tf_op jit(solution)/shard_map/all_to_all | solution.py:103
  60.1 2.5 gather_fusion.8
  65.6 3.9 broadcast_select_fusion.2
  76.8 10.2 %all-to-all-start.1 = ((bf16[128,4,2048]{2,1,0:T(4,128)(2,1)}), bf16[128,4,2048]{2,1,0:T(4,128)(2,1)}, u32[]{:S(2)}, u32[]{:S(2)}) async-start(bf16[128,4,2048]{2,1,0:T(4,128)(2,1)} %broadcast_select_fusion.2), calls=%async_computation.1 | async-start | bytes 4194304 | tf_op jit(solution)/shard_map/all_to_all | solution.py:102
  88.4 15.8 %psum.67 = f32[16]{0:T(128)S(1)} all-reduce(f32[16]{0:T(128)S(1)} %broadcast_multiply_fusion), channel_id=1, replica_groups=mesh['cmp'=32,'off'=4] {'off'}, use_global_device_ids=true, to_apply=%region_7.9 | all-reduce | flops 16 | bytes 128 | tf_op jit(solution)/shard_map/psum | solution.py:141
  106.3 10.9 %all-to-all-done.1 = bf16[128,4,2048]{2,1,0:T(4,128)(2,1)} async-done(((bf16[128,4,2048]{2,1,0:T(4,128)(2,1)}), bf16[128,4,2048]{2,1,0:T(4,128)(2,1)}, u32[]{:S(2)}, u32[]{:S(2)}) %all-to-all-start.1) | async-done | bytes 2097184 | tf_op jit(solution)/shard_map/all_to_all | solution.py:102
  117.3 2.5 reshape.120
  119.8 29.2 %multiply_reduce_fusion.1 = (f32[512]{0:T(512)S(1)}, bf16[512,2048]{1,0:T(8,128)(2,1)}) fusion(f32[512]{0:T(512)S(1)} %bitcast.541, f32[512]{0:T(512)S(1)} %bitcast.542, f32[512]{0:T(512)S(1)} %bitcast.543, f32[512]{0:T(512)S(1)} %bitcast.544, f32[512]{0:T(512)S(1)} %bitcast.545, f32[512]{0:T(512)S(1)} %bitcast.546, f32[512]{0:T(512)S(1)} %bitcast.547, ...), kind=kLoop, calls=%fused_computation.153 | loop fusion | flops 103808512 | bytes 4261888 | tf_op jit(solution)/shard_map/reduce_sum | solution.py:155
  149.0 2.6 convolution_multiply_fusion.1
  152.1 38.1 %all-reduce.8.cloned.1.call-done = f32[16,2048]{1,0:T(8,128)} async-done(((f32[16,2048]{1,0:T(8,128)}), f32[16,2048]{1,0:T(8,128)}) %all-reduce.8.cloned.1.call-update) | async-done | bytes 131088 | tf_op jit(solution)/shard_map/psum | solution.py:141
  200.7 8.2 %multiply_reduce_fusion.3 = f32[512,101]{0,1:T(8,128)S(1)} fusion(f32[512,16]{0,1:T(8,128)S(1)} %get-tuple-element.191, bf16[16,101,2048]{2,0,1:T(8,128)(2,1)S(1)} %constant_dynamic-update-slice_fusion.6, bf16[512,2048]{1,0:T(8,128)(2,1)S(1)} %copy-done.5), kind=kOutput, calls=%fused_computation.155 | convolution fusion | flops 3390600704 | bytes 8955904 | tf_op jit(solution)/shard_map/tn,bln->tbl/dot_general | solution.py:150
  210.3 66.8 %all-reduce.4 = (f32[256]{0:T(256)S(1)}, f32[256]{0:T(256)S(1)}, f32[1024]{0:T(1024)S(1)}, f32[1024]{0:T(1024)S(1)}) all-reduce(f32[256]{0:T(256)S(1)} %bitcast.628, f32[256]{0:T(256)S(1)} %scatter_custom_fusion.1, f32[1024]{0:T(1024)S(1)} %bitcast.607, ...), channel_id=1, replica_groups=mesh['cmp'=32,'off'=4] {'cmp','off'}, use_global_device_ids=true, to_apply=%region_12.14 | all-reduce | flops 2560 | bytes 20480 | tf_op jit(solution)/shard_map/psum | solution.py:160
  280.6 29.2 %multiply_reduce_fusion = (f32[512]{0:T(512)S(1)}, bf16[512,2048]{1,0:T(8,128)(2,1)}) fusion(f32[512]{0:T(512)S(1)} %bitcast.560, f32[512]{0:T(512)S(1)} %bitcast.561, f32[512]{0:T(512)S(1)} %bitcast.562, f32[512]{0:T(512)S(1)} %bitcast.563, f32[512]{0:T(512)S(1)} %bitcast.564, f32[512]{0:T(512)S(1)} %bitcast.565, f32[512]{0:T(512)S(1)} %bitcast.566, ...), kind=kLoop, calls=%fused_computation.152 | loop fusion | flops 103808512 | bytes 4261888 | tf_op jit(solution)/shard_map/reduce_sum | solution.py:155
  309.8 2.6 convolution_multiply_fusion
  313.0 35.4 %all-reduce.10.cloned.1.call-done = f32[16,2048]{1,0:T(8,128)} async-done(((f32[16,2048]{1,0:T(8,128)}), f32[16,2048]{1,0:T(8,128)}) %all-reduce.10.cloned.1.call-update) | async-done | bytes 131088 | tf_op jit(solution)/shard_map/psum | solution.py:141
  358.7 8.2 %multiply_reduce_fusion.2 = f32[512,101]{0,1:T(8,128)S(1)} fusion(f32[512,16]{0,1:T(8,128)S(1)} %get-tuple-element.191, bf16[16,101,2048]{2,0,1:T(8,128)(2,1)S(1)} %constant_dynamic-update-slice_fusion.107, bf16[512,2048]{1,0:T(8,128)(2,1)S(1)} %copy-done.6), kind=kOutput, calls=%fused_computation.154 | convolution fusion | flops 3390600704 | bytes 8955904 | tf_op jit(solution)/shard_map/tn,bln->tbl/dot_general | solution.py:150
  368.3 66.7 %all-reduce.3 = (f32[256]{0:T(256)S(1)}, f32[1024]{0:T(1024)S(1)}) all-reduce(f32[256]{0:T(256)S(1)} %bitcast.629, f32[1024]{0:T(1024)S(1)} %bitcast.605), channel_id=1, replica_groups=mesh['cmp'=32,'off'=4] {'cmp','off'}, use_global_device_ids=true, to_apply=%region_25.27 | all-reduce | flops 1280 | bytes 10240 | tf_op jit(solution)/shard_map/psum | solution.py:160
  (344 shorter events, 61.7 us)
Async XLA Ops:
  7.2 52.9 %copy-start = (bf16[256,2048]{1,0:T(8,128)(2,1)S(1)}, bf16[256,2048]{1,0:T(8,128)(2,1)}, u32[]{:S(2)}) copy-start(bf16[256,2048]{1,0:T(8,128)(2,1)} %param.12) | copy-start | bytes 3145732
  7.2 25.1 %copy-start.3 = (s32[256]{0:T(256)S(1)}, s32[256]{0:T(256)}, u32[]{:S(2)}) copy-start(s32[256]{0:T(256)} %param.14) | copy-start | bytes 3076
  7.2 32.4 %copy-start.1 = (s32[256]{0:T(256)S(1)}, s32[256]{0:T(256)}, u32[]{:S(2)}) copy-start(s32[256]{0:T(256)} %param.17) | copy-start | bytes 3076
  13.1 30.0 %copy-start.2 = (s32[256]{0:T(256)S(1)}, s32[256]{0:T(256)}, u32[]{:S(2)}) copy-start(s32[256]{0:T(256)} %param.18) | copy-start | bytes 3076
  48.6 28.3 %all-to-all-start = ((s32[128,4,6]{2,1,0:T(4,128)}), s32[128,4,6]{2,1,0:T(4,128)S(1)}, u32[]{:S(2)}, u32[]{:S(2)}) async-start(s32[128,4,6]{2,1,0:T(4,128)} %copy.24), calls=%async_computation | async-start | bytes 524288 | tf_op jit(solution)/shard_map/all_to_all | solution.py:103
  60.1 4.9 %copy-start.7 = (s32[2]{0:T(128)S(1)}, s32[2]{0:T(128)}, u32[]{:S(2)}) copy-start(s32[2]{0:T(128)} %param.20) | copy-start | bytes 28
  62.6 6.9 %copy-start.8 = (f32[8]{0:T(128)S(1)}, f32[8]{0:T(128)}, u32[]{:S(2)}) copy-start(f32[8]{0:T(128)} %param.19) | copy-start | bytes 100
  76.8 40.4 %all-to-all-start.1 = ((bf16[128,4,2048]{2,1,0:T(4,128)(2,1)}), bf16[128,4,2048]{2,1,0:T(4,128)(2,1)}, u32[]{:S(2)}, u32[]{:S(2)}) async-start(bf16[128,4,2048]{2,1,0:T(4,128)(2,1)} %broadcast_select_fusion.2), calls=%async_computation.1 | async-start | bytes 4194304 | tf_op jit(solution)/shard_map/all_to_all | solution.py:102
  87.1 103.2 %all-reduce.8.cloned.1.call-start = ((), (), s32[]{:S(2)}) async-start(), calls=%async_computation.2 | async-start | bytes 262144 | tf_op jit(solution)/shard_map/psum | solution.py:141
  151.7 196.7 %all-reduce.10.cloned.1.call-start = ((), (), s32[]{:S(2)}) async-start(), calls=%async_computation.3 | async-start | bytes 262144 | tf_op jit(solution)/shard_map/psum | solution.py:141
  191.4 9.3 %copy-start.5 = (bf16[512,2048]{1,0:T(8,128)(2,1)S(1)}, bf16[512,2048]{1,0:T(8,128)(2,1)}, u32[]{:S(2)}) copy-start(bf16[512,2048]{1,0:T(8,128)(2,1)} %get-tuple-element.114) | copy-start | bytes 6291460
  349.5 9.2 %copy-start.4 = (bf16[16,2048]{1,0:T(8,128)(2,1)}, bf16[16,2048]{1,0:T(8,128)(2,1)S(1)}, u32[]{:S(2)}) copy-start(bf16[16,2048]{1,0:T(8,128)(2,1)S(1)} %get-tuple-element.112) | copy-start | bytes 196612
  349.5 9.2 %copy-start.6 = (bf16[512,2048]{1,0:T(8,128)(2,1)S(1)}, bf16[512,2048]{1,0:T(8,128)(2,1)}, u32[]{:S(2)}) copy-start(bf16[512,2048]{1,0:T(8,128)(2,1)} %get-tuple-element.110) | copy-start | bytes 6291460
Sparse Core Ops, SparseCore 0:
  151.8 38.4 all-reduce.7
  312.5 35.7 all-reduce.9
where the time goes:
time: 453 us; the launch traced here: 444 us
  blocking collectives  149 us (33%)
  waiting for transfers between devices  84.5 us (19%)
  other arithmetic  81.1 us (18%)
  local copies, waits for them, and re-layouts  62.4 us (14%)
  matrix products  27.3 us (6%)
  starting transfers between devices  22.2 us (5%)
  between operations  17.2 us (4%)
    psum x2, blocking collectives, on_device(): lax.psum((jnp.dot(misfit, shot_table, precision=highest), jnp.dot(misfit,...  133 us
    psum x2, waiting for transfers between devices, on_device(): stacked, weight_sum = lax.psum((partial_value, weight_part), 'off')  73.5 us
    reduce_sum x2, other arithmetic, on_device(): trace_scale = lax.rsqrt(jnp.sum(shifted_wide * shifted_wide, axis=1) + EPS)  58.4 us
    unnamed x229, local copies, waits for them, and re-layouts  17.8 us
    dot_general x2, matrix products, on_device(): jnp.einsum('tn,bln->tbl', shifted, lag_table, preferred_element_type=jnp....  16.3 us
    psum x1, blocking collectives, on_device(): stacked, weight_sum = lax.psum((partial_value, weight_part), 'off')  15.8 us
    all_to_all x1, starting transfers between devices, on_device(): lax.all_to_all(header, ('cmp', 'off'), split_axis=0, concat_axis=0, tiled...  11.5 us
    gather x9, local copies, waits for them, and re-layouts, on_device(): starts = jnp.searchsorted(dest_sorted, jnp.arange(devices, dtype=jnp.int32))  11.4 us
  transfers between devices with their start and end apart: 4, of which 3 were waited for; matrix products, arithmetic and copies ran while one was open for 4% of the time, Pallas kernels for 0%

commit v1 on v0

v1 whole, which is shorter than its diff:
```python
import functools

import jax
import jax.numpy as jnp
from jax import lax
from jax.experimental import pallas as pl
from jax.experimental.pallas import tpu as pltpu
from jax.sharding import PartitionSpec as P

NS = 2048
LAGS = 101
HALF = LAGS // 2
TAPS = 16
NPHASE = 32
SHIFT_MAX = 8
CLASSES = 4
TRACE_LIMIT = 4
BIN_DEV = 16
TR_DEV = 256
DEVICES = 128
SLOTS = DEVICES * TRACE_LIMIT
LANES = 128
WIDE = NS + LANES
LROWS = 112
LAG_TOP = 106
BINS_STEP = 4
BETA = 24.0
EPS = 1e-06
F32 = jnp.float32
BF16 = jnp.bfloat16
HEAD = 16

NN = (((1,), (0,)), ((), ()))
NT = (((1,), (1,)), ((), ()))
TN = (((0,), (0,)), ((), ()))


def dot(a, b, dims, precision=None):
    return lax.dot_general(a, b, dims, precision=precision, preferred_element_type=F32)


def iota(shape, axis):
    return lax.broadcasted_iota(jnp.int32, shape, axis)


def pack_kernel(meta_ref, x_ref, out_ref, y_ref):
    meta = meta_ref[...]
    shot, rec, bin_, cls, shift, frac = [meta[i : i + 1, :] for i in range(6)]
    dest = (bin_ // BIN_DEV) * CLASSES + cls
    rows = [
        shot // 128,
        shot % 128,
        rec // 128,
        rec % 128,
        bin_ % BIN_DEV,
        frac,
        jnp.ones_like(shot),
        shift + SHIFT_MAX,
        dest,
    ]
    sub = iota((16, TR_DEV), 0)
    info = jnp.zeros((16, TR_DEV), F32)
    for i, row in enumerate(rows):
        info = jnp.where(sub == i, row.astype(F32), info)
    place = (iota((16, LANES), 1) == iota((16, LANES), 0) + HEAD).astype(F32).astype(BF16)
    cols = dot(info.astype(BF16), place, TN)
    shift_col = cols[:, HEAD + 7 : HEAD + 8].astype(jnp.int32)
    dest_col = cols[:, HEAD + 8 : HEAD + 9]
    same = (dest_col == dest.astype(F32)) & (iota((TR_DEV, TR_DEV), 0) < iota((TR_DEV, TR_DEV), 1))
    rank = jnp.sum(jnp.where(same, 1.0, 0.0), axis=0, keepdims=True).astype(jnp.int32)
    slot = dest * TRACE_LIMIT + rank
    onehot = (iota((SLOTS, TR_DEV), 0) == slot).astype(F32).astype(BF16)
    step = 32
    for r in range(0, TR_DEV, step):
        y = jnp.concatenate([x_ref[r : r + step, :].astype(F32), jnp.zeros((step, LANES), F32)], axis=1)
        y = pltpu.roll(y, SHIFT_MAX, 1)
        amount = shift_col[r : r + step, :]
        for bit in range(5):
            on = ((amount >> bit) & 1) == 1
            y = jnp.where(on, pltpu.roll(y, WIDE - (1 << bit), 1), y)
        y_ref[r : r + step, :NS] = y[:, :NS].astype(BF16)
        y_ref[r : r + step, NS:] = (y[:, NS:] + cols[r : r + step, :]).astype(BF16)
    out_ref[...] = dot(onehot, y_ref[...], NN).astype(BF16)


def spread_slots(y_ref, xt_ref):
    eye = (iota((LANES, LANES), 0) == iota((LANES, LANES), 1)).astype(F32).astype(BF16)
    for c in range(NS // LANES):
        block = dot(eye, y_ref[:, c * LANES : (c + 1) * LANES], NT)
        for q in range(SLOTS // LANES):
            xt_ref[q, 8 + c * LANES : 8 + (c + 1) * LANES, :] = block[:, q * LANES : (q + 1) * LANES]
    block = dot(eye, y_ref[:, NS:], NT)
    for q in range(SLOTS // LANES):
        part = block[:, q * LANES : (q + 1) * LANES]
        xt_ref[q, 0:8, :] = part[120:128, :]
        xt_ref[q, 8 + NS : 16 + NS, :] = part[0:8, :]
    return block[HEAD : HEAD + 16, :]


def one_hot_rows(row, count):
    return (iota((count, SLOTS), 0) == row.astype(jnp.int32)).astype(F32)


def damped(grad_count, damp):
    return grad_count[0:8, :] / ((1.0 + damp) * grad_count[8:16, :] + damp)


def stack_kernel(first, *refs):
    if first:
        weight_ref, y_ref, part_ref, st_ref, side_ref, xt_ref = refs
    else:
        weight_ref, y_ref, rec_ref, shot_ref, part_ref, st_ref, side_ref, xt_ref = refs
    head = spread_slots(y_ref, xt_ref)
    frac = head[5:6, :] * (1.0 / NPHASE)
    live = head[6:7, :]
    if not first:
        for table_ref, at in ((shot_ref, 0), (rec_ref, 2)):
            low = one_hot_rows(head[at + 1 : at + 2, :], 128)
            high = one_hot_rows(head[at : at + 1, :], 8)
            found = dot(table_ref[...], low, NN, lax.Precision.HIGHEST)
            frac = frac + jnp.sum(found * high, axis=0, keepdims=True)
    u = (iota((TAPS, SLOTS), 0) - (TAPS // 2 - 1)).astype(F32) - frac
    angle = jnp.pi * u
    safe = jnp.where(u == 0.0, 1.0, angle)
    sinc = jnp.where(u == 0.0, 1.0, jnp.sin(safe) / safe)
    taps = sinc * (0.5 + 0.5 * jnp.cos(angle * (1.0 / (TAPS // 2))))
    chunk = 16
    energies = []
    for q in range(SLOTS // LANES):
        tap = [jnp.broadcast_to(taps[k : k + 1, q * LANES : (q + 1) * LANES], (8, LANES)) for k in range(TAPS)]

        def body(i, energy):
            base = i * chunk
            halves = []
            for h in range(chunk // 8):
                total = tap[0] * xt_ref[q, pl.ds(base + 8 * h + 1, 8), :]
                for k in range(1, TAPS):
                    total = total + tap[k] * xt_ref[q, pl.ds(base + 8 * h + 1 + k, 8), :]
                halves.append(total)
            rounded = jnp.concatenate(halves, axis=0).astype(BF16)
            st_ref[pl.ds(pl.multiple_of(base, chunk), chunk), q * LANES : (q + 1) * LANES] = rounded
            wide = rounded.astype(F32)
            return energy + wide[0:8, :] * wide[0:8, :] + wide[8:16, :] * wide[8:16, :]

        energy = lax.fori_loop(0, NS // chunk, body, jnp.zeros((8, LANES), F32), unroll=4)
        energies.append(jnp.sum(energy, axis=0, keepdims=True))
    side_ref[0:16, :] = head
    side_ref[16:24, :] = jnp.broadcast_to(jnp.concatenate(energies, axis=1), (8, SLOTS))
    weight = weight_ref[0, 0]
    member = one_hot_rows(head[4:5, :], BIN_DEV) * live
    part_ref[:, :NS] = (weight * dot(member.astype(BF16), st_ref[...], NT)).astype(BF16)
    mass = weight * jnp.sum(member, axis=1, keepdims=True)
    m0 = mass.astype(BF16).astype(F32)
    m1 = (mass - m0).astype(BF16).astype(F32)
    m2 = mass - m0 - m1
    lane = iota((BIN_DEV, LANES), 1)
    tail = jnp.where(lane == 0, m0, jnp.where(lane == 1, m1, jnp.where(lane == 2, m2, 0.0)))
    part_ref[:, NS:] = tail.astype(BF16)


def corr_kernel(first, p0_ref, p1_ref, p2_ref, p3_ref, st_ref, side_ref, pilot_ref, grad_ref, lag_ref, wide_ref):
    total = (p0_ref[...].astype(F32) + p2_ref[...].astype(F32)) + (
        p1_ref[...].astype(F32) + p3_ref[...].astype(F32)
    )
    mass = (total[:, NS : NS + 1] + total[:, NS + 1 : NS + 2]) + total[:, NS + 2 : NS + 3]
    pilot = (total[:, :NS] * lax.rsqrt(mass + 1.0)).astype(BF16)
    pilot_ref[...] = pilot
    wide = pilot.astype(F32)
    wide_ref[:, :NS] = wide
    wide_ref[:, NS:] = jnp.zeros((BIN_DEV, LANES), F32)
    pilot_scale = lax.rsqrt(jnp.sum(wide * wide, axis=1, keepdims=True) + EPS)
    head = side_ref[0:16, :]
    live = head[6:7, :]
    member = one_hot_rows(head[4:5, :], BIN_DEV) * live
    corr = jnp.zeros((LROWS, SLOTS), F32)
    for b0 in range(0, BIN_DEV, BINS_STEP):
        for bb in range(BINS_STEP):
            row = jnp.broadcast_to(wide_ref[b0 + bb : b0 + bb + 1, :], (8, WIDE))
            for g in range(0, LROWS, 16):
                two = [
                    pltpu.roll(row, (WIDE - (LAG_TOP - HALF) + g + h) % WIDE, 1, stride=1, stride_axis=0)[:, :NS]
                    for h in (0, 8)
                ]
                at = (b0 + bb) * LROWS + g
                lag_ref[at : at + 16, :] = jnp.concatenate(two, axis=0).astype(BF16)
        every = dot(lag_ref[b0 * LROWS : (b0 + BINS_STEP) * LROWS, :], st_ref[...], NN)
        for bb in range(BINS_STEP):
            corr = corr + member[b0 + bb : b0 + bb + 1, :] * every[bb * LROWS : (bb + 1) * LROWS, :]
    scale = lax.rsqrt(side_ref[16:17, :] + EPS) * jnp.sum(member * pilot_scale, axis=0, keepdims=True)
    lag = LAG_TOP - iota((LROWS, SLOTS), 0)
    exponent = jnp.where((lag >= 0) & (lag < LAGS), jnp.exp(BETA * (corr * scale)), 0.0)
    delay = jnp.sum(exponent * (lag - HALF).astype(F32), axis=0, keepdims=True) / jnp.sum(
        exponent, axis=0, keepdims=True
    )
    misfit = -delay * live
    for at, out in ((2, 0), (0, 16 if first else 8)):
        low = one_hot_rows(head[at + 1 : at + 2, :], 128)
        high = one_hot_rows(head[at : at + 1, :], 8)
        values = high * misfit
        if first:
            values = jnp.concatenate([values, high * live], axis=0)
        sums = dot(values, low, NT, lax.Precision.HIGHEST)
        grad_ref[out : out + sums.shape[0], :] = sums


VMEM = pl.BlockSpec(memory_space=pltpu.VMEM)
SMEM = pl.BlockSpec(memory_space=pltpu.SMEM)
PARAMS = pltpu.CompilerParams(vmem_limit_bytes=40 * 1024 * 1024)


def shape(dims, dtype):
    return jax.ShapeDtypeStruct(dims, dtype)


def pack(meta, traces):
    return pl.pallas_call(
        pack_kernel,
        out_shape=shape((SLOTS, WIDE), BF16),
        in_specs=[VMEM, VMEM],
        out_specs=VMEM,
        scratch_shapes=[pltpu.VMEM((TR_DEV, WIDE), BF16)],
        compiler_params=PARAMS,
        name="pack",
    )(meta, traces)


def stack(weight, slots, tables):
    first = tables is None
    args = (weight, slots) + (() if first else tables)
    return pl.pallas_call(
        functools.partial(stack_kernel, first),
        out_shape=(shape((BIN_DEV, WIDE), BF16), shape((NS, SLOTS), BF16), shape((24, SLOTS), F32)),
        in_specs=[SMEM] + [VMEM] * (len(args) - 1),
        out_specs=(VMEM, VMEM, VMEM),
        scratch_shapes=[pltpu.VMEM((SLOTS // LANES, NS + 16, LANES), F32)],
        compiler_params=PARAMS,
        name="stack",
    )(*args)


def correlate(first, parts, shifted, side):
    return pl.pallas_call(
        functools.partial(corr_kernel, first),
        out_shape=(shape((BIN_DEV, NS), BF16), shape((32 if first else 16, LANES), F32)),
        in_specs=[VMEM] * 6,
        out_specs=(VMEM, VMEM),
        scratch_shapes=[pltpu.VMEM((BIN_DEV * LROWS, NS), BF16), pltpu.VMEM((BIN_DEV, WIDE), F32)],
        compiler_params=PARAMS,
        name="correlate",
    )(*parts, shifted, side)


def cmp_pairs(move):
    pairs = []
    for y in range(4):
        for x in range(4):
            for c in range(2):
                y2, x2, c2 = move(y, x, c)
                pairs.append(((y * 4 + x) * 2 + c, (y2 * 4 + x2) * 2 + c2))
    return pairs


def ring_sum(value, axis, perms):
    got = [lax.ppermute(value, axis, perm) for perm in perms]
    if len(got) == 1:
        return value + got[0]
    return (value + got[1]) + (got[0] + got[2])


def off_perm(d):
    return [(i, (i + d) % 4) for i in range(4)]


def sum_all(value):
    value = ring_sum(value, "cmp", [cmp_pairs(lambda y, x, c: (y, x, 1 - c))])
    value = ring_sum(value, "cmp", [cmp_pairs(lambda y, x, c, d=d: (y, (x + d) % 4, c)) for d in (1, 2, 3)])
    value = ring_sum(value, "cmp", [cmp_pairs(lambda y, x, c, d=d: ((y + d) % 4, x, c)) for d in (1, 2, 3)])
    return ring_sum(value, "off", [off_perm(d) for d in (1, 2, 3)])


def on_device(
    traces,
    shot_id,
    receiver_id,
    cmp_bin,
    offset_class,
    shift_int,
    frac_index,
    damping_table,
    damping_index,
):
    meta = jnp.stack([shot_id, receiver_id, cmp_bin, offset_class, shift_int, frac_index, frac_index, frac_index])
    outgoing = pack(meta, traces).reshape(DEVICES, TRACE_LIMIT, WIDE)
    arrived = lax.all_to_all(outgoing, ("cmp", "off"), split_axis=0, concat_axis=0, tiled=True)
    slots = arrived.reshape(SLOTS, WIDE)
    weight = (1.0 / (1.0 + lax.axis_index("off").astype(F32))).reshape(1, 1)
    entries = jnp.arange(damping_table.shape[0], dtype=jnp.int32)
    damps = [jnp.sum(jnp.where(entries == damping_index[i], damping_table, 0.0)) for i in range(2)]
    tables = None
    for iteration in range(2):
        first = iteration == 0
        part, shifted, side = stack(weight, slots, tables)
        others = [lax.ppermute(part, "off", off_perm(d)) for d in (1, 2, 3)]
        pilot, sums = correlate(first, (part, *others), shifted, side)
        sums = sum_all(sums)
        damp = damps[iteration]
        if first:
            rec_count, shot_count = sums[8:16], sums[24:32]
            rec = sums[0:8] / ((1.0 + damp) * rec_count + damp)
            shot = sums[16:24] / ((1.0 + damp) * shot_count + damp)
            tables = (rec, shot)
        else:
            rec = rec + sums[0:8] / ((1.0 + damp) * rec_count + damp)
            shot = shot + sums[8:16] / ((1.0 + damp) * shot_count + damp)
    return (shot[0:2].reshape(256), rec.reshape(1024), pilot)


def solution(mesh):
    placed = (
        P(("cmp", "off"), None),
        P(("cmp", "off")),
        P(("cmp", "off")),
        P(("cmp", "off")),
        P(("cmp", "off")),
        P(("cmp", "off")),
        P(("cmp", "off")),
        P(),
        P(),
    )
    return jax.shard_map(
        on_device, mesh=mesh, in_specs=placed, out_specs=(P(), P(), P("cmp", None)), check_vma=False
    )
```

time: 453 us -> 143 us (0.32)
  the two profiles are of different devices: /device:TPU:1 before, /device:TPU:0 now
where the time goes in v1:
time: 143 us
  starting transfers between devices  49 us (34%)
  waiting for transfers between devices  48.8 us (34%)
  Pallas kernels  31.4 us (22%)
  local copies, waits for them, and re-layouts  7.92 us (6%)
  other arithmetic  3.86 us (3%)
  between operations  2.07 us (1%)
    all_to_all x1, waiting for transfers between devices, on_device(): lax.all_to_all(outgoing, ('cmp', 'off'), split_axis=0, concat_axis=0, til...  30.8 us
    ppermute x20, starting transfers between devices, ring_sum(): got = [lax.ppermute(value, axis, perm) for perm in perms]  29.4 us
    pallas_call x2, Pallas kernels, stack(): pl.pallas_call(functools.partial(stack_kernel, first), out_shape=(shape((...  16.4 us
    all_to_all x1, starting transfers between devices, on_device(): lax.all_to_all(outgoing, ('cmp', 'off'), split_axis=0, concat_axis=0, til...  11.6 us
    ppermute x20, waiting for transfers between devices, ring_sum(): got = [lax.ppermute(value, axis, perm) for perm in perms]  10.3 us
    pallas_call x2, Pallas kernels, correlate(): pl.pallas_call(functools.partial(corr_kernel, first), out_shape=(shape((B...  10.3 us
    ppermute x6, starting transfers between devices, on_device(): others = [lax.ppermute(part, 'off', off_perm(d)) for d in (1, 2, 3)]  8 us
    ppermute x6, waiting for transfers between devices, on_device(): others = [lax.ppermute(part, 'off', off_perm(d)) for d in (1, 2, 3)]  7.71 us
  transfers between devices with their start and end apart: 27, of which 17 were waited for; matrix products, arithmetic and copies ran while one was open for 2% of the time, Pallas kernels for 0%

profile of v1, /device:TPU:0, one launch (start us, length us, event | category | flops | bytes accessed | tf_op | source)
XLA Modules:
  0.0 143.1 jit_solution(13895953657369182314)
XLA Ops:
  2.7 4.8 %pack.1 = bf16[512,2176]{1,0:T(8,128)(2,1)S(1)} custom-call(s32[8,256]{1,0:T(8,128)S(1)} %stack.31.meta_ref, bf16[256,2048]{1,0:T(8,128)(2,1)S(1)} %copy-done), custom_call_target="tpu_custom_call" | custom-call | tf_op jit(solution)/shard_map/pack/pallas_call | solution.py:216
  7.5 2.1 %reshape.22 = bf16[128,4,2176]{2,1,0:T(4,128)(2,1)} reshape(bf16[512,2176]{1,0:T(8,128)(2,1)S(1)} %pack.1) | data formatting | bytes 4456448 | tf_op jit(solution)/shard_map/reshape | solution.py:293
  9.6 11.6 %all-to-all-start = ((bf16[128,4,2176]{2,1,0:T(4,128)(2,1)}), bf16[128,4,2176]{2,1,0:T(4,128)(2,1)}, u32[]{:S(2)}, u32[]{:S(2)}) async-start(bf16[128,4,2176]{2,1,0:T(4,128)(2,1)} %reshape.22), calls=%async_computation | async-start | bytes 4456448 | tf_op jit(solution)/shard_map/all_to_all | solution.py:294
  21.3 30.8 %all-to-all-done = bf16[128,4,2176]{2,1,0:T(4,128)(2,1)} async-done(((bf16[128,4,2176]{2,1,0:T(4,128)(2,1)}), bf16[128,4,2176]{2,1,0:T(4,128)(2,1)}, u32[]{:S(2)}, u32[]{:S(2)}) %all-to-all-start) | async-done | bytes 2228256 | tf_op jit(solution)/shard_map/all_to_all | solution.py:294
  52.0 2.6 %reshape.23.refs_1_ = bf16[512,2176]{1,0:T(8,128)(2,1)S(1)} reshape(bf16[128,4,2176]{2,1,0:T(4,128)(2,1)} %all-to-all-done) | data formatting | bytes 4456448 | tf_op jit(solution)/shard_map/reshape | solution.py:295
  54.7 8.0 %stack.32 = (bf16[16,2176]{1,0:T(8,128)(2,1)S(1)}, bf16[2048,512]{1,0:T(8,128)(2,1)S(1)}, f32[24,512]{1,0:T(8,128)S(1)}) custom-call(f32[1,1]{1,0:T(1,128)} %bitcast.refs_0_, bf16[512,2176]{1,0:T(8,128)(2,1)S(1)} %reshape.23.refs_1_), custom_call_target="tpu_custom_call" | custom-call | tf_op jit(solution)/shard_map/stack/pallas_call | solution.py:230
  63.5 1.7 %collective-permute-start.1 = (bf16[16,2176]{1,0:T(8,128)(2,1)S(1)}, bf16[16,2176]{1,0:T(8,128)(2,1)S(1)}, u32[]{:S(2)}, u32[]{:S(2)}) collective-permute-start(bf16[16,2176]{1,0:T(8,128)(2,1)S(1)} %get-tuple-element.12.p0_ref), channel_id=1, source_target_pairs={{0,2},{1,3},{2,0},{3,1},{4,6},{5,7},{6,4},{7,5},{8,10},{9,11},{10,... | collective-permute-start | bytes 208904 | tf_op jit(solution)/shard_map/ppermute | solution.py:303
  66.2 3.4 %collective-permute-done.p1_ref = bf16[16,2176]{1,0:T(8,128)(2,1)S(1)} collective-permute-done((bf16[16,2176]{1,0:T(8,128)(2,1)S(1)}, bf16[16,2176]{1,0:T(8,128)(2,1)S(1)}, u32[]{:S(2)}, u32[]{:S(2)}) %collective-permute-start) | collective-permute-done | bytes 69664 | tf_op jit(solution)/shard_map/ppermute | solution.py:303
  70.2 5.1 %correlate.2 = (bf16[16,2048]{1,0:T(8,128)(2,1)}, f32[32,128]{1,0:T(8,128)S(1)}) custom-call(bf16[16,2176]{1,0:T(8,128)(2,1)S(1)} %get-tuple-element.12.p0_ref, bf16[16,2176]{1,0:T(8,128)(2,1)S(1)} %collective-permute-done.p1_ref, bf16[16,2176]{1,0:T(8,128)(2,1)S(1)} %collective-permute-done.1.p2_ref, bf16[16,2176]{1,0:T(8,128)(2,1)S(1)} %collective-permute-done.2.p3_ref, ...), custom_call_target="tpu_custom_call" | custom-call | tf_op jit(solution)/shard_map/correlate/pallas_call | solution.py:242
  78.5 2.2 %collective-permute-start.6 = (f32[32,128]{1,0:T(8,128)S(1)}, f32[32,128]{1,0:T(8,128)S(1)}, u32[]{:S(2)}, u32[]{:S(2)}) collective-permute-start(f32[32,128]{1,0:T(8,128)S(1)} %add.98), channel_id=1, source_target_pairs={{0,24},{4,28},{8,0},{12,4},{16,8},{20,12},{24,16},{28,20},{32,56},... | collective-permute-start | bytes 49160 | tf_op jit(solution)/shard_map/ppermute | solution.py:264
  84.6 2.2 %collective-permute-start.9 = (f32[32,128]{1,0:T(8,128)S(1)}, f32[32,128]{1,0:T(8,128)S(1)}, u32[]{:S(2)}, u32[]{:S(2)}) collective-permute-start(f32[32,128]{1,0:T(8,128)S(1)} %add_add_fusion.2), channel_id=1, source_target_pairs={{0,96},{4,100},{8,104},{12,108},{16,112},{20,116},{24,120},{28,124... | collective-permute-start | bytes 49160 | tf_op jit(solution)/shard_map/ppermute | solution.py:264
  88.6 1.6 %collective-permute-start.10 = (f32[32,128]{1,0:T(8,128)S(1)}, f32[32,128]{1,0:T(8,128)S(1)}, u32[]{:S(2)}, u32[]{:S(2)}) collective-permute-start(f32[32,128]{1,0:T(8,128)S(1)} %add_add_fusion.1), channel_id=1, source_target_pairs={{0,2},{1,3},{2,0},{3,1},{4,6},{5,7},{6,4},{7,5},{8,10},{9,11},{10,... | collective-permute-start | bytes 49160 | tf_op jit(solution)/shard_map/ppermute | solution.py:264
  90.2 2.0 %collective-permute-start.11 = (f32[32,128]{1,0:T(8,128)S(1)}, f32[32,128]{1,0:T(8,128)S(1)}, u32[]{:S(2)}, u32[]{:S(2)}) collective-permute-start(f32[32,128]{1,0:T(8,128)S(1)} %add_add_fusion.1), channel_id=1, source_target_pairs={{0,1},{1,2},{2,3},{3,0},{4,5},{5,6},{6,7},{7,4},{8,9},{9,10},{10,1... | collective-permute-start | bytes 49160 | tf_op jit(solution)/shard_map/ppermute | solution.py:264
  93.4 2.0 %fusion.4 = (f32[]{:T(128)}, f32[]{:T(128)}) fusion(f32[8]{0:T(128)S(1)} %copy-done.2, s32[]{:T(128)} %bitcast.8, s32[]{:T(128)} %bitcast.7), kind=kLoop, calls=%fused_computation.17 | loop fusion | flops 46 | bytes 48 | tf_op jit(solution)/shard_map/reduce_sum | solution.py:298
  96.6 8.4 %stack.33 = (bf16[16,2176]{1,0:T(8,128)(2,1)S(1)}, bf16[2048,512]{1,0:T(8,128)(2,1)S(1)}, f32[24,512]{1,0:T(8,128)S(1)}) custom-call(f32[1,1]{1,0:T(1,128)} %bitcast.refs_0_, bf16[512,2176]{1,0:T(8,128)(2,1)S(1)} %reshape.23.refs_1_, f32[8,128]{1,0:T(8,128)S(1)} %get-tuple-element.25.refs_2_, f32[8,128]{1,0:T(8,128)S(1)} %get-tuple-element.26.refs_3_), custom_call_target="tpu_custom_call" | custom-call | tf_op jit(solution)/shard_map/stack/pallas_call | solution.py:230
  105.8 3.0 %collective-permute-start.14 = (bf16[16,2176]{1,0:T(8,128)(2,1)S(1)}, bf16[16,2176]{1,0:T(8,128)(2,1)S(1)}, u32[]{:S(2)}, u32[]{:S(2)}) collective-permute-start(bf16[16,2176]{1,0:T(8,128)(2,1)S(1)} %get-tuple-element.16.p0_ref), channel_id=1, source_target_pairs={{0,2},{1,3},{2,0},{3,1},{4,6},{5,7},{6,4},{7,5},{8,10},{9,11},{10,... | collective-permute-start | bytes 208904 | tf_op jit(solution)/shard_map/ppermute | solution.py:303
  113.1 5.1 %correlate.3 = (bf16[16,2048]{1,0:T(8,128)(2,1)}, f32[16,128]{1,0:T(8,128)S(1)}) custom-call(bf16[16,2176]{1,0:T(8,128)(2,1)S(1)} %get-tuple-element.16.p0_ref, bf16[16,2176]{1,0:T(8,128)(2,1)S(1)} %collective-permute-done.13.p1_ref, bf16[16,2176]{1,0:T(8,128)(2,1)S(1)} %collective-permute-done.14.p2_ref, ...), custom_call_target="tpu_custom_call" | custom-call | tf_op jit(solution)/shard_map/correlate/pallas_call | solution.py:242
  119.4 2.3 %collective-permute-start.17 = (f32[16,128]{1,0:T(8,128)S(1)}, f32[16,128]{1,0:T(8,128)S(1)}, u32[]{:S(2)}, u32[]{:S(2)}) collective-permute-start(f32[16,128]{1,0:T(8,128)S(1)} %add.112), channel_id=1, source_target_pairs={{0,16},{4,20},{8,24},{12,28},{16,0},{20,4},{24,8},{28,12},{32,48},... | collective-permute-start | bytes 24584 | tf_op jit(solution)/shard_map/ppermute | solution.py:264
  121.8 1.8 %collective-permute-start.18 = (f32[16,128]{1,0:T(8,128)S(1)}, f32[16,128]{1,0:T(8,128)S(1)}, u32[]{:S(2)}, u32[]{:S(2)}) collective-permute-start(f32[16,128]{1,0:T(8,128)S(1)} %add.112), channel_id=1, source_target_pairs={{0,8},{4,12},{8,16},{12,20},{16,24},{20,28},{24,0},{28,4},{32,40},... | collective-permute-start | bytes 24584 | tf_op jit(solution)/shard_map/ppermute | solution.py:264
  125.0 1.6 %collective-permute-done.18 = f32[16,128]{1,0:T(8,128)S(1)} collective-permute-done((f32[16,128]{1,0:T(8,128)S(1)}, f32[16,128]{1,0:T(8,128)S(1)}, u32[]{:S(2)}, u32[]{:S(2)}) %collective-permute-start.18) | collective-permute-done | bytes 8224 | tf_op jit(solution)/shard_map/ppermute | solution.py:264
  127.2 2.5 %collective-permute-start.20 = (f32[16,128]{1,0:T(8,128)S(1)}, f32[16,128]{1,0:T(8,128)S(1)}, u32[]{:S(2)}, u32[]{:S(2)}) collective-permute-start(f32[16,128]{1,0:T(8,128)S(1)} %add_add_fusion.5), channel_id=1, source_target_pairs={{0,64},{4,68},{8,72},{12,76},{16,80},{20,84},{24,88},{28,92},{32,9... | collective-permute-start | bytes 24584 | tf_op jit(solution)/shard_map/ppermute | solution.py:264
  131.3 1.7 %collective-permute-start.22 = (f32[16,128]{1,0:T(8,128)S(1)}, f32[16,128]{1,0:T(8,128)S(1)}, u32[]{:S(2)}, u32[]{:S(2)}) collective-permute-start(f32[16,128]{1,0:T(8,128)S(1)} %add_add_fusion.5), channel_id=1, source_target_pairs={{0,96},{4,100},{8,104},{12,108},{16,112},{20,116},{24,120},{28,124... | collective-permute-start | bytes 24584 | tf_op jit(solution)/shard_map/ppermute | solution.py:264
  132.9 1.6 %collective-permute-done.21 = f32[16,128]{1,0:T(8,128)S(1)} collective-permute-done((f32[16,128]{1,0:T(8,128)S(1)}, f32[16,128]{1,0:T(8,128)S(1)}, u32[]{:S(2)}, u32[]{:S(2)}) %collective-permute-start.21) | collective-permute-done | bytes 8224 | tf_op jit(solution)/shard_map/ppermute | solution.py:264
  137.6 2.1 %collective-permute-start.25 = (f32[16,128]{1,0:T(8,128)S(1)}, f32[16,128]{1,0:T(8,128)S(1)}, u32[]{:S(2)}, u32[]{:S(2)}) collective-permute-start(f32[16,128]{1,0:T(8,128)S(1)} %add_add_fusion.4), channel_id=1, source_target_pairs={{0,3},{1,0},{2,1},{3,2},{4,7},{5,4},{6,5},{7,6},{8,11},{9,8},{10,9... | collective-permute-start | bytes 24584 | tf_op jit(solution)/shard_map/ppermute | solution.py:264
  (57 shorter events, 30.8 us)
Async XLA Ops:
  9.6 42.5 %all-to-all-start = ((bf16[128,4,2176]{2,1,0:T(4,128)(2,1)}), bf16[128,4,2176]{2,1,0:T(4,128)(2,1)}, u32[]{:S(2)}, u32[]{:S(2)}) async-start(bf16[128,4,2176]{2,1,0:T(4,128)(2,1)} %reshape.22), calls=%async_computation | async-start | bytes 4456448 | tf_op jit(solution)/shard_map/all_to_all | solution.py:294
  62.6 7.0 %collective-permute-start = (bf16[16,2176]{1,0:T(8,128)(2,1)S(1)}, bf16[16,2176]{1,0:T(8,128)(2,1)S(1)}, u32[]{:S(2)}, u32[]{:S(2)}) collective-permute-start(bf16[16,2176]{1,0:T(8,128)(2,1)S(1)} %get-tuple-element.12.p0_ref), channel_id=1, source_target_pairs={{0,1},{1,2},{2,3},{3,0},{4,5},{5,6},{6,7},{7,4},{8,9},{9,10},{10,1... | collective-permute-start | bytes 208904 | tf_op jit(solution)/shard_map/ppermute | solution.py:303
  63.5 6.2 %collective-permute-start.1 = (bf16[16,2176]{1,0:T(8,128)(2,1)S(1)}, bf16[16,2176]{1,0:T(8,128)(2,1)S(1)}, u32[]{:S(2)}, u32[]{:S(2)}) collective-permute-start(bf16[16,2176]{1,0:T(8,128)(2,1)S(1)} %get-tuple-element.12.p0_ref), channel_id=1, source_target_pairs={{0,2},{1,3},{2,0},{3,1},{4,6},{5,7},{6,4},{7,5},{8,10},{9,11},{10,... | collective-permute-start | bytes 208904 | tf_op jit(solution)/shard_map/ppermute | solution.py:303
  65.2 5.0 %collective-permute-start.2 = (bf16[16,2176]{1,0:T(8,128)(2,1)S(1)}, bf16[16,2176]{1,0:T(8,128)(2,1)S(1)}, u32[]{:S(2)}, u32[]{:S(2)}) collective-permute-start(bf16[16,2176]{1,0:T(8,128)(2,1)S(1)} %get-tuple-element.12.p0_ref), channel_id=1, source_target_pairs={{0,3},{1,0},{2,1},{3,2},{4,7},{5,4},{6,5},{7,6},{8,11},{9,8},{10,9... | collective-permute-start | bytes 208904 | tf_op jit(solution)/shard_map/ppermute | solution.py:303
  76.6 5.4 %collective-permute-start.4 = (f32[32,128]{1,0:T(8,128)S(1)}, f32[32,128]{1,0:T(8,128)S(1)}, u32[]{:S(2)}, u32[]{:S(2)}) collective-permute-start(f32[32,128]{1,0:T(8,128)S(1)} %add.98), channel_id=1, source_target_pairs={{0,16},{4,20},{8,24},{12,28},{16,0},{20,4},{24,8},{28,12},{32,48},... | collective-permute-start | bytes 49160 | tf_op jit(solution)/shard_map/ppermute | solution.py:264
  77.5 4.9 %collective-permute-start.5 = (f32[32,128]{1,0:T(8,128)S(1)}, f32[32,128]{1,0:T(8,128)S(1)}, u32[]{:S(2)}, u32[]{:S(2)}) collective-permute-start(f32[32,128]{1,0:T(8,128)S(1)} %add.98), channel_id=1, source_target_pairs={{0,8},{4,12},{8,16},{12,20},{16,24},{20,28},{24,0},{28,4},{32,40},... | collective-permute-start | bytes 49160 | tf_op jit(solution)/shard_map/ppermute | solution.py:264
  78.5 3.9 %collective-permute-start.6 = (f32[32,128]{1,0:T(8,128)S(1)}, f32[32,128]{1,0:T(8,128)S(1)}, u32[]{:S(2)}, u32[]{:S(2)}) collective-permute-start(f32[32,128]{1,0:T(8,128)S(1)} %add.98), channel_id=1, source_target_pairs={{0,24},{4,28},{8,0},{12,4},{16,8},{20,12},{24,16},{28,20},{32,56},... | collective-permute-start | bytes 49160 | tf_op jit(solution)/shard_map/ppermute | solution.py:264
  82.5 5.3 %collective-permute-start.7 = (f32[32,128]{1,0:T(8,128)S(1)}, f32[32,128]{1,0:T(8,128)S(1)}, u32[]{:S(2)}, u32[]{:S(2)}) collective-permute-start(f32[32,128]{1,0:T(8,128)S(1)} %add_add_fusion.2), channel_id=1, source_target_pairs={{0,64},{4,68},{8,72},{12,76},{16,80},{20,84},{24,88},{28,92},{32,9... | collective-permute-start | bytes 49160 | tf_op jit(solution)/shard_map/ppermute | solution.py:264
  83.6 4.9 %collective-permute-start.8 = (f32[32,128]{1,0:T(8,128)S(1)}, f32[32,128]{1,0:T(8,128)S(1)}, u32[]{:S(2)}, u32[]{:S(2)}) collective-permute-start(f32[32,128]{1,0:T(8,128)S(1)} %add_add_fusion.2), channel_id=1, source_target_pairs={{0,32},{4,36},{8,40},{12,44},{16,48},{20,52},{24,56},{28,60},{32,6... | collective-permute-start | bytes 49160 | tf_op jit(solution)/shard_map/ppermute | solution.py:264
  84.6 3.9 %collective-permute-start.9 = (f32[32,128]{1,0:T(8,128)S(1)}, f32[32,128]{1,0:T(8,128)S(1)}, u32[]{:S(2)}, u32[]{:S(2)}) collective-permute-start(f32[32,128]{1,0:T(8,128)S(1)} %add_add_fusion.2), channel_id=1, source_target_pairs={{0,96},{4,100},{8,104},{12,108},{16,112},{20,116},{24,120},{28,124... | collective-permute-start | bytes 49160 | tf_op jit(solution)/shard_map/ppermute | solution.py:264
  88.6 7.4 %collective-permute-start.10 = (f32[32,128]{1,0:T(8,128)S(1)}, f32[32,128]{1,0:T(8,128)S(1)}, u32[]{:S(2)}, u32[]{:S(2)}) collective-permute-start(f32[32,128]{1,0:T(8,128)S(1)} %add_add_fusion.1), channel_id=1, source_target_pairs={{0,2},{1,3},{2,0},{3,1},{4,6},{5,7},{6,4},{7,5},{8,10},{9,11},{10,... | collective-permute-start | bytes 49160 | tf_op jit(solution)/shard_map/ppermute | solution.py:264
  90.2 5.8 %collective-permute-start.11 = (f32[32,128]{1,0:T(8,128)S(1)}, f32[32,128]{1,0:T(8,128)S(1)}, u32[]{:S(2)}, u32[]{:S(2)}) collective-permute-start(f32[32,128]{1,0:T(8,128)S(1)} %add_add_fusion.1), channel_id=1, source_target_pairs={{0,1},{1,2},{2,3},{3,0},{4,5},{5,6},{6,7},{7,4},{8,9},{9,10},{10,1... | collective-permute-start | bytes 49160 | tf_op jit(solution)/shard_map/ppermute | solution.py:264
  92.2 3.8 %collective-permute-start.12 = (f32[32,128]{1,0:T(8,128)S(1)}, f32[32,128]{1,0:T(8,128)S(1)}, u32[]{:S(2)}, u32[]{:S(2)}) collective-permute-start(f32[32,128]{1,0:T(8,128)S(1)} %add_add_fusion.1), channel_id=1, source_target_pairs={{0,3},{1,0},{2,1},{3,2},{4,7},{5,4},{6,5},{7,6},{8,11},{9,8},{10,9... | collective-permute-start | bytes 49160 | tf_op jit(solution)/shard_map/ppermute | solution.py:264
  105.0 5.5 %collective-permute-start.13 = (bf16[16,2176]{1,0:T(8,128)(2,1)S(1)}, bf16[16,2176]{1,0:T(8,128)(2,1)S(1)}, u32[]{:S(2)}, u32[]{:S(2)}) collective-permute-start(bf16[16,2176]{1,0:T(8,128)(2,1)S(1)} %get-tuple-element.16.p0_ref), channel_id=1, source_target_pairs={{0,1},{1,2},{2,3},{3,0},{4,5},{5,6},{6,7},{7,4},{8,9},{9,10},{10,1... | collective-permute-start | bytes 208904 | tf_op jit(solution)/shard_map/ppermute | solution.py:303
  105.8 6.0 %collective-permute-start.14 = (bf16[16,2176]{1,0:T(8,128)(2,1)S(1)}, bf16[16,2176]{1,0:T(8,128)(2,1)S(1)}, u32[]{:S(2)}, u32[]{:S(2)}) collective-permute-start(bf16[16,2176]{1,0:T(8,128)(2,1)S(1)} %get-tuple-element.16.p0_ref), channel_id=1, source_target_pairs={{0,2},{1,3},{2,0},{3,1},{4,6},{5,7},{6,4},{7,5},{8,10},{9,11},{10,... | collective-permute-start | bytes 208904 | tf_op jit(solution)/shard_map/ppermute | solution.py:303
  108.8 4.3 %collective-permute-start.15 = (bf16[16,2176]{1,0:T(8,128)(2,1)S(1)}, bf16[16,2176]{1,0:T(8,128)(2,1)S(1)}, u32[]{:S(2)}, u32[]{:S(2)}) collective-permute-start(bf16[16,2176]{1,0:T(8,128)(2,1)S(1)} %get-tuple-element.16.p0_ref), channel_id=1, source_target_pairs={{0,3},{1,0},{2,1},{3,2},{4,7},{5,4},{6,5},{7,6},{8,11},{9,8},{10,9... | collective-permute-start | bytes 208904 | tf_op jit(solution)/shard_map/ppermute | solution.py:303
  119.4 5.6 %collective-permute-start.17 = (f32[16,128]{1,0:T(8,128)S(1)}, f32[16,128]{1,0:T(8,128)S(1)}, u32[]{:S(2)}, u32[]{:S(2)}) collective-permute-start(f32[16,128]{1,0:T(8,128)S(1)} %add.112), channel_id=1, source_target_pairs={{0,16},{4,20},{8,24},{12,28},{16,0},{20,4},{24,8},{28,12},{32,48},... | collective-permute-start | bytes 24584 | tf_op jit(solution)/shard_map/ppermute | solution.py:264
  121.8 4.9 %collective-permute-start.18 = (f32[16,128]{1,0:T(8,128)S(1)}, f32[16,128]{1,0:T(8,128)S(1)}, u32[]{:S(2)}, u32[]{:S(2)}) collective-permute-start(f32[16,128]{1,0:T(8,128)S(1)} %add.112), channel_id=1, source_target_pairs={{0,8},{4,12},{8,16},{12,20},{16,24},{20,28},{24,0},{28,4},{32,40},... | collective-permute-start | bytes 24584 | tf_op jit(solution)/shard_map/ppermute | solution.py:264
  123.5 3.7 %collective-permute-start.19 = (f32[16,128]{1,0:T(8,128)S(1)}, f32[16,128]{1,0:T(8,128)S(1)}, u32[]{:S(2)}, u32[]{:S(2)}) collective-permute-start(f32[16,128]{1,0:T(8,128)S(1)} %add.112), channel_id=1, source_target_pairs={{0,24},{4,28},{8,0},{12,4},{16,8},{20,12},{24,16},{28,20},{32,56},... | collective-permute-start | bytes 24584 | tf_op jit(solution)/shard_map/ppermute | solution.py:264
  127.2 5.7 %collective-permute-start.20 = (f32[16,128]{1,0:T(8,128)S(1)}, f32[16,128]{1,0:T(8,128)S(1)}, u32[]{:S(2)}, u32[]{:S(2)}) collective-permute-start(f32[16,128]{1,0:T(8,128)S(1)} %add_add_fusion.5), channel_id=1, source_target_pairs={{0,64},{4,68},{8,72},{12,76},{16,80},{20,84},{24,88},{28,92},{32,9... | collective-permute-start | bytes 24584 | tf_op jit(solution)/shard_map/ppermute | solution.py:264
  129.7 4.9 %collective-permute-start.21 = (f32[16,128]{1,0:T(8,128)S(1)}, f32[16,128]{1,0:T(8,128)S(1)}, u32[]{:S(2)}, u32[]{:S(2)}) collective-permute-start(f32[16,128]{1,0:T(8,128)S(1)} %add_add_fusion.5), channel_id=1, source_target_pairs={{0,32},{4,36},{8,40},{12,44},{16,48},{20,52},{24,56},{28,60},{32,6... | collective-permute-start | bytes 24584 | tf_op jit(solution)/shard_map/ppermute | solution.py:264
  134.9 5.4 %collective-permute-start.23 = (f32[16,128]{1,0:T(8,128)S(1)}, f32[16,128]{1,0:T(8,128)S(1)}, u32[]{:S(2)}, u32[]{:S(2)}) collective-permute-start(f32[16,128]{1,0:T(8,128)S(1)} %add_add_fusion.4), channel_id=1, source_target_pairs={{0,2},{1,3},{2,0},{3,1},{4,6},{5,7},{6,4},{7,5},{8,10},{9,11},{10,... | collective-permute-start | bytes 24584 | tf_op jit(solution)/shard_map/ppermute | solution.py:264
  136.4 4.9 %collective-permute-start.24 = (f32[16,128]{1,0:T(8,128)S(1)}, f32[16,128]{1,0:T(8,128)S(1)}, u32[]{:S(2)}, u32[]{:S(2)}) collective-permute-start(f32[16,128]{1,0:T(8,128)S(1)} %add_add_fusion.4), channel_id=1, source_target_pairs={{0,1},{1,2},{2,3},{3,0},{4,5},{5,6},{6,7},{7,4},{8,9},{9,10},{10,1... | collective-permute-start | bytes 24584 | tf_op jit(solution)/shard_map/ppermute | solution.py:264
  137.6 3.7 %collective-permute-start.25 = (f32[16,128]{1,0:T(8,128)S(1)}, f32[16,128]{1,0:T(8,128)S(1)}, u32[]{:S(2)}, u32[]{:S(2)}) collective-permute-start(f32[16,128]{1,0:T(8,128)S(1)} %add_add_fusion.4), channel_id=1, source_target_pairs={{0,3},{1,0},{2,1},{3,2},{4,7},{5,4},{6,5},{7,6},{8,11},{9,8},{10,9... | collective-permute-start | bytes 24584 | tf_op jit(solution)/shard_map/ppermute | solution.py:264
  (6 other events, 78.2 us)

commit v2 on v1

v2 whole, which is shorter than its diff:
```python
import functools

import jax
import jax.numpy as jnp
from jax import lax
from jax.experimental import pallas as pl
from jax.experimental.pallas import tpu as pltpu
from jax.sharding import PartitionSpec as P

NS = 2048
LAGS = 101
HALF = LAGS // 2
TAPS = 16
NPHASE = 32
SHIFT_MAX = 8
CLASSES = 4
TRACE_LIMIT = 4
BIN_DEV = 16
TR_DEV = 256
DEVICES = 128
SLOTS = DEVICES * TRACE_LIMIT
LANES = 128
WIDE = NS + LANES
LROWS = 112
LAG_TOP = 106
BINS_STEP = 4
BETA = 24.0
EPS = 1e-06
F32 = jnp.float32
BF16 = jnp.bfloat16
HEAD = 16

NN = (((1,), (0,)), ((), ()))
NT = (((1,), (1,)), ((), ()))
TN = (((0,), (0,)), ((), ()))


def dot(a, b, dims, precision=None):
    return lax.dot_general(a, b, dims, precision=precision, preferred_element_type=F32)


def iota(shape, axis):
    return lax.broadcasted_iota(jnp.int32, shape, axis)


def pack_kernel(shot_ref, rec_ref, bin_ref, cls_ref, shift_ref, frac_ref, x_ref, out_ref, y_ref):
    shot, rec, bin_, cls = shot_ref[...], rec_ref[...], bin_ref[...], cls_ref[...]
    dest = (bin_ // BIN_DEV) * CLASSES + cls
    rows = [
        shot // 128,
        shot % 128,
        rec // 128,
        rec % 128,
        bin_ % BIN_DEV,
        frac_ref[...],
        jnp.ones_like(shot),
        shift_ref[...] + SHIFT_MAX,
        dest,
    ]
    sub = iota((16, TR_DEV), 0)
    info = jnp.zeros((16, TR_DEV), F32)
    for i, row in enumerate(rows):
        info = jnp.where(sub == i, row.astype(F32), info)
    place = (iota((16, LANES), 1) == iota((16, LANES), 0) + HEAD).astype(F32).astype(BF16)
    cols = dot(info.astype(BF16), place, TN)
    amount = cols[:, HEAD + 7 : HEAD + 8].astype(jnp.int32)
    dest_col = cols[:, HEAD + 8 : HEAD + 9]
    same = (dest_col == dest.astype(F32)) & (iota((TR_DEV, TR_DEV), 0) < iota((TR_DEV, TR_DEV), 1))
    rank = jnp.sum(jnp.where(same, 1.0, 0.0), axis=0, keepdims=True).astype(jnp.int32)
    slot = dest * TRACE_LIMIT + rank
    onehot = (iota((SLOTS, TR_DEV), 0) == slot).astype(F32).astype(BF16)
    on = [((amount >> bit) & 1).astype(F32).astype(BF16) > 0 for bit in range(5)]
    cols = cols.astype(BF16)
    step = 32
    for r in range(0, TR_DEV, step):
        y = jnp.concatenate([x_ref[r : r + step, :], jnp.zeros((step, LANES), BF16)], axis=1)
        y = pltpu.roll(y, SHIFT_MAX, 1)
        for bit in range(5):
            y = jnp.where(on[bit][r : r + step, :], pltpu.roll(y, WIDE - (1 << bit), 1), y)
        y_ref[r : r + step, :NS] = y[:, :NS]
        y_ref[r : r + step, NS:] = y[:, NS:] + cols[r : r + step, :]
    out_ref[...] = dot(onehot, y_ref[...], NN).reshape(DEVICES, TRACE_LIMIT, WIDE).astype(BF16)


def one_hot_rows(row, count):
    return (iota((count, SLOTS), 0) == row.astype(jnp.int32)).astype(F32)


def unit(size):
    return (iota((size, size), 0) == iota((size, size), 1)).astype(F32).astype(BF16)


def stack_rows(weight, y_ref, head, frac, side_ref, part_ref, sum_ref):
    live = head[6:7, :]
    u = (iota((TAPS, SLOTS), 0) - (TAPS // 2 - 1)).astype(F32) - frac
    angle = jnp.pi * u
    safe = jnp.where(u == 0.0, 1.0, angle)
    sinc = jnp.where(u == 0.0, 1.0, jnp.sin(safe) / safe)
    taps = sinc * (0.5 + 0.5 * jnp.cos(angle * (1.0 / (TAPS // 2))))
    side_ref[0:16, :] = head
    side_ref[16:32, :] = taps
    member = one_hot_rows(head[4:5, :], BIN_DEV) * live
    rows = [member * taps[k : k + 1, :] for k in range(TAPS)]
    high = [row.astype(BF16) for row in rows]
    low = [(row - top.astype(F32)).astype(BF16) for row, top in zip(rows, high)]
    slots = y_ref[...]
    sum_ref[...] = dot(jnp.concatenate(high, axis=0), slots, NN) + dot(jnp.concatenate(low, axis=0), slots, NN)
    total = jnp.zeros((BIN_DEV, WIDE), F32)
    for k in range(TAPS):
        total = total + pltpu.roll(sum_ref[k * BIN_DEV : (k + 1) * BIN_DEV, :], (TAPS // 2 - 1 - k) % WIDE, 1)
    part_ref[:, :NS] = (weight * total[:, :NS]).astype(BF16)
    mass = weight * jnp.sum(member, axis=1, keepdims=True)
    m0 = mass.astype(BF16).astype(F32)
    m1 = (mass - m0).astype(BF16).astype(F32)
    m2 = mass - m0 - m1
    lane = iota((BIN_DEV, LANES), 1)
    tail = jnp.where(lane == 0, m0, jnp.where(lane == 1, m1, jnp.where(lane == 2, m2, 0.0)))
    part_ref[:, NS:] = tail.astype(BF16)


def first_kernel(weight_ref, slots_ref, part_ref, side_ref, y_ref, sum_ref):
    y_ref[...] = slots_ref[...].reshape(SLOTS, WIDE)
    head = dot(unit(LANES), y_ref[:, NS:], NT)[HEAD : HEAD + 16, :]
    stack_rows(weight_ref[0, 0], y_ref, head, head[5:6, :] * (1.0 / NPHASE), side_ref, part_ref, sum_ref)


def next_kernel(weight_ref, y_ref, head_ref, rec_ref, shot_ref, part_ref, side_ref, sum_ref):
    head = head_ref[0:16, :]
    frac = head[5:6, :] * (1.0 / NPHASE)
    for table_ref, at in ((shot_ref, 0), (rec_ref, 2)):
        low = one_hot_rows(head[at + 1 : at + 2, :], 128)
        high = one_hot_rows(head[at : at + 1, :], 8)
        found = dot(table_ref[...], low, NN, lax.Precision.HIGHEST)
        frac = frac + jnp.sum(found * high, axis=0, keepdims=True)
    stack_rows(weight_ref[0, 0], y_ref, head, frac, side_ref, part_ref, sum_ref)


def shift_kernel(y_ref, side_ref, st_ref, energy_ref, xt_ref):
    eye = unit(LANES)
    groups = SLOTS // LANES
    for c in range(NS // LANES):
        block = dot(eye, y_ref[:, c * LANES : (c + 1) * LANES], NT)
        for q in range(groups):
            xt_ref[q, 8 + c * LANES : 8 + (c + 1) * LANES, :] = block[:, q * LANES : (q + 1) * LANES]
    block = dot(eye, y_ref[:, NS:], NT)
    for q in range(groups):
        part = block[:, q * LANES : (q + 1) * LANES]
        xt_ref[q, 0:8, :] = part[120:128, :]
        xt_ref[q, 8 + NS : 16 + NS, :] = part[0:8, :]
    chunk = 32
    energies = []
    for q in range(groups):
        tap = [
            jnp.broadcast_to(side_ref[16 + k : 17 + k, q * LANES : (q + 1) * LANES], (8, LANES)) for k in range(TAPS)
        ]

        def body(i, energy):
            base = pl.multiple_of(i * chunk, chunk)
            totals = [None] * (chunk // 8)
            for p in range(chunk + TAPS - 8):
                window = xt_ref[q, pl.ds(base + 1 + p, 8), :]
                for h in range(chunk // 8):
                    k = p - 8 * h
                    if 0 <= k < TAPS:
                        term = tap[k] * window
                        totals[h] = term if totals[h] is None else totals[h] + term
            for h in range(0, chunk // 8, 2):
                rounded = jnp.concatenate(totals[h : h + 2], axis=0).astype(BF16)
                st_ref[pl.ds(base + 8 * h, 16), q * LANES : (q + 1) * LANES] = rounded
                wide = rounded.astype(F32)
                energy = energy + wide[0:8, :] * wide[0:8, :] + wide[8:16, :] * wide[8:16, :]
            return energy

        energy = lax.fori_loop(0, NS // chunk, body, jnp.zeros((8, LANES), F32), unroll=2)
        energies.append(jnp.sum(energy, axis=0, keepdims=True))
    energy_ref[...] = jnp.broadcast_to(jnp.concatenate(energies, axis=1), (8, SLOTS))


def corr_kernel(first, p0_ref, p1_ref, p2_ref, p3_ref, st_ref, energy_ref, side_ref, pilot_ref, grad_ref, lag_ref, wide_ref):
    total = (p0_ref[...].astype(F32) + p2_ref[...].astype(F32)) + (
        p1_ref[...].astype(F32) + p3_ref[...].astype(F32)
    )
    mass = (total[:, NS : NS + 1] + total[:, NS + 1 : NS + 2]) + total[:, NS + 2 : NS + 3]
    pilot = (total[:, :NS] * lax.rsqrt(mass + 1.0)).astype(BF16)
    pilot_ref[...] = pilot
    wide = pilot.astype(F32)
    wide_ref[:, :NS] = wide
    wide_ref[:, NS:] = jnp.zeros((BIN_DEV, LANES), F32)
    pilot_scale = lax.rsqrt(jnp.sum(wide * wide, axis=1, keepdims=True) + EPS)
    head = side_ref[0:16, :]
    live = head[6:7, :]
    member = one_hot_rows(head[4:5, :], BIN_DEV) * live
    corr = jnp.zeros((LROWS, SLOTS), F32)
    for b0 in range(0, BIN_DEV, BINS_STEP):
        for bb in range(BINS_STEP):
            row = jnp.broadcast_to(wide_ref[b0 + bb : b0 + bb + 1, :], (16, WIDE)).astype(BF16)
            row = pltpu.roll(row, 0, 1, stride=1, stride_axis=0)
            for g in range(0, LROWS, 16):
                at = (b0 + bb) * LROWS + g
                lag_ref[at : at + 16, :] = pltpu.roll(row, (WIDE - (LAG_TOP - HALF) + g) % WIDE, 1)[:, :NS]
        every = dot(lag_ref[b0 * LROWS : (b0 + BINS_STEP) * LROWS, :], st_ref[...], NN)
        for bb in range(BINS_STEP):
            corr = corr + member[b0 + bb : b0 + bb + 1, :] * every[bb * LROWS : (bb + 1) * LROWS, :]
    scale = lax.rsqrt(energy_ref[0:1, :] + EPS) * jnp.sum(member * pilot_scale, axis=0, keepdims=True)
    lag = LAG_TOP - iota((LROWS, SLOTS), 0)
    exponent = jnp.where((lag >= 0) & (lag < LAGS), jnp.exp(BETA * (corr * scale)), 0.0)
    delay = jnp.sum(exponent * (lag - HALF).astype(F32), axis=0, keepdims=True) / jnp.sum(
        exponent, axis=0, keepdims=True
    )
    misfit = -delay * live
    for at, out in ((2, 0), (0, 16 if first else 8)):
        low = one_hot_rows(head[at + 1 : at + 2, :], 128)
        high = one_hot_rows(head[at : at + 1, :], 8)
        values = high * misfit
        if first:
            values = jnp.concatenate([values, high * live], axis=0)
        sums = dot(values, low, NT, lax.Precision.HIGHEST)
        grad_ref[out : out + sums.shape[0], :] = sums


VMEM = pl.BlockSpec(memory_space=pltpu.VMEM)
SMEM = pl.BlockSpec(memory_space=pltpu.SMEM)
PARAMS = pltpu.CompilerParams(vmem_limit_bytes=40 * 1024 * 1024)


def shape(dims, dtype):
    return jax.ShapeDtypeStruct(dims, dtype)


def call(kernel, out, memory, scratch, name, flops, moved, *args):
    return pl.pallas_call(
        kernel,
        out_shape=out,
        in_specs=[SMEM if space else VMEM for space in memory],
        out_specs=jax.tree.map(lambda _: VMEM, out),
        scratch_shapes=scratch,
        compiler_params=PARAMS,
        cost_estimate=pl.CostEstimate(flops=flops, bytes_accessed=moved, transcendentals=0),
        name=name,
    )(*args)


def pack(traces, *meta):
    return call(
        pack_kernel,
        shape((DEVICES, TRACE_LIMIT, WIDE), BF16),
        (0,) * 7,
        [pltpu.VMEM((TR_DEV, WIDE), BF16)],
        "pack",
        10**9,
        3 * 2**20,
        *[row.reshape(1, TR_DEV) for row in meta],
        traces,
    )


PART = shape((BIN_DEV, WIDE), BF16)
SIDE = shape((32, SLOTS), F32)
ROWS = pltpu.VMEM((TAPS * BIN_DEV, WIDE), F32)


def stack_first(weight, slots):
    out = (PART, SIDE, shape((SLOTS, WIDE), BF16))
    return call(first_kernel, out, (1, 0), [ROWS], "stack_first", 3 * 10**9, 10**7, weight, slots)


def stack_next(weight, rows, side, rec, shot):
    return call(
        next_kernel, (PART, SIDE), (1, 0, 0, 0, 0), [ROWS], "stack_next", 3 * 10**9, 10**7, weight, rows, side, rec, shot
    )


def shift(rows, side):
    out = (shape((NS, SLOTS), BF16), shape((8, SLOTS), F32))
    scratch = [pltpu.VMEM((SLOTS // LANES, NS + 16, LANES), F32)]
    return call(shift_kernel, out, (0, 0), scratch, "shift", 6 * 10**9, 2 * 10**7, rows, side)


def correlate(first, parts, shifted, energy, side):
    out = (shape((BIN_DEV, NS), BF16), shape((32 if first else 16, LANES), F32))
    scratch = [pltpu.VMEM((BIN_DEV * LROWS, NS), BF16), pltpu.VMEM((BIN_DEV, WIDE), F32)]
    kernel = functools.partial(corr_kernel, first)
    return call(kernel, out, (0,) * 7, scratch, "correlate", 4 * 10**9, 10**7, *parts, shifted, energy, side)


def cmp_pairs(move):
    pairs = []
    for y in range(4):
        for x in range(4):
            for c in range(2):
                y2, x2, c2 = move(y, x, c)
                pairs.append(((y * 4 + x) * 2 + c, (y2 * 4 + x2) * 2 + c2))
    return pairs


def ring_sum(value, axis, perms):
    got = [lax.ppermute(value, axis, perm) for perm in perms]
    if len(got) == 1:
        return value + got[0]
    return (value + got[1]) + (got[0] + got[2])


def off_perm(d):
    return [(i, (i + d) % 4) for i in range(4)]


def sum_all(value):
    value = ring_sum(value, "cmp", [cmp_pairs(lambda y, x, c: (y, x, 1 - c))])
    value = ring_sum(value, "cmp", [cmp_pairs(lambda y, x, c, d=d: (y, (x + d) % 4, c)) for d in (1, 2, 3)])
    value = ring_sum(value, "cmp", [cmp_pairs(lambda y, x, c, d=d: ((y + d) % 4, x, c)) for d in (1, 2, 3)])
    return ring_sum(value, "off", [off_perm(d) for d in (1, 2, 3)])


def on_device(
    traces,
    shot_id,
    receiver_id,
    cmp_bin,
    offset_class,
    shift_int,
    frac_index,
    damping_table,
    damping_index,
):
    outgoing = pack(traces, shot_id, receiver_id, cmp_bin, offset_class, shift_int, frac_index)
    slots = lax.all_to_all(outgoing, ("cmp", "off"), split_axis=0, concat_axis=0, tiled=True)
    weight = (1.0 / (1.0 + lax.axis_index("off").astype(F32))).reshape(1, 1)
    entries = jnp.arange(damping_table.shape[0], dtype=jnp.int32)
    damps = [jnp.sum(jnp.where(entries == damping_index[i], damping_table, 0.0)) for i in range(2)]
    for iteration in range(2):
        first = iteration == 0
        if first:
            part, side, rows = stack_first(weight, slots)
        else:
            part, side = stack_next(weight, rows, side, rec, shot)
        others = [lax.ppermute(part, "off", off_perm(d)) for d in (1, 2, 3)]
        shifted, energy = shift(rows, side)
        pilot, sums = correlate(first, (part, *others), shifted, energy, side)
        sums = sum_all(sums)
        damp = damps[iteration]
        if first:
            rec_count, shot_count = sums[8:16], sums[24:32]
            rec = sums[0:8] / ((1.0 + damp) * rec_count + damp)
            shot = sums[16:24] / ((1.0 + damp) * shot_count + damp)
        else:
            rec = rec + sums[0:8] / ((1.0 + damp) * rec_count + damp)
            shot = shot + sums[8:16] / ((1.0 + damp) * shot_count + damp)
    return (shot[0:2].reshape(256), rec.reshape(1024), pilot)


def solution(mesh):
    placed = (
        P(("cmp", "off"), None),
        P(("cmp", "off")),
        P(("cmp", "off")),
        P(("cmp", "off")),
        P(("cmp", "off")),
        P(("cmp", "off")),
        P(("cmp", "off")),
        P(),
        P(),
    )
    return jax.shard_map(
        on_device, mesh=mesh, in_specs=placed, out_specs=(P(), P(), P("cmp", None)), check_vma=False
    )
```

time: 143 us -> 142 us (level)
  waiting for transfers between devices: 48.8 us -> 42 us
  Pallas kernels: 31.4 us -> 35.6 us
    ppermute x6, waiting for transfers between devices: 7.71 us -> 0.02 us  [on_device(): others = [lax.ppermute(part, 'off', off_perm(d)) for d in (1, 2, 3)]]
    unnamed x6 -> x24, local copies, waits for them, and re-layouts: 1.23 us -> 6.68 us
    reshape x2 -> x0, local copies, waits for them, and re-layouts: 4.69 us -> none  [the longest x1 2.58 us: on_device(): slots = arrived.reshape(SLOTS, WIDE)]
    pallas_call x5 -> x7, Pallas kernels: 31.4 us -> 35.6 us  [call(): pl.pallas_call(kernel, out_shape=out, in_specs=[SMEM if space else VMEM f...]
    ppermute x20, starting transfers between devices: 29.4 us -> 31.2 us  [ring_sum(): got = [lax.ppermute(value, axis, perm) for perm in perms]]
  transfers between devices with their start and end apart: 27 -> 27, of which waited for: 17 -> 12; matrix products, arithmetic and copies ran while one was open for 2% -> 2% of each run, Pallas kernels for 0% -> 10%
where the time goes in v2:
time: 142 us; the launch traced here: 141 us
  starting transfers between devices  49.9 us (35%)
  waiting for transfers between devices  42 us (30%)
  Pallas kernels  35.6 us (25%)
  local copies, waits for them, and re-layouts  7.82 us (6%)
  other arithmetic  3.75 us (3%)
  between operations  2.1 us (1%)
    pallas_call x7, Pallas kernels, call(): pl.pallas_call(kernel, out_shape=out, in_specs=[SMEM if space else VMEM f...  35.6 us
    ppermute x20, starting transfers between devices, ring_sum(): got = [lax.ppermute(value, axis, perm) for perm in perms]  31.2 us
    all_to_all x1, waiting for transfers between devices, on_device(): lax.all_to_all(outgoing, ('cmp', 'off'), split_axis=0, concat_axis=0, til...  31.1 us
    all_to_all x1, starting transfers between devices, on_device(): lax.all_to_all(outgoing, ('cmp', 'off'), split_axis=0, concat_axis=0, til...  11.1 us
    ppermute x20, waiting for transfers between devices, ring_sum(): got = [lax.ppermute(value, axis, perm) for perm in perms]  10.8 us
    ppermute x6, starting transfers between devices, on_device(): others = [lax.ppermute(part, 'off', off_perm(d)) for d in (1, 2, 3)]  7.62 us
    unnamed x24, local copies, waits for them, and re-layouts  6.68 us
  transfers between devices with their start and end apart: 27, of which 12 were waited for; matrix products, arithmetic and copies ran while one was open for 2% of the time, Pallas kernels for 10%

profile of v2, /device:TPU:0, one launch (start us, length us, event | category | flops | bytes accessed | tf_op | source)
XLA Modules:
  0.0 141.2 jit_solution(16894038021880688618)
XLA Ops:
  5.9 3.9 %pack.1 = bf16[128,4,2176]{2,1,0:T(4,128)(2,1)S(1)} custom-call(s32[1,256]{1,0:T(1,128)S(1)} %bitcast.13, s32[1,256]{1,0:T(1,128)S(1)} %bitcast.14, s32[1,256]{1,0:T(1,128)S(1)} %bitcast.15, s32[1,256]{1,0:T(1,128)S(1)} %bitcast.16, s32[1,256]{1,0:T(1,128)S(1)} %bitcast.17, s32[1,256]{1,0:T(1,128)S(1)} %bitcast.18, bf16[256,2048]{1,0:T(8,128)(2,1)S(1)} %copy-done.1), custom_call_target="tpu_custom_call" | custom-call | flops 1000000000 | bytes 3145728 | tf_op jit(solution)/shard_map/pack/pallas_call | solution.py:231
  11.2 11.1 %all-to-all-start = ((bf16[128,4,2176]{2,1,0:T(4,128)(2,1)}), bf16[128,4,2176]{2,1,0:T(4,128)(2,1)S(1)}, u32[]{:S(2)}, u32[]{:S(2)}) async-start(bf16[128,4,2176]{2,1,0:T(4,128)(2,1)} %copy-done), calls=%async_computation | async-start | bytes 4456448 | tf_op jit(solution)/shard_map/all_to_all | solution.py:326
  22.4 31.1 %all-to-all-done.slots_ref = bf16[128,4,2176]{2,1,0:T(4,128)(2,1)S(1)} async-done(((bf16[128,4,2176]{2,1,0:T(4,128)(2,1)}), bf16[128,4,2176]{2,1,0:T(4,128)(2,1)S(1)}, u32[]{:S(2)}, u32[]{:S(2)}) %all-to-all-start) | async-done | bytes 2228256 | tf_op jit(solution)/shard_map/all_to_all | solution.py:326
  53.6 1.9 %stack_first.1 = (bf16[16,2176]{1,0:T(8,128)(2,1)S(1)}, f32[32,512]{1,0:T(8,128)S(1)}, bf16[512,2176]{1,0:T(8,128)(2,1)S(1)}) custom-call(f32[1,1]{1,0:T(1,128)} %bitcast.weight_ref, bf16[128,4,2176]{2,1,0:T(4,128)(2,1)S(1)} %all-to-all-done.slots_ref), custom_call_target="tpu_custom_call" | custom-call | flops 3000000000 | bytes 10000000 | tf_op jit(solution)/shard_map/stack_first/pallas_call | solution.py:231
  56.4 1.7 %collective-permute-start.1 = (bf16[16,2176]{1,0:T(8,128)(2,1)S(1)}, bf16[16,2176]{1,0:T(8,128)(2,1)S(1)}, u32[]{:S(2)}, u32[]{:S(2)}) collective-permute-start(bf16[16,2176]{1,0:T(8,128)(2,1)S(1)} %get-tuple-element.15.p0_ref), channel_id=1, source_target_pairs={{0,2},{1,3},{2,0},{3,1},{4,6},{5,7},{6,4},{7,5},{8,10},{9,11},{10,... | collective-permute-start | bytes 208904 | tf_op jit(solution)/shard_map/ppermute | solution.py:336
  59.2 7.0 %shift.2 = (bf16[2048,512]{1,0:T(8,128)(2,1)S(1)}, f32[8,512]{1,0:T(8,128)S(1)}) custom-call(bf16[512,2176]{1,0:T(8,128)(2,1)S(1)} %get-tuple-element.16.y_ref, f32[32,512]{1,0:T(8,128)S(1)} %get-tuple-element.17.side_ref.head_ref), custom_call_target="tpu_custom_call" | custom-call | flops 6000000000 | bytes 20000000 | tf_op jit(solution)/shard_map/shift/pallas_call | solution.py:231
  66.3 6.9 %correlate.2 = (bf16[16,2048]{1,0:T(8,128)(2,1)}, f32[32,128]{1,0:T(8,128)S(1)}) custom-call(bf16[16,2176]{1,0:T(8,128)(2,1)S(1)} %get-tuple-element.15.p0_ref, bf16[16,2176]{1,0:T(8,128)(2,1)S(1)} %collective-permute-done.p1_ref, bf16[16,2176]{1,0:T(8,128)(2,1)S(1)} %collective-permute-done.1.p2_ref, bf16[16,2176]{1,0:T(8,128)(2,1)S(1)} %collective-permute-done.2.p3_ref, ...), custom_call_target="tpu_custom_call" | custom-call | flops 4000000000 | bytes 10000000 | tf_op jit(solution)/shard_map/correlate/pallas_call | solution.py:231
  76.8 2.4 %collective-permute-start.6 = (f32[32,128]{1,0:T(8,128)S(1)}, f32[32,128]{1,0:T(8,128)S(1)}, u32[]{:S(2)}, u32[]{:S(2)}) collective-permute-start(f32[32,128]{1,0:T(8,128)S(1)} %add.98), channel_id=1, source_target_pairs={{0,24},{4,28},{8,0},{12,4},{16,8},{20,12},{24,16},{28,20},{32,56},... | collective-permute-start | bytes 49160 | tf_op jit(solution)/shard_map/ppermute | solution.py:297
  82.8 2.2 %collective-permute-start.9 = (f32[32,128]{1,0:T(8,128)S(1)}, f32[32,128]{1,0:T(8,128)S(1)}, u32[]{:S(2)}, u32[]{:S(2)}) collective-permute-start(f32[32,128]{1,0:T(8,128)S(1)} %add_add_fusion.2), channel_id=1, source_target_pairs={{0,96},{4,100},{8,104},{12,108},{16,112},{20,116},{24,120},{28,124... | collective-permute-start | bytes 49160 | tf_op jit(solution)/shard_map/ppermute | solution.py:297
  86.7 2.7 %collective-permute-start.10 = (f32[32,128]{1,0:T(8,128)S(1)}, f32[32,128]{1,0:T(8,128)S(1)}, u32[]{:S(2)}, u32[]{:S(2)}) collective-permute-start(f32[32,128]{1,0:T(8,128)S(1)} %add_add_fusion.1), channel_id=1, source_target_pairs={{0,2},{1,3},{2,0},{3,1},{4,6},{5,7},{6,4},{7,5},{8,10},{9,11},{10,... | collective-permute-start | bytes 49160 | tf_op jit(solution)/shard_map/ppermute | solution.py:297
  89.4 3.2 %collective-permute-start.12 = (f32[32,128]{1,0:T(8,128)S(1)}, f32[32,128]{1,0:T(8,128)S(1)}, u32[]{:S(2)}, u32[]{:S(2)}) collective-permute-start(f32[32,128]{1,0:T(8,128)S(1)} %add_add_fusion.1), channel_id=1, source_target_pairs={{0,3},{1,0},{2,1},{3,2},{4,7},{5,4},{6,5},{7,6},{8,11},{9,8},{10,9... | collective-permute-start | bytes 49160 | tf_op jit(solution)/shard_map/ppermute | solution.py:297
  92.6 1.9 %fusion.4 = (f32[]{:T(128)}, f32[]{:T(128)}) fusion(f32[8]{0:T(128)S(1)} %copy-done.11, s32[]{:T(128)} %bitcast.8, s32[]{:T(128)} %bitcast.7), kind=kLoop, calls=%fused_computation.17 | loop fusion | flops 46 | bytes 48 | tf_op jit(solution)/shard_map/reduce_sum | solution.py:329
  95.7 2.1 %stack_next.1 = (bf16[16,2176]{1,0:T(8,128)(2,1)S(1)}, f32[32,512]{1,0:T(8,128)S(1)}) custom-call(f32[1,1]{1,0:T(1,128)} %bitcast.weight_ref, bf16[512,2176]{1,0:T(8,128)(2,1)S(1)} %copy-done.9, f32[32,512]{1,0:T(8,128)S(1)} %get-tuple-element.17.side_ref.head_ref, f32[8,128]{1,0:T(8,128)S(1)} %get-tuple-element.31.rec_ref, ...), custom_call_target="tpu_custom_call" | custom-call | flops 3000000000 | bytes 10000000 | tf_op jit(solution)/shard_map/stack_next/pallas_call | solution.py:231
  97.9 3.9 %collective-permute-start.14 = (bf16[16,2176]{1,0:T(8,128)(2,1)S(1)}, bf16[16,2176]{1,0:T(8,128)(2,1)S(1)}, u32[]{:S(2)}, u32[]{:S(2)}) collective-permute-start(bf16[16,2176]{1,0:T(8,128)(2,1)S(1)} %get-tuple-element.21.p0_ref), channel_id=1, source_target_pairs={{0,2},{1,3},{2,0},{3,1},{4,6},{5,7},{6,4},{7,5},{8,10},{9,11},{10,... | collective-permute-start | bytes 208904 | tf_op jit(solution)/shard_map/ppermute | solution.py:336
  101.8 7.0 %shift.3 = (bf16[2048,512]{1,0:T(8,128)(2,1)S(1)}, f32[8,512]{1,0:T(8,128)S(1)}) custom-call(bf16[512,2176]{1,0:T(8,128)(2,1)S(1)} %copy-done.9, f32[32,512]{1,0:T(8,128)S(1)} %get-tuple-element.22.side_ref), custom_call_target="tpu_custom_call" | custom-call | flops 6000000000 | bytes 20000000 | tf_op jit(solution)/shard_map/shift/pallas_call | solution.py:231
  108.9 6.8 %correlate.3 = (bf16[16,2048]{1,0:T(8,128)(2,1)}, f32[16,128]{1,0:T(8,128)S(1)}) custom-call(bf16[16,2176]{1,0:T(8,128)(2,1)S(1)} %get-tuple-element.21.p0_ref, bf16[16,2176]{1,0:T(8,128)(2,1)S(1)} %collective-permute-done.13.p1_ref, bf16[16,2176]{1,0:T(8,128)(2,1)S(1)} %collective-permute-done.14.p2_ref, ...), custom_call_target="tpu_custom_call" | custom-call | flops 4000000000 | bytes 10000000 | tf_op jit(solution)/shard_map/correlate/pallas_call | solution.py:231
  116.8 2.2 %collective-permute-start.17 = (f32[16,128]{1,0:T(8,128)S(1)}, f32[16,128]{1,0:T(8,128)S(1)}, u32[]{:S(2)}, u32[]{:S(2)}) collective-permute-start(f32[16,128]{1,0:T(8,128)S(1)} %add.112), channel_id=1, source_target_pairs={{0,16},{4,20},{8,24},{12,28},{16,0},{20,4},{24,8},{28,12},{32,48},... | collective-permute-start | bytes 24584 | tf_op jit(solution)/shard_map/ppermute | solution.py:297
  119.0 1.9 %collective-permute-start.18 = (f32[16,128]{1,0:T(8,128)S(1)}, f32[16,128]{1,0:T(8,128)S(1)}, u32[]{:S(2)}, u32[]{:S(2)}) collective-permute-start(f32[16,128]{1,0:T(8,128)S(1)} %add.112), channel_id=1, source_target_pairs={{0,8},{4,12},{8,16},{12,20},{16,24},{20,28},{24,0},{28,4},{32,40},... | collective-permute-start | bytes 24584 | tf_op jit(solution)/shard_map/ppermute | solution.py:297
  122.2 1.6 %collective-permute-done.18 = f32[16,128]{1,0:T(8,128)S(1)} collective-permute-done((f32[16,128]{1,0:T(8,128)S(1)}, f32[16,128]{1,0:T(8,128)S(1)}, u32[]{:S(2)}, u32[]{:S(2)}) %collective-permute-start.18) | collective-permute-done | bytes 8224 | tf_op jit(solution)/shard_map/ppermute | solution.py:297
  124.5 2.2 %collective-permute-start.20 = (f32[16,128]{1,0:T(8,128)S(1)}, f32[16,128]{1,0:T(8,128)S(1)}, u32[]{:S(2)}, u32[]{:S(2)}) collective-permute-start(f32[16,128]{1,0:T(8,128)S(1)} %add_add_fusion.5), channel_id=1, source_target_pairs={{0,64},{4,68},{8,72},{12,76},{16,80},{20,84},{24,88},{28,92},{32,9... | collective-permute-start | bytes 24584 | tf_op jit(solution)/shard_map/ppermute | solution.py:297
  126.7 1.9 %collective-permute-start.21 = (f32[16,128]{1,0:T(8,128)S(1)}, f32[16,128]{1,0:T(8,128)S(1)}, u32[]{:S(2)}, u32[]{:S(2)}) collective-permute-start(f32[16,128]{1,0:T(8,128)S(1)} %add_add_fusion.5), channel_id=1, source_target_pairs={{0,32},{4,36},{8,40},{12,44},{16,48},{20,52},{24,56},{28,60},{32,6... | collective-permute-start | bytes 24584 | tf_op jit(solution)/shard_map/ppermute | solution.py:297
  130.0 1.6 %collective-permute-done.21 = f32[16,128]{1,0:T(8,128)S(1)} collective-permute-done((f32[16,128]{1,0:T(8,128)S(1)}, f32[16,128]{1,0:T(8,128)S(1)}, u32[]{:S(2)}, u32[]{:S(2)}) %collective-permute-start.21) | collective-permute-done | bytes 8224 | tf_op jit(solution)/shard_map/ppermute | solution.py:297
  132.3 2.3 %collective-permute-start.23 = (f32[16,128]{1,0:T(8,128)S(1)}, f32[16,128]{1,0:T(8,128)S(1)}, u32[]{:S(2)}, u32[]{:S(2)}) collective-permute-start(f32[16,128]{1,0:T(8,128)S(1)} %add_add_fusion.4), channel_id=1, source_target_pairs={{0,2},{1,3},{2,0},{3,1},{4,6},{5,7},{6,4},{7,5},{8,10},{9,11},{10,... | collective-permute-start | bytes 24584 | tf_op jit(solution)/shard_map/ppermute | solution.py:297
  134.5 3.2 %collective-permute-start.25 = (f32[16,128]{1,0:T(8,128)S(1)}, f32[16,128]{1,0:T(8,128)S(1)}, u32[]{:S(2)}, u32[]{:S(2)}) collective-permute-start(f32[16,128]{1,0:T(8,128)S(1)} %add_add_fusion.4), channel_id=1, source_target_pairs={{0,3},{1,0},{2,1},{3,2},{4,7},{5,4},{6,5},{7,6},{8,11},{9,8},{10,9... | collective-permute-start | bytes 24584 | tf_op jit(solution)/shard_map/ppermute | solution.py:297
  (74 shorter events, 26.3 us)
Async XLA Ops:
  11.2 42.3 %all-to-all-start = ((bf16[128,4,2176]{2,1,0:T(4,128)(2,1)}), bf16[128,4,2176]{2,1,0:T(4,128)(2,1)S(1)}, u32[]{:S(2)}, u32[]{:S(2)}) async-start(bf16[128,4,2176]{2,1,0:T(4,128)(2,1)} %copy-done), calls=%async_computation | async-start | bytes 4456448 | tf_op jit(solution)/shard_map/all_to_all | solution.py:326
  55.5 10.7 %collective-permute-start = (bf16[16,2176]{1,0:T(8,128)(2,1)S(1)}, bf16[16,2176]{1,0:T(8,128)(2,1)S(1)}, u32[]{:S(2)}, u32[]{:S(2)}) collective-permute-start(bf16[16,2176]{1,0:T(8,128)(2,1)S(1)} %get-tuple-element.15.p0_ref), channel_id=1, source_target_pairs={{0,1},{1,2},{2,3},{3,0},{4,5},{5,6},{6,7},{7,4},{8,9},{9,10},{10,1... | collective-permute-start | bytes 208904 | tf_op jit(solution)/shard_map/ppermute | solution.py:336
  56.4 9.8 %collective-permute-start.1 = (bf16[16,2176]{1,0:T(8,128)(2,1)S(1)}, bf16[16,2176]{1,0:T(8,128)(2,1)S(1)}, u32[]{:S(2)}, u32[]{:S(2)}) collective-permute-start(bf16[16,2176]{1,0:T(8,128)(2,1)S(1)} %get-tuple-element.15.p0_ref), channel_id=1, source_target_pairs={{0,2},{1,3},{2,0},{3,1},{4,6},{5,7},{6,4},{7,5},{8,10},{9,11},{10,... | collective-permute-start | bytes 208904 | tf_op jit(solution)/shard_map/ppermute | solution.py:336
  58.2 8.1 %collective-permute-start.2 = (bf16[16,2176]{1,0:T(8,128)(2,1)S(1)}, bf16[16,2176]{1,0:T(8,128)(2,1)S(1)}, u32[]{:S(2)}, u32[]{:S(2)}) collective-permute-start(bf16[16,2176]{1,0:T(8,128)(2,1)S(1)} %get-tuple-element.15.p0_ref), channel_id=1, source_target_pairs={{0,3},{1,0},{2,1},{3,2},{4,7},{5,4},{6,5},{7,6},{8,11},{9,8},{10,9... | collective-permute-start | bytes 208904 | tf_op jit(solution)/shard_map/ppermute | solution.py:336
  74.3 5.2 %collective-permute-start.4 = (f32[32,128]{1,0:T(8,128)S(1)}, f32[32,128]{1,0:T(8,128)S(1)}, u32[]{:S(2)}, u32[]{:S(2)}) collective-permute-start(f32[32,128]{1,0:T(8,128)S(1)} %add.98), channel_id=1, source_target_pairs={{0,16},{4,20},{8,24},{12,28},{16,0},{20,4},{24,8},{28,12},{32,48},... | collective-permute-start | bytes 49160 | tf_op jit(solution)/shard_map/ppermute | solution.py:297
  75.9 5.0 %collective-permute-start.5 = (f32[32,128]{1,0:T(8,128)S(1)}, f32[32,128]{1,0:T(8,128)S(1)}, u32[]{:S(2)}, u32[]{:S(2)}) collective-permute-start(f32[32,128]{1,0:T(8,128)S(1)} %add.98), channel_id=1, source_target_pairs={{0,8},{4,12},{8,16},{12,20},{16,24},{20,28},{24,0},{28,4},{32,40},... | collective-permute-start | bytes 49160 | tf_op jit(solution)/shard_map/ppermute | solution.py:297
  76.8 4.1 %collective-permute-start.6 = (f32[32,128]{1,0:T(8,128)S(1)}, f32[32,128]{1,0:T(8,128)S(1)}, u32[]{:S(2)}, u32[]{:S(2)}) collective-permute-start(f32[32,128]{1,0:T(8,128)S(1)} %add.98), channel_id=1, source_target_pairs={{0,24},{4,28},{8,0},{12,4},{16,8},{20,12},{24,16},{28,20},{32,56},... | collective-permute-start | bytes 49160 | tf_op jit(solution)/shard_map/ppermute | solution.py:297
  80.8 5.3 %collective-permute-start.7 = (f32[32,128]{1,0:T(8,128)S(1)}, f32[32,128]{1,0:T(8,128)S(1)}, u32[]{:S(2)}, u32[]{:S(2)}) collective-permute-start(f32[32,128]{1,0:T(8,128)S(1)} %add_add_fusion.2), channel_id=1, source_target_pairs={{0,64},{4,68},{8,72},{12,76},{16,80},{20,84},{24,88},{28,92},{32,9... | collective-permute-start | bytes 49160 | tf_op jit(solution)/shard_map/ppermute | solution.py:297
  81.8 4.9 %collective-permute-start.8 = (f32[32,128]{1,0:T(8,128)S(1)}, f32[32,128]{1,0:T(8,128)S(1)}, u32[]{:S(2)}, u32[]{:S(2)}) collective-permute-start(f32[32,128]{1,0:T(8,128)S(1)} %add_add_fusion.2), channel_id=1, source_target_pairs={{0,32},{4,36},{8,40},{12,44},{16,48},{20,52},{24,56},{28,60},{32,6... | collective-permute-start | bytes 49160 | tf_op jit(solution)/shard_map/ppermute | solution.py:297
  82.8 4.0 %collective-permute-start.9 = (f32[32,128]{1,0:T(8,128)S(1)}, f32[32,128]{1,0:T(8,128)S(1)}, u32[]{:S(2)}, u32[]{:S(2)}) collective-permute-start(f32[32,128]{1,0:T(8,128)S(1)} %add_add_fusion.2), channel_id=1, source_target_pairs={{0,96},{4,100},{8,104},{12,108},{16,112},{20,116},{24,120},{28,124... | collective-permute-start | bytes 49160 | tf_op jit(solution)/shard_map/ppermute | solution.py:297
  86.7 8.4 %collective-permute-start.10 = (f32[32,128]{1,0:T(8,128)S(1)}, f32[32,128]{1,0:T(8,128)S(1)}, u32[]{:S(2)}, u32[]{:S(2)}) collective-permute-start(f32[32,128]{1,0:T(8,128)S(1)} %add_add_fusion.1), channel_id=1, source_target_pairs={{0,2},{1,3},{2,0},{3,1},{4,6},{5,7},{6,4},{7,5},{8,10},{9,11},{10,... | collective-permute-start | bytes 49160 | tf_op jit(solution)/shard_map/ppermute | solution.py:297
  89.4 5.7 %collective-permute-start.11 = (f32[32,128]{1,0:T(8,128)S(1)}, f32[32,128]{1,0:T(8,128)S(1)}, u32[]{:S(2)}, u32[]{:S(2)}) collective-permute-start(f32[32,128]{1,0:T(8,128)S(1)} %add_add_fusion.1), channel_id=1, source_target_pairs={{0,1},{1,2},{2,3},{3,0},{4,5},{5,6},{6,7},{7,4},{8,9},{9,10},{10,1... | collective-permute-start | bytes 49160 | tf_op jit(solution)/shard_map/ppermute | solution.py:297
  89.4 5.7 %collective-permute-start.12 = (f32[32,128]{1,0:T(8,128)S(1)}, f32[32,128]{1,0:T(8,128)S(1)}, u32[]{:S(2)}, u32[]{:S(2)}) collective-permute-start(f32[32,128]{1,0:T(8,128)S(1)} %add_add_fusion.1), channel_id=1, source_target_pairs={{0,3},{1,0},{2,1},{3,2},{4,7},{5,4},{6,5},{7,6},{8,11},{9,8},{10,9... | collective-permute-start | bytes 49160 | tf_op jit(solution)/shard_map/ppermute | solution.py:297
  97.9 11.0 %collective-permute-start.13 = (bf16[16,2176]{1,0:T(8,128)(2,1)S(1)}, bf16[16,2176]{1,0:T(8,128)(2,1)S(1)}, u32[]{:S(2)}, u32[]{:S(2)}) collective-permute-start(bf16[16,2176]{1,0:T(8,128)(2,1)S(1)} %get-tuple-element.21.p0_ref), channel_id=1, source_target_pairs={{0,1},{1,2},{2,3},{3,0},{4,5},{5,6},{6,7},{7,4},{8,9},{9,10},{10,1... | collective-permute-start | bytes 208904 | tf_op jit(solution)/shard_map/ppermute | solution.py:336
  97.9 10.9 %collective-permute-start.14 = (bf16[16,2176]{1,0:T(8,128)(2,1)S(1)}, bf16[16,2176]{1,0:T(8,128)(2,1)S(1)}, u32[]{:S(2)}, u32[]{:S(2)}) collective-permute-start(bf16[16,2176]{1,0:T(8,128)(2,1)S(1)} %get-tuple-element.21.p0_ref), channel_id=1, source_target_pairs={{0,2},{1,3},{2,0},{3,1},{4,6},{5,7},{6,4},{7,5},{8,10},{9,11},{10,... | collective-permute-start | bytes 208904 | tf_op jit(solution)/shard_map/ppermute | solution.py:336
  101.8 7.0 %collective-permute-start.15 = (bf16[16,2176]{1,0:T(8,128)(2,1)S(1)}, bf16[16,2176]{1,0:T(8,128)(2,1)S(1)}, u32[]{:S(2)}, u32[]{:S(2)}) collective-permute-start(bf16[16,2176]{1,0:T(8,128)(2,1)S(1)} %get-tuple-element.21.p0_ref), channel_id=1, source_target_pairs={{0,3},{1,0},{2,1},{3,2},{4,7},{5,4},{6,5},{7,6},{8,11},{9,8},{10,9... | collective-permute-start | bytes 208904 | tf_op jit(solution)/shard_map/ppermute | solution.py:336
  116.8 5.4 %collective-permute-start.17 = (f32[16,128]{1,0:T(8,128)S(1)}, f32[16,128]{1,0:T(8,128)S(1)}, u32[]{:S(2)}, u32[]{:S(2)}) collective-permute-start(f32[16,128]{1,0:T(8,128)S(1)} %add.112), channel_id=1, source_target_pairs={{0,16},{4,20},{8,24},{12,28},{16,0},{20,4},{24,8},{28,12},{32,48},... | collective-permute-start | bytes 24584 | tf_op jit(solution)/shard_map/ppermute | solution.py:297
  119.0 4.9 %collective-permute-start.18 = (f32[16,128]{1,0:T(8,128)S(1)}, f32[16,128]{1,0:T(8,128)S(1)}, u32[]{:S(2)}, u32[]{:S(2)}) collective-permute-start(f32[16,128]{1,0:T(8,128)S(1)} %add.112), channel_id=1, source_target_pairs={{0,8},{4,12},{8,16},{12,20},{16,24},{20,28},{24,0},{28,4},{32,40},... | collective-permute-start | bytes 24584 | tf_op jit(solution)/shard_map/ppermute | solution.py:297
  120.9 3.7 %collective-permute-start.19 = (f32[16,128]{1,0:T(8,128)S(1)}, f32[16,128]{1,0:T(8,128)S(1)}, u32[]{:S(2)}, u32[]{:S(2)}) collective-permute-start(f32[16,128]{1,0:T(8,128)S(1)} %add.112), channel_id=1, source_target_pairs={{0,24},{4,28},{8,0},{12,4},{16,8},{20,12},{24,16},{28,20},{32,56},... | collective-permute-start | bytes 24584 | tf_op jit(solution)/shard_map/ppermute | solution.py:297
  124.5 5.4 %collective-permute-start.20 = (f32[16,128]{1,0:T(8,128)S(1)}, f32[16,128]{1,0:T(8,128)S(1)}, u32[]{:S(2)}, u32[]{:S(2)}) collective-permute-start(f32[16,128]{1,0:T(8,128)S(1)} %add_add_fusion.5), channel_id=1, source_target_pairs={{0,64},{4,68},{8,72},{12,76},{16,80},{20,84},{24,88},{28,92},{32,9... | collective-permute-start | bytes 24584 | tf_op jit(solution)/shard_map/ppermute | solution.py:297
  126.7 4.9 %collective-permute-start.21 = (f32[16,128]{1,0:T(8,128)S(1)}, f32[16,128]{1,0:T(8,128)S(1)}, u32[]{:S(2)}, u32[]{:S(2)}) collective-permute-start(f32[16,128]{1,0:T(8,128)S(1)} %add_add_fusion.5), channel_id=1, source_target_pairs={{0,32},{4,36},{8,40},{12,44},{16,48},{20,52},{24,56},{28,60},{32,6... | collective-permute-start | bytes 24584 | tf_op jit(solution)/shard_map/ppermute | solution.py:297
  132.3 6.1 %collective-permute-start.23 = (f32[16,128]{1,0:T(8,128)S(1)}, f32[16,128]{1,0:T(8,128)S(1)}, u32[]{:S(2)}, u32[]{:S(2)}) collective-permute-start(f32[16,128]{1,0:T(8,128)S(1)} %add_add_fusion.4), channel_id=1, source_target_pairs={{0,2},{1,3},{2,0},{3,1},{4,6},{5,7},{6,4},{7,5},{8,10},{9,11},{10,... | collective-permute-start | bytes 24584 | tf_op jit(solution)/shard_map/ppermute | solution.py:297
  134.5 4.9 %collective-permute-start.24 = (f32[16,128]{1,0:T(8,128)S(1)}, f32[16,128]{1,0:T(8,128)S(1)}, u32[]{:S(2)}, u32[]{:S(2)}) collective-permute-start(f32[16,128]{1,0:T(8,128)S(1)} %add_add_fusion.4), channel_id=1, source_target_pairs={{0,1},{1,2},{2,3},{3,0},{4,5},{5,6},{6,7},{7,4},{8,9},{9,10},{10,1... | collective-permute-start | bytes 24584 | tf_op jit(solution)/shard_map/ppermute | solution.py:297
  134.5 4.9 %collective-permute-start.25 = (f32[16,128]{1,0:T(8,128)S(1)}, f32[16,128]{1,0:T(8,128)S(1)}, u32[]{:S(2)}, u32[]{:S(2)}) collective-permute-start(f32[16,128]{1,0:T(8,128)S(1)} %add_add_fusion.4), channel_id=1, source_target_pairs={{0,3},{1,0},{2,1},{3,2},{4,7},{5,4},{6,5},{7,6},{8,11},{9,8},{10,9... | collective-permute-start | bytes 24584 | tf_op jit(solution)/shard_map/ppermute | solution.py:297
  (15 other events, 98.0 us)

commit v3 on v2

--- a/solution.py
+++ b/solution.py
@@ -24,6 +24,9 @@
 LROWS = 112
 LAG_TOP = 106
 BINS_STEP = 4
+PACK_ROWS = 64
+PACK_OUT = 4
+PACK_VMEM = 63 * 1024 * 1024
 BETA = 24.0
 EPS = 1e-06
 F32 = jnp.float32
@@ -43,8 +46,22 @@
     return lax.broadcasted_iota(jnp.int32, shape, axis)
 
 
-def pack_kernel(shot_ref, rec_ref, bin_ref, cls_ref, shift_ref, frac_ref, x_ref, out_ref, y_ref):
-    shot, rec, bin_, cls = shot_ref[...], rec_ref[...], bin_ref[...], cls_ref[...]
+def pack_kernel(*refs):
+    meta_in, x_in, out_ref = refs[:6], refs[6], refs[7]
+    meta_refs, (x_ref, y_ref, o_ref, meta_sem, x_sem, o_sem) = refs[8:14], refs[14:]
+    parts = TR_DEV // PACK_ROWS
+    x_copies = [
+        pltpu.make_async_copy(
+            x_in.at[pl.ds(i * PACK_ROWS, PACK_ROWS), :], x_ref.at[pl.ds(i * PACK_ROWS, PACK_ROWS), :], x_sem.at[i]
+        )
+        for i in range(parts)
+    ]
+    meta_copies = [pltpu.make_async_copy(meta_in[i], meta_refs[i], meta_sem.at[i]) for i in range(6)]
+    for copy in meta_copies + x_copies:
+        copy.start()
+    for copy in meta_copies:
+        copy.wait()
+    shot, rec, bin_, cls, whole, frac = [ref[...] for ref in meta_refs]
     dest = (bin_ // BIN_DEV) * CLASSES + cls
     rows = [
         shot // 128,
@@ -52,9 +69,9 @@
         rec // 128,
         rec % 128,
         bin_ % BIN_DEV,
-        frac_ref[...],
+        frac,
         jnp.ones_like(shot),
-        shift_ref[...] + SHIFT_MAX,
+        whole + SHIFT_MAX,
         dest,
     ]
     sub = iota((16, TR_DEV), 0)
@@ -73,13 +90,27 @@
     cols = cols.astype(BF16)
     step = 32
     for r in range(0, TR_DEV, step):
+        if r % PACK_ROWS == 0:
+            x_copies[r // PACK_ROWS].wait()
         y = jnp.concatenate([x_ref[r : r + step, :], jnp.zeros((step, LANES), BF16)], axis=1)
         y = pltpu.roll(y, SHIFT_MAX, 1)
         for bit in range(5):
             y = jnp.where(on[bit][r : r + step, :], pltpu.roll(y, WIDE - (1 << bit), 1), y)
         y_ref[r : r + step, :NS] = y[:, :NS]
         y_ref[r : r + step, NS:] = y[:, NS:] + cols[r : r + step, :]
-    out_ref[...] = dot(onehot, y_ref[...], NN).reshape(DEVICES, TRACE_LIMIT, WIDE).astype(BF16)
+    out_copies = []
+    group = DEVICES // PACK_OUT
+    for i in range(PACK_OUT):
+        rows = onehot[i * group * TRACE_LIMIT : (i + 1) * group * TRACE_LIMIT, :]
+        placed = dot(rows, y_ref[...], NN).reshape(group, TRACE_LIMIT, WIDE).astype(BF16)
+        o_ref[i * group : (i + 1) * group] = placed
+        copy = pltpu.make_async_copy(
+            o_ref.at[pl.ds(i * group, group)], out_ref.at[pl.ds(i * group, group)], o_sem.at[i]
+        )
+        copy.start()
+        out_copies.append(copy)
+    for copy in out_copies:
+        copy.wait()
 
 
 def one_hot_rows(row, count):
@@ -124,15 +155,34 @@
     stack_rows(weight_ref[0, 0], y_ref, head, head[5:6, :] * (1.0 / NPHASE), side_ref, part_ref, sum_ref)
 
 
-def next_kernel(weight_ref, y_ref, head_ref, rec_ref, shot_ref, part_ref, side_ref, sum_ref):
+def paired(refs):
+    return (refs[0][...] + refs[2][...]) + (refs[1][...] + refs[3][...])
+
+
+def next_kernel(
+    weight_ref, index_ref, table_ref, y_ref, head_ref, g0, g1, g2, g3, part_ref, side_ref, known_ref, sum_ref
+):
+    damp = table_ref[index_ref[0]]
+    sums = paired((g0, g1, g2, g3))
+    known_ref[0:8, :] = sums[0:8, :] / ((1.0 + damp) * sums[8:16, :] + damp)
+    known_ref[8:16, :] = sums[16:24, :] / ((1.0 + damp) * sums[24:32, :] + damp)
+    known_ref[16:24, :] = sums[8:16, :]
+    known_ref[24:32, :] = sums[24:32, :]
     head = head_ref[0:16, :]
     frac = head[5:6, :] * (1.0 / NPHASE)
-    for table_ref, at in ((shot_ref, 0), (rec_ref, 2)):
+    for base, at in ((8, 0), (0, 2)):
         low = one_hot_rows(head[at + 1 : at + 2, :], 128)
         high = one_hot_rows(head[at : at + 1, :], 8)
-        found = dot(table_ref[...], low, NN, lax.Precision.HIGHEST)
+        found = dot(known_ref[base : base + 8, :], low, NN, lax.Precision.HIGHEST)
         frac = frac + jnp.sum(found * high, axis=0, keepdims=True)
     stack_rows(weight_ref[0, 0], y_ref, head, frac, side_ref, part_ref, sum_ref)
+
+
+def last_kernel(index_ref, table_ref, known_ref, g0, g1, g2, g3, rec_ref, shot_ref):
+    damp = table_ref[index_ref[1]]
+    sums = paired((g0, g1, g2, g3))
+    rec_ref[...] = known_ref[0:8, :] + sums[0:8, :] / ((1.0 + damp) * known_ref[16:24, :] + damp)
+    shot_ref[...] = known_ref[8:10, :] + sums[8:10, :] / ((1.0 + damp) * known_ref[24:26, :] + damp)
 
 
 def shift_kernel(y_ref, side_ref, st_ref, energy_ref, xt_ref):
@@ -193,11 +243,14 @@
     corr = jnp.zeros((LROWS, SLOTS), F32)
     for b0 in range(0, BIN_DEV, BINS_STEP):
         for bb in range(BINS_STEP):
-            row = jnp.broadcast_to(wide_ref[b0 + bb : b0 + bb + 1, :], (16, WIDE)).astype(BF16)
-            row = pltpu.roll(row, 0, 1, stride=1, stride_axis=0)
+            row = jnp.broadcast_to(wide_ref[b0 + bb : b0 + bb + 1, :], (8, WIDE))
             for g in range(0, LROWS, 16):
+                two = [
+                    pltpu.roll(row, (WIDE - (LAG_TOP - HALF) + g + h) % WIDE, 1, stride=1, stride_axis=0)[:, :NS]
+                    for h in (0, 8)
+                ]
                 at = (b0 + bb) * LROWS + g
-                lag_ref[at : at + 16, :] = pltpu.roll(row, (WIDE - (LAG_TOP - HALF) + g) % WIDE, 1)[:, :NS]
+                lag_ref[at : at + 16, :] = jnp.concatenate(two, axis=0).astype(BF16)
         every = dot(lag_ref[b0 * LROWS : (b0 + BINS_STEP) * LROWS, :], st_ref[...], NN)
         for bb in range(BINS_STEP):
             corr = corr + member[b0 + bb : b0 + bb + 1, :] * every[bb * LROWS : (bb + 1) * LROWS, :]
@@ -219,6 +272,7 @@
 
 
 VMEM = pl.BlockSpec(memory_space=pltpu.VMEM)
+HBM = pl.BlockSpec(memory_space=pl.ANY)
 SMEM = pl.BlockSpec(memory_space=pltpu.SMEM)
 PARAMS = pltpu.CompilerParams(vmem_limit_bytes=40 * 1024 * 1024)
 
@@ -241,17 +295,23 @@
 
 
 def pack(traces, *meta):
-    return call(
+    scratch = [pltpu.VMEM((1, TR_DEV), jnp.int32)] * 6 + [
+        pltpu.VMEM((TR_DEV, NS), BF16),
+        pltpu.VMEM((TR_DEV, WIDE), BF16),
+        pltpu.VMEM((DEVICES, TRACE_LIMIT, WIDE), BF16),
+        pltpu.SemaphoreType.DMA((6,)),
+        pltpu.SemaphoreType.DMA((TR_DEV // PACK_ROWS,)),
+        pltpu.SemaphoreType.DMA((PACK_OUT,)),
+    ]
+    return pl.pallas_call(
         pack_kernel,
-        shape((DEVICES, TRACE_LIMIT, WIDE), BF16),
-        (0,) * 7,
-        [pltpu.VMEM((TR_DEV, WIDE), BF16)],
-        "pack",
-        10**9,
-        3 * 2**20,
-        *[row.reshape(1, TR_DEV) for row in meta],
-        traces,
-    )
+        out_shape=shape((DEVICES, TRACE_LIMIT, WIDE), BF16),
+        in_specs=[HBM] * 7,
+        out_specs=HBM,
+        scratch_shapes=scratch,
+        compiler_params=pltpu.CompilerParams(vmem_limit_bytes=PACK_VMEM),
+        name="pack",
+    )(*[row.reshape(1, TR_DEV) for row in meta], traces)
 
 
 PART = shape((BIN_DEV, WIDE), BF16)
@@ -264,10 +324,20 @@
     return call(first_kernel, out, (1, 0), [ROWS], "stack_first", 3 * 10**9, 10**7, weight, slots)
 
 
-def stack_next(weight, rows, side, rec, shot):
+KNOWN = shape((32, LANES), F32)
+
+
+def stack_next(weight, index, table, rows, side, sums):
+    memory = (1, 1, 1) + (0,) * 6
+    out = (PART, SIDE, KNOWN)
     return call(
-        next_kernel, (PART, SIDE), (1, 0, 0, 0, 0), [ROWS], "stack_next", 3 * 10**9, 10**7, weight, rows, side, rec, shot
+        next_kernel, out, memory, [ROWS], "stack_next", 3 * 10**9, 10**7, weight, index, table, rows, side, *sums
     )
+
+
+def finish(index, table, known, sums):
+    out = (shape((8, LANES), F32), shape((2, LANES), F32))
+    return call(last_kernel, out, (1, 1) + (0,) * 5, [], "finish", 10**4, 10**5, index, table, known, *sums)
 
 
 def shift(rows, side):
@@ -304,11 +374,18 @@
     return [(i, (i + d) % 4) for i in range(4)]
 
 
-def sum_all(value):
+def sum_most(value):
     value = ring_sum(value, "cmp", [cmp_pairs(lambda y, x, c: (y, x, 1 - c))])
     value = ring_sum(value, "cmp", [cmp_pairs(lambda y, x, c, d=d: (y, (x + d) % 4, c)) for d in (1, 2, 3)])
     value = ring_sum(value, "cmp", [cmp_pairs(lambda y, x, c, d=d: ((y + d) % 4, x, c)) for d in (1, 2, 3)])
-    return ring_sum(value, "off", [off_perm(d) for d in (1, 2, 3)])
+    return (value, *[lax.ppermute(value, "off", off_perm(d)) for d in (1, 2, 3)])
+
+
+def from_stack(first, part, rows, side):
+    others = [lax.ppermute(part, "off", off_perm(d)) for d in (1, 2, 3)]
+    shifted, energy = shift(rows, side)
+    pilot, sums = correlate(first, (part, *others), shifted, energy, side)
+    return pilot, sum_most(sums)
 
 
 def on_device(
@@ -325,27 +402,12 @@
     outgoing = pack(traces, shot_id, receiver_id, cmp_bin, offset_class, shift_int, frac_index)
     slots = lax.all_to_all(outgoing, ("cmp", "off"), split_axis=0, concat_axis=0, tiled=True)
     weight = (1.0 / (1.0 + lax.axis_index("off").astype(F32))).reshape(1, 1)
-    entries = jnp.arange(damping_table.shape[0], dtype=jnp.int32)
-    damps = [jnp.sum(jnp.where(entries == damping_index[i], damping_table, 0.0)) for i in range(2)]
-    for iteration in range(2):
-        first = iteration == 0
-        if first:
-            part, side, rows = stack_first(weight, slots)
-        else:
-            part, side = stack_next(weight, rows, side, rec, shot)
-        others = [lax.ppermute(part, "off", off_perm(d)) for d in (1, 2, 3)]
-        shifted, energy = shift(rows, side)
-        pilot, sums = correlate(first, (part, *others), shifted, energy, side)
-        sums = sum_all(sums)
-        damp = damps[iteration]
-        if first:
-            rec_count, shot_count = sums[8:16], sums[24:32]
-            rec = sums[0:8] / ((1.0 + damp) * rec_count + damp)
-            shot = sums[16:24] / ((1.0 + damp) * shot_count + damp)
-        else:
-            rec = rec + sums[0:8] / ((1.0 + damp) * rec_count + damp)
-            shot = shot + sums[8:16] / ((1.0 + damp) * shot_count + damp)
-    return (shot[0:2].reshape(256), rec.reshape(1024), pilot)
+    part, side, rows = stack_first(weight, slots)
+    pilot, sums = from_stack(True, part, rows, side)
+    part, side, known = stack_next(weight, damping_index, damping_table, rows, side, sums)
+    pilot, sums = from_stack(False, part, rows, side)
+    rec, shot = finish(damping_index, damping_table, known, sums)
+    return (shot.reshape(-1), rec.reshape(-1), pilot)
 
 
 def solution(mesh):

time: 142 us -> 135 us (0.951)
  waiting for transfers between devices: 42 us -> 56.4 us
  starting transfers between devices: 49.9 us -> 41 us
  local copies, waits for them, and re-layouts: 7.82 us -> 0.01 us
  other arithmetic: 3.75 us -> 0.03 us
    ppermute x20 -> x14, starting transfers between devices: 31.2 us -> 14.2 us  [ring_sum(): got = [lax.ppermute(value, axis, perm) for perm in perms]]
    ppermute x6 -> x12, starting transfers between devices: 7.62 us -> 15.7 us  [the longest x6 9.42 us: sum_most(): lax.ppermute(value, 'off', off_perm(d))]
    ppermute x6 -> x12, waiting for transfers between devices: 0.02 us -> 7.56 us  [the longest x6 7.55 us: sum_most(): lax.ppermute(value, 'off', off_perm(d))]
    ppermute x20 -> x14, waiting for transfers between devices: 10.8 us -> 17.7 us  [ring_sum(): got = [lax.ppermute(value, axis, perm) for perm in perms]]
    unnamed x24 -> x4, local copies, waits for them, and re-layouts: 6.68 us -> 0.01 us
    pallas_call x0 -> x1, Pallas kernels: none -> 6.26 us  [pack(): pl.pallas_call(pack_kernel, out_shape=shape((DEVICES, TRACE_LIMIT, WIDE),...]
    pallas_call x7, Pallas kernels: 35.6 us -> 30.1 us  [call(): pl.pallas_call(kernel, out_shape=out, in_specs=[SMEM if space else VMEM f...]
    reduce_sum x1 -> x0, other arithmetic: 1.92 us -> none  [on_device(): jnp.sum(jnp.where(entries == damping_index[i], damping_table, 0.0))]
  transfers between devices with their start and end apart: 27 -> 27, of which waited for: 12 -> 18; matrix products, arithmetic and copies ran while one was open for 2% -> 0% of each run, Pallas kernels for 10% -> 10%
where the time goes in v3:
time: 135 us
  waiting for transfers between devices  56.4 us (42%)
  starting transfers between devices  41 us (30%)
  Pallas kernels  36.3 us (27%)
    all_to_all x1, waiting for transfers between devices, on_device(): lax.all_to_all(outgoing, ('cmp', 'off'), split_axis=0, concat_axis=0, til...  31.1 us
    pallas_call x7, Pallas kernels, call(): pl.pallas_call(kernel, out_shape=out, in_specs=[SMEM if space else VMEM f...  30.1 us
    ppermute x14, waiting for transfers between devices, ring_sum(): got = [lax.ppermute(value, axis, perm) for perm in perms]  17.7 us
    ppermute x14, starting transfers between devices, ring_sum(): got = [lax.ppermute(value, axis, perm) for perm in perms]  14.2 us
    all_to_all x1, starting transfers between devices, on_device(): lax.all_to_all(outgoing, ('cmp', 'off'), split_axis=0, concat_axis=0, til...  11.1 us
    ppermute x6, starting transfers between devices, sum_most(): lax.ppermute(value, 'off', off_perm(d))  9.42 us
    ppermute x6, waiting for transfers between devices, sum_most(): lax.ppermute(value, 'off', off_perm(d))  7.55 us
    pallas_call x1, Pallas kernels, pack(): pl.pallas_call(pack_kernel, out_shape=shape((DEVICES, TRACE_LIMIT, WIDE),...  6.26 us
  transfers between devices with their start and end apart: 27, of which 18 were waited for; matrix products, arithmetic and copies ran while one was open for 0% of the time, Pallas kernels for 10%

profile of v3, /device:TPU:0, one launch (start us, length us, event | category | flops | bytes accessed | tf_op | source)
XLA Modules:
  0.0 134.6 jit_solution(334175568070303754)
XLA Ops:
  0.6 6.3 %pack.1 = bf16[128,4,2176]{2,1,0:T(4,128)(2,1)} custom-call(s32[1,256]{1,0:T(1,128)} %bitcast.9, s32[1,256]{1,0:T(1,128)} %bitcast.10, s32[1,256]{1,0:T(1,128)} %bitcast.11, s32[1,256]{1,0:T(1,128)} %bitcast.12, s32[1,256]{1,0:T(1,128)} %bitcast.13, s32[1,256]{1,0:T(1,128)} %bitcast.14, bf16[256,2048]{1,0:T(8,128)(2,1)} %refs_6_.1), custom_call_target="tpu_custom_call" | custom-call | tf_op jit(solution)/shard_map/pack/pallas_call | solution.py:306
  6.9 11.1 %all-to-all-start = ((bf16[128,4,2176]{2,1,0:T(4,128)(2,1)}), bf16[128,4,2176]{2,1,0:T(4,128)(2,1)S(1)}, u32[]{:S(2)}, u32[]{:S(2)}) async-start(bf16[128,4,2176]{2,1,0:T(4,128)(2,1)} %pack.1), calls=%async_computation | async-start | bytes 4456448 | tf_op jit(solution)/shard_map/all_to_all | solution.py:403
  18.1 31.1 %all-to-all-done.slots_ref = bf16[128,4,2176]{2,1,0:T(4,128)(2,1)S(1)} async-done(((bf16[128,4,2176]{2,1,0:T(4,128)(2,1)}), bf16[128,4,2176]{2,1,0:T(4,128)(2,1)S(1)}, u32[]{:S(2)}, u32[]{:S(2)}) %all-to-all-start) | async-done | bytes 2228256 | tf_op jit(solution)/shard_map/all_to_all | solution.py:403
  49.2 2.0 %stack_first.1 = (bf16[16,2176]{1,0:T(8,128)(2,1)S(1)}, f32[32,512]{1,0:T(8,128)S(1)}, bf16[512,2176]{1,0:T(8,128)(2,1)S(1)}) custom-call(f32[1,1]{1,0:T(1,128)} %bitcast.weight_ref, bf16[128,4,2176]{2,1,0:T(4,128)(2,1)S(1)} %all-to-all-done.slots_ref), custom_call_target="tpu_custom_call" | custom-call | flops 3000000000 | bytes 10000000 | tf_op jit(solution)/shard_map/stack_first/pallas_call | solution.py:285
  52.4 1.8 %collective-permute-start.1 = (bf16[16,2176]{1,0:T(8,128)(2,1)S(1)}, bf16[16,2176]{1,0:T(8,128)(2,1)S(1)}, u32[]{:S(2)}, u32[]{:S(2)}) collective-permute-start(bf16[16,2176]{1,0:T(8,128)(2,1)S(1)} %get-tuple-element.20.p0_ref), channel_id=1, source_target_pairs={{0,2},{1,3},{2,0},{3,1},{4,6},{5,7},{6,4},{7,5},{8,10},{9,11},{10,... | collective-permute-start | bytes 208904 | tf_op jit(solution)/shard_map/ppermute | solution.py:385
  54.2 7.0 %shift.2 = (bf16[2048,512]{1,0:T(8,128)(2,1)S(1)}, f32[8,512]{1,0:T(8,128)S(1)}) custom-call(bf16[512,2176]{1,0:T(8,128)(2,1)S(1)} %get-tuple-element.18.y_ref, f32[32,512]{1,0:T(8,128)S(1)} %get-tuple-element.19.side_ref.head_ref), custom_call_target="tpu_custom_call" | custom-call | flops 6000000000 | bytes 20000000 | tf_op jit(solution)/shard_map/shift/pallas_call | solution.py:285
  61.2 5.2 %correlate.2 = (bf16[16,2048]{1,0:T(8,128)(2,1)}, f32[32,128]{1,0:T(8,128)S(1)}) custom-call(bf16[16,2176]{1,0:T(8,128)(2,1)S(1)} %get-tuple-element.20.p0_ref, bf16[16,2176]{1,0:T(8,128)(2,1)S(1)} %collective-permute-done.p1_ref, bf16[16,2176]{1,0:T(8,128)(2,1)S(1)} %collective-permute-done.1.p2_ref, bf16[16,2176]{1,0:T(8,128)(2,1)S(1)} %collective-permute-done.2.p3_ref, ...), custom_call_target="tpu_custom_call" | custom-call | flops 4000000000 | bytes 10000000 | tf_op jit(solution)/shard_map/correlate/pallas_call | solution.py:285
  69.6 1.5 %collective-permute-start.4 = (f32[32,128]{1,0:T(8,128)S(1)}, f32[32,128]{1,0:T(8,128)S(1)}, u32[]{:S(2)}, u32[]{:S(2)}) collective-permute-start(f32[32,128]{1,0:T(8,128)S(1)} %add.46), channel_id=1, source_target_pairs={{0,16},{4,20},{8,24},{12,28},{16,0},{20,4},{24,8},{28,12},{32,48},... | collective-permute-start | bytes 49160 | tf_op jit(solution)/shard_map/ppermute | solution.py:367
  71.3 2.6 %collective-permute-done.5 = f32[32,128]{1,0:T(8,128)S(1)} collective-permute-done((f32[32,128]{1,0:T(8,128)S(1)}, f32[32,128]{1,0:T(8,128)S(1)}, u32[]{:S(2)}, u32[]{:S(2)}) %collective-permute-start.5) | collective-permute-done | bytes 16416 | tf_op jit(solution)/shard_map/ppermute | solution.py:367
  78.8 2.2 %collective-permute-done.8 = f32[32,128]{1,0:T(8,128)S(1)} collective-permute-done((f32[32,128]{1,0:T(8,128)S(1)}, f32[32,128]{1,0:T(8,128)S(1)}, u32[]{:S(2)}, u32[]{:S(2)}) %collective-permute-start.8) | collective-permute-done | bytes 16416 | tf_op jit(solution)/shard_map/ppermute | solution.py:367
  82.2 3.3 %collective-permute-start.12 = (f32[32,128]{1,0:T(8,128)S(1)}, f32[32,128]{1,0:T(8,128)S(1)}, u32[]{:S(2)}, u32[]{:S(2)}) collective-permute-start(f32[32,128]{1,0:T(8,128)S(1)} %add_add_fusion.g0), channel_id=1, source_target_pairs={{0,3},{1,0},{2,1},{3,2},{4,7},{5,4},{6,5},{7,6},{8,11},{9,8},{10,9... | collective-permute-start | bytes 49160 | tf_op jit(solution)/shard_map/ppermute | solution.py:381
  87.0 3.8 %collective-permute-done.11.g2 = f32[32,128]{1,0:T(8,128)S(1)} collective-permute-done((f32[32,128]{1,0:T(8,128)S(1)}, f32[32,128]{1,0:T(8,128)S(1)}, u32[]{:S(2)}, u32[]{:S(2)}) %collective-permute-start.11) | collective-permute-done | bytes 16416 | tf_op jit(solution)/shard_map/ppermute | solution.py:381
  91.0 2.7 %stack_next.1 = (bf16[16,2176]{1,0:T(8,128)(2,1)S(1)}, f32[32,512]{1,0:T(8,128)S(1)}, f32[32,128]{1,0:T(8,128)S(1)}) custom-call(f32[1,1]{1,0:T(1,128)} %bitcast.weight_ref, s32[2]{0:T(128)S(1)} %copy-done, f32[8]{0:T(128)S(1)} %copy-done.1, bf16[512,2176]{1,0:T(8,128)(2,1)S(1)} %get-tuple-element.18.y_ref, ...), custom_call_target="tpu_custom_call" | custom-call | flops 3000000000 | bytes 10000000 | tf_op jit(solution)/shard_map/stack_next/pallas_call | solution.py:285
  96.9 7.0 %shift.3 = (bf16[2048,512]{1,0:T(8,128)(2,1)S(1)}, f32[8,512]{1,0:T(8,128)S(1)}) custom-call(bf16[512,2176]{1,0:T(8,128)(2,1)S(1)} %get-tuple-element.18.y_ref, f32[32,512]{1,0:T(8,128)S(1)} %get-tuple-element.26.side_ref), custom_call_target="tpu_custom_call" | custom-call | flops 6000000000 | bytes 20000000 | tf_op jit(solution)/shard_map/shift/pallas_call | solution.py:285
  104.0 5.1 %correlate.3 = (bf16[16,2048]{1,0:T(8,128)(2,1)}, f32[16,128]{1,0:T(8,128)S(1)}) custom-call(bf16[16,2176]{1,0:T(8,128)(2,1)S(1)} %get-tuple-element.25.p0_ref, bf16[16,2176]{1,0:T(8,128)(2,1)S(1)} %collective-permute-done.13.p1_ref, bf16[16,2176]{1,0:T(8,128)(2,1)S(1)} %collective-permute-done.14.p2_ref, ...), custom_call_target="tpu_custom_call" | custom-call | flops 4000000000 | bytes 10000000 | tf_op jit(solution)/shard_map/correlate/pallas_call | solution.py:285
  110.3 2.6 %collective-permute-start.19 = (f32[16,128]{1,0:T(8,128)S(1)}, f32[16,128]{1,0:T(8,128)S(1)}, u32[]{:S(2)}, u32[]{:S(2)}) collective-permute-start(f32[16,128]{1,0:T(8,128)S(1)} %add.53), channel_id=1, source_target_pairs={{0,24},{4,28},{8,0},{12,4},{16,8},{20,12},{24,16},{28,20},{32,56},... | collective-permute-start | bytes 24584 | tf_op jit(solution)/shard_map/ppermute | solution.py:367
  112.9 1.5 %collective-permute-start.17 = (f32[16,128]{1,0:T(8,128)S(1)}, f32[16,128]{1,0:T(8,128)S(1)}, u32[]{:S(2)}, u32[]{:S(2)}) collective-permute-start(f32[16,128]{1,0:T(8,128)S(1)} %add.53), channel_id=1, source_target_pairs={{0,16},{4,20},{8,24},{12,28},{16,0},{20,4},{24,8},{28,12},{32,48},... | collective-permute-start | bytes 24584 | tf_op jit(solution)/shard_map/ppermute | solution.py:367
  114.4 3.4 %collective-permute-done.18 = f32[16,128]{1,0:T(8,128)S(1)} collective-permute-done((f32[16,128]{1,0:T(8,128)S(1)}, f32[16,128]{1,0:T(8,128)S(1)}, u32[]{:S(2)}, u32[]{:S(2)}) %collective-permute-start.18) | collective-permute-done | bytes 8224 | tf_op jit(solution)/shard_map/ppermute | solution.py:367
  118.1 1.9 %collective-permute-start.22 = (f32[16,128]{1,0:T(8,128)S(1)}, f32[16,128]{1,0:T(8,128)S(1)}, u32[]{:S(2)}, u32[]{:S(2)}) collective-permute-start(f32[16,128]{1,0:T(8,128)S(1)} %add_add_fusion.3), channel_id=1, source_target_pairs={{0,96},{4,100},{8,104},{12,108},{16,112},{20,116},{24,120},{28,124... | collective-permute-start | bytes 24584 | tf_op jit(solution)/shard_map/ppermute | solution.py:367
  120.1 1.4 %collective-permute-start.20 = (f32[16,128]{1,0:T(8,128)S(1)}, f32[16,128]{1,0:T(8,128)S(1)}, u32[]{:S(2)}, u32[]{:S(2)}) collective-permute-start(f32[16,128]{1,0:T(8,128)S(1)} %add_add_fusion.3), channel_id=1, source_target_pairs={{0,64},{4,68},{8,72},{12,76},{16,80},{20,84},{24,88},{28,92},{32,9... | collective-permute-start | bytes 24584 | tf_op jit(solution)/shard_map/ppermute | solution.py:367
  121.7 3.1 %collective-permute-done.21 = f32[16,128]{1,0:T(8,128)S(1)} collective-permute-done((f32[16,128]{1,0:T(8,128)S(1)}, f32[16,128]{1,0:T(8,128)S(1)}, u32[]{:S(2)}, u32[]{:S(2)}) %collective-permute-start.21) | collective-permute-done | bytes 8224 | tf_op jit(solution)/shard_map/ppermute | solution.py:367
  125.3 1.9 %collective-permute-start.25 = (f32[16,128]{1,0:T(8,128)S(1)}, f32[16,128]{1,0:T(8,128)S(1)}, u32[]{:S(2)}, u32[]{:S(2)}) collective-permute-start(f32[16,128]{1,0:T(8,128)S(1)} %add_add_fusion.2.g0), channel_id=1, source_target_pairs={{0,3},{1,0},{2,1},{3,2},{4,7},{5,4},{6,5},{7,6},{8,11},{9,8},{10,9... | collective-permute-start | bytes 24584 | tf_op jit(solution)/shard_map/ppermute | solution.py:381
  127.2 1.4 %collective-permute-start.24 = (f32[16,128]{1,0:T(8,128)S(1)}, f32[16,128]{1,0:T(8,128)S(1)}, u32[]{:S(2)}, u32[]{:S(2)}) collective-permute-start(f32[16,128]{1,0:T(8,128)S(1)} %add_add_fusion.2.g0), channel_id=1, source_target_pairs={{0,2},{1,3},{2,0},{3,1},{4,6},{5,7},{6,4},{7,5},{8,10},{9,11},{10,... | collective-permute-start | bytes 24584 | tf_op jit(solution)/shard_map/ppermute | solution.py:381
  129.9 2.4 %collective-permute-done.24.g2 = f32[16,128]{1,0:T(8,128)S(1)} collective-permute-done((f32[16,128]{1,0:T(8,128)S(1)}, f32[16,128]{1,0:T(8,128)S(1)}, u32[]{:S(2)}, u32[]{:S(2)}) %collective-permute-start.24) | collective-permute-done | bytes 8224 | tf_op jit(solution)/shard_map/ppermute | solution.py:381
  (48 shorter events, 21.4 us)
Async XLA Ops:
  6.9 42.3 %all-to-all-start = ((bf16[128,4,2176]{2,1,0:T(4,128)(2,1)}), bf16[128,4,2176]{2,1,0:T(4,128)(2,1)S(1)}, u32[]{:S(2)}, u32[]{:S(2)}) async-start(bf16[128,4,2176]{2,1,0:T(4,128)(2,1)} %pack.1), calls=%async_computation | async-start | bytes 4456448 | tf_op jit(solution)/shard_map/all_to_all | solution.py:403
  51.2 10.0 %collective-permute-start.2 = (bf16[16,2176]{1,0:T(8,128)(2,1)S(1)}, bf16[16,2176]{1,0:T(8,128)(2,1)S(1)}, u32[]{:S(2)}, u32[]{:S(2)}) collective-permute-start(bf16[16,2176]{1,0:T(8,128)(2,1)S(1)} %get-tuple-element.20.p0_ref), channel_id=1, source_target_pairs={{0,3},{1,0},{2,1},{3,2},{4,7},{5,4},{6,5},{7,6},{8,11},{9,8},{10,9... | collective-permute-start | bytes 208904 | tf_op jit(solution)/shard_map/ppermute | solution.py:385
  52.4 8.8 %collective-permute-start.1 = (bf16[16,2176]{1,0:T(8,128)(2,1)S(1)}, bf16[16,2176]{1,0:T(8,128)(2,1)S(1)}, u32[]{:S(2)}, u32[]{:S(2)}) collective-permute-start(bf16[16,2176]{1,0:T(8,128)(2,1)S(1)} %get-tuple-element.20.p0_ref), channel_id=1, source_target_pairs={{0,2},{1,3},{2,0},{3,1},{4,6},{5,7},{6,4},{7,5},{8,10},{9,11},{10,... | collective-permute-start | bytes 208904 | tf_op jit(solution)/shard_map/ppermute | solution.py:385
  54.2 7.0 %collective-permute-start = (bf16[16,2176]{1,0:T(8,128)(2,1)S(1)}, bf16[16,2176]{1,0:T(8,128)(2,1)S(1)}, u32[]{:S(2)}, u32[]{:S(2)}) collective-permute-start(bf16[16,2176]{1,0:T(8,128)(2,1)S(1)} %get-tuple-element.20.p0_ref), channel_id=1, source_target_pairs={{0,1},{1,2},{2,3},{3,0},{4,5},{5,6},{6,7},{7,4},{8,9},{9,10},{10,1... | collective-permute-start | bytes 208904 | tf_op jit(solution)/shard_map/ppermute | solution.py:385
  67.6 3.7 %collective-permute-start.6 = (f32[32,128]{1,0:T(8,128)S(1)}, f32[32,128]{1,0:T(8,128)S(1)}, u32[]{:S(2)}, u32[]{:S(2)}) collective-permute-start(f32[32,128]{1,0:T(8,128)S(1)} %add.46), channel_id=1, source_target_pairs={{0,24},{4,28},{8,0},{12,4},{16,8},{20,12},{24,16},{28,20},{32,56},... | collective-permute-start | bytes 49160 | tf_op jit(solution)/shard_map/ppermute | solution.py:367
  69.0 4.9 %collective-permute-start.5 = (f32[32,128]{1,0:T(8,128)S(1)}, f32[32,128]{1,0:T(8,128)S(1)}, u32[]{:S(2)}, u32[]{:S(2)}) collective-permute-start(f32[32,128]{1,0:T(8,128)S(1)} %add.46), channel_id=1, source_target_pairs={{0,8},{4,12},{8,16},{12,20},{16,24},{20,28},{24,0},{28,4},{32,40},... | collective-permute-start | bytes 49160 | tf_op jit(solution)/shard_map/ppermute | solution.py:367
  69.6 5.2 %collective-permute-start.4 = (f32[32,128]{1,0:T(8,128)S(1)}, f32[32,128]{1,0:T(8,128)S(1)}, u32[]{:S(2)}, u32[]{:S(2)}) collective-permute-start(f32[32,128]{1,0:T(8,128)S(1)} %add.46), channel_id=1, source_target_pairs={{0,16},{4,20},{8,24},{12,28},{16,0},{20,4},{24,8},{28,12},{32,48},... | collective-permute-start | bytes 49160 | tf_op jit(solution)/shard_map/ppermute | solution.py:367
  74.9 3.9 %collective-permute-start.9 = (f32[32,128]{1,0:T(8,128)S(1)}, f32[32,128]{1,0:T(8,128)S(1)}, u32[]{:S(2)}, u32[]{:S(2)}) collective-permute-start(f32[32,128]{1,0:T(8,128)S(1)} %add_add_fusion.1), channel_id=1, source_target_pairs={{0,96},{4,100},{8,104},{12,108},{16,112},{20,116},{24,120},{28,124... | collective-permute-start | bytes 49160 | tf_op jit(solution)/shard_map/ppermute | solution.py:367
  76.0 4.9 %collective-permute-start.8 = (f32[32,128]{1,0:T(8,128)S(1)}, f32[32,128]{1,0:T(8,128)S(1)}, u32[]{:S(2)}, u32[]{:S(2)}) collective-permute-start(f32[32,128]{1,0:T(8,128)S(1)} %add_add_fusion.1), channel_id=1, source_target_pairs={{0,32},{4,36},{8,40},{12,44},{16,48},{20,52},{24,56},{28,60},{32,6... | collective-permute-start | bytes 49160 | tf_op jit(solution)/shard_map/ppermute | solution.py:367
  77.0 5.2 %collective-permute-start.7 = (f32[32,128]{1,0:T(8,128)S(1)}, f32[32,128]{1,0:T(8,128)S(1)}, u32[]{:S(2)}, u32[]{:S(2)}) collective-permute-start(f32[32,128]{1,0:T(8,128)S(1)} %add_add_fusion.1), channel_id=1, source_target_pairs={{0,64},{4,68},{8,72},{12,76},{16,80},{20,84},{24,88},{28,92},{32,9... | collective-permute-start | bytes 49160 | tf_op jit(solution)/shard_map/ppermute | solution.py:367
  82.2 4.7 %collective-permute-start.12 = (f32[32,128]{1,0:T(8,128)S(1)}, f32[32,128]{1,0:T(8,128)S(1)}, u32[]{:S(2)}, u32[]{:S(2)}) collective-permute-start(f32[32,128]{1,0:T(8,128)S(1)} %add_add_fusion.g0), channel_id=1, source_target_pairs={{0,3},{1,0},{2,1},{3,2},{4,7},{5,4},{6,5},{7,6},{8,11},{9,8},{10,9... | collective-permute-start | bytes 49160 | tf_op jit(solution)/shard_map/ppermute | solution.py:381
  85.5 5.2 %collective-permute-start.11 = (f32[32,128]{1,0:T(8,128)S(1)}, f32[32,128]{1,0:T(8,128)S(1)}, u32[]{:S(2)}, u32[]{:S(2)}) collective-permute-start(f32[32,128]{1,0:T(8,128)S(1)} %add_add_fusion.g0), channel_id=1, source_target_pairs={{0,2},{1,3},{2,0},{3,1},{4,6},{5,7},{6,4},{7,5},{8,10},{9,11},{10,... | collective-permute-start | bytes 49160 | tf_op jit(solution)/shard_map/ppermute | solution.py:381
  86.0 4.9 %collective-permute-start.10 = (f32[32,128]{1,0:T(8,128)S(1)}, f32[32,128]{1,0:T(8,128)S(1)}, u32[]{:S(2)}, u32[]{:S(2)}) collective-permute-start(f32[32,128]{1,0:T(8,128)S(1)} %add_add_fusion.g0), channel_id=1, source_target_pairs={{0,1},{1,2},{2,3},{3,0},{4,5},{5,6},{6,7},{7,4},{8,9},{9,10},{10,1... | collective-permute-start | bytes 49160 | tf_op jit(solution)/shard_map/ppermute | solution.py:381
  93.7 10.3 %collective-permute-start.15 = (bf16[16,2176]{1,0:T(8,128)(2,1)S(1)}, bf16[16,2176]{1,0:T(8,128)(2,1)S(1)}, u32[]{:S(2)}, u32[]{:S(2)}) collective-permute-start(bf16[16,2176]{1,0:T(8,128)(2,1)S(1)} %get-tuple-element.25.p0_ref), channel_id=1, source_target_pairs={{0,3},{1,0},{2,1},{3,2},{4,7},{5,4},{6,5},{7,6},{8,11},{9,8},{10,9... | collective-permute-start | bytes 208904 | tf_op jit(solution)/shard_map/ppermute | solution.py:385
  94.2 9.7 %collective-permute-start.14 = (bf16[16,2176]{1,0:T(8,128)(2,1)S(1)}, bf16[16,2176]{1,0:T(8,128)(2,1)S(1)}, u32[]{:S(2)}, u32[]{:S(2)}) collective-permute-start(bf16[16,2176]{1,0:T(8,128)(2,1)S(1)} %get-tuple-element.25.p0_ref), channel_id=1, source_target_pairs={{0,2},{1,3},{2,0},{3,1},{4,6},{5,7},{6,4},{7,5},{8,10},{9,11},{10,... | collective-permute-start | bytes 208904 | tf_op jit(solution)/shard_map/ppermute | solution.py:385
  95.6 8.3 %collective-permute-start.13 = (bf16[16,2176]{1,0:T(8,128)(2,1)S(1)}, bf16[16,2176]{1,0:T(8,128)(2,1)S(1)}, u32[]{:S(2)}, u32[]{:S(2)}) collective-permute-start(bf16[16,2176]{1,0:T(8,128)(2,1)S(1)} %get-tuple-element.25.p0_ref), channel_id=1, source_target_pairs={{0,1},{1,2},{2,3},{3,0},{4,5},{5,6},{6,7},{7,4},{8,9},{9,10},{10,1... | collective-permute-start | bytes 208904 | tf_op jit(solution)/shard_map/ppermute | solution.py:385
  110.3 4.1 %collective-permute-start.19 = (f32[16,128]{1,0:T(8,128)S(1)}, f32[16,128]{1,0:T(8,128)S(1)}, u32[]{:S(2)}, u32[]{:S(2)}) collective-permute-start(f32[16,128]{1,0:T(8,128)S(1)} %add.53), channel_id=1, source_target_pairs={{0,24},{4,28},{8,0},{12,4},{16,8},{20,12},{24,16},{28,20},{32,56},... | collective-permute-start | bytes 24584 | tf_op jit(solution)/shard_map/ppermute | solution.py:367
  112.9 4.9 %collective-permute-start.18 = (f32[16,128]{1,0:T(8,128)S(1)}, f32[16,128]{1,0:T(8,128)S(1)}, u32[]{:S(2)}, u32[]{:S(2)}) collective-permute-start(f32[16,128]{1,0:T(8,128)S(1)} %add.53), channel_id=1, source_target_pairs={{0,8},{4,12},{8,16},{12,20},{16,24},{20,28},{24,0},{28,4},{32,40},... | collective-permute-start | bytes 24584 | tf_op jit(solution)/shard_map/ppermute | solution.py:367
  112.9 5.2 %collective-permute-start.17 = (f32[16,128]{1,0:T(8,128)S(1)}, f32[16,128]{1,0:T(8,128)S(1)}, u32[]{:S(2)}, u32[]{:S(2)}) collective-permute-start(f32[16,128]{1,0:T(8,128)S(1)} %add.53), channel_id=1, source_target_pairs={{0,16},{4,20},{8,24},{12,28},{16,0},{20,4},{24,8},{28,12},{32,48},... | collective-permute-start | bytes 24584 | tf_op jit(solution)/shard_map/ppermute | solution.py:367
  120.0 4.9 %collective-permute-start.21 = (f32[16,128]{1,0:T(8,128)S(1)}, f32[16,128]{1,0:T(8,128)S(1)}, u32[]{:S(2)}, u32[]{:S(2)}) collective-permute-start(f32[16,128]{1,0:T(8,128)S(1)} %add_add_fusion.3), channel_id=1, source_target_pairs={{0,32},{4,36},{8,40},{12,44},{16,48},{20,52},{24,56},{28,60},{32,6... | collective-permute-start | bytes 24584 | tf_op jit(solution)/shard_map/ppermute | solution.py:367
  120.1 5.2 %collective-permute-start.20 = (f32[16,128]{1,0:T(8,128)S(1)}, f32[16,128]{1,0:T(8,128)S(1)}, u32[]{:S(2)}, u32[]{:S(2)}) collective-permute-start(f32[16,128]{1,0:T(8,128)S(1)} %add_add_fusion.3), channel_id=1, source_target_pairs={{0,64},{4,68},{8,72},{12,76},{16,80},{20,84},{24,88},{28,92},{32,9... | collective-permute-start | bytes 24584 | tf_op jit(solution)/shard_map/ppermute | solution.py:367
  125.3 4.7 %collective-permute-start.25 = (f32[16,128]{1,0:T(8,128)S(1)}, f32[16,128]{1,0:T(8,128)S(1)}, u32[]{:S(2)}, u32[]{:S(2)}) collective-permute-start(f32[16,128]{1,0:T(8,128)S(1)} %add_add_fusion.2.g0), channel_id=1, source_target_pairs={{0,3},{1,0},{2,1},{3,2},{4,7},{5,4},{6,5},{7,6},{8,11},{9,8},{10,9... | collective-permute-start | bytes 24584 | tf_op jit(solution)/shard_map/ppermute | solution.py:381
  127.2 5.2 %collective-permute-start.24 = (f32[16,128]{1,0:T(8,128)S(1)}, f32[16,128]{1,0:T(8,128)S(1)}, u32[]{:S(2)}, u32[]{:S(2)}) collective-permute-start(f32[16,128]{1,0:T(8,128)S(1)} %add_add_fusion.2.g0), channel_id=1, source_target_pairs={{0,2},{1,3},{2,0},{3,1},{4,6},{5,7},{6,4},{7,5},{8,10},{9,11},{10,... | collective-permute-start | bytes 24584 | tf_op jit(solution)/shard_map/ppermute | solution.py:381
  128.6 4.9 %collective-permute-start.23 = (f32[16,128]{1,0:T(8,128)S(1)}, f32[16,128]{1,0:T(8,128)S(1)}, u32[]{:S(2)}, u32[]{:S(2)}) collective-permute-start(f32[16,128]{1,0:T(8,128)S(1)} %add_add_fusion.2.g0), channel_id=1, source_target_pairs={{0,1},{1,2},{2,3},{3,0},{4,5},{5,6},{6,7},{7,4},{8,9},{9,10},{10,1... | collective-permute-start | bytes 24584 | tf_op jit(solution)/shard_map/ppermute | solution.py:381
  (5 other events, 65.5 us)

commit v4 on v3

--- a/solution.py
+++ b/solution.py
@@ -5,6 +5,7 @@
 from jax import lax
 from jax.experimental import pallas as pl
 from jax.experimental.pallas import tpu as pltpu
+from jax.sharding import Mesh
 from jax.sharding import PartitionSpec as P
 
 NS = 2048
@@ -32,6 +33,7 @@
 F32 = jnp.float32
 BF16 = jnp.bfloat16
 HEAD = 16
+AXES = ("y", "x", "core", "off")
 
 NN = (((1,), (0,)), ((), ()))
 NT = (((1,), (1,)), ((), ()))
@@ -155,19 +157,15 @@
     stack_rows(weight_ref[0, 0], y_ref, head, head[5:6, :] * (1.0 / NPHASE), side_ref, part_ref, sum_ref)
 
 
-def paired(refs):
-    return (refs[0][...] + refs[2][...]) + (refs[1][...] + refs[3][...])
-
-
 def next_kernel(
-    weight_ref, index_ref, table_ref, y_ref, head_ref, g0, g1, g2, g3, part_ref, side_ref, known_ref, sum_ref
+    weight_ref, index_ref, table_ref, y_ref, head_ref, sums_ref, part_ref, side_ref, known_ref, sum_ref
 ):
     damp = table_ref[index_ref[0]]
-    sums = paired((g0, g1, g2, g3))
-    known_ref[0:8, :] = sums[0:8, :] / ((1.0 + damp) * sums[8:16, :] + damp)
-    known_ref[8:16, :] = sums[16:24, :] / ((1.0 + damp) * sums[24:32, :] + damp)
-    known_ref[16:24, :] = sums[8:16, :]
-    known_ref[24:32, :] = sums[24:32, :]
+    sums = gathered(sums_ref)
+    count = 256.0 * sums[10:20, :] + sums[20:30, :]
+    known_ref[...] = jnp.zeros_like(known_ref)
+    known_ref[0:10, :] = sums[0:10, :] / ((1.0 + damp) * count + damp)
+    known_ref[16:26, :] = count
     head = head_ref[0:16, :]
     frac = head[5:6, :] * (1.0 / NPHASE)
     for base, at in ((8, 0), (0, 2)):
@@ -178,11 +176,12 @@
     stack_rows(weight_ref[0, 0], y_ref, head, frac, side_ref, part_ref, sum_ref)
 
 
-def last_kernel(index_ref, table_ref, known_ref, g0, g1, g2, g3, rec_ref, shot_ref):
+def last_kernel(index_ref, table_ref, known_ref, sums_ref, rec_ref, shot_ref):
     damp = table_ref[index_ref[1]]
-    sums = paired((g0, g1, g2, g3))
-    rec_ref[...] = known_ref[0:8, :] + sums[0:8, :] / ((1.0 + damp) * known_ref[16:24, :] + damp)
-    shot_ref[...] = known_ref[8:10, :] + sums[8:10, :] / ((1.0 + damp) * known_ref[24:26, :] + damp)
+    step = gathered(sums_ref) / ((1.0 + damp) * known_ref[16:32, :] + damp)
+    total = known_ref[0:16, :] + step
+    rec_ref[...] = total[0:8, :]
+    shot_ref[...] = total[8:10, :]
 
 
 def shift_kernel(y_ref, side_ref, st_ref, energy_ref, xt_ref):
@@ -261,14 +260,33 @@
         exponent, axis=0, keepdims=True
     )
     misfit = -delay * live
-    for at, out in ((2, 0), (0, 16 if first else 8)):
+    grad_ref[...] = jnp.zeros_like(grad_ref)
+    for at, out, rows in ((2, 0, 8), (0, 8, 2)):
         low = one_hot_rows(head[at + 1 : at + 2, :], 128)
         high = one_hot_rows(head[at : at + 1, :], 8)
         values = high * misfit
         if first:
             values = jnp.concatenate([values, high * live], axis=0)
         sums = dot(values, low, NT, lax.Precision.HIGHEST)
-        grad_ref[out : out + sums.shape[0], :] = sums
+        grad_ref[out : out + rows, :] = sums[0:rows, :]
+        if first:
+            grad_ref[16 + out : 16 + out + rows, :] = sums[8 : 8 + rows, :]
+
+
+def spread_kernel(own_ref, other_ref, out_ref, rows_ref):
+    total = own_ref[...] + other_ref[...]
+    rows_ref[...] = jnp.zeros_like(rows_ref)
+    rows_ref[0:10, :] = total[0:10, :]
+    if total.shape[0] > 16:
+        count = total[16:26, :]
+        large = jnp.floor(count * (1.0 / 256.0))
+        rows_ref[10:20, :] = large
+        rows_ref[20:30, :] = count - 256.0 * large
+    out_ref[...] = jnp.broadcast_to(rows_ref[...].astype(BF16)[None], out_ref.shape)
+
+
+def gathered(ref):
+    return jnp.sum(ref[...].astype(F32), axis=0)
 
 
 VMEM = pl.BlockSpec(memory_space=pltpu.VMEM)
@@ -328,16 +346,16 @@
 
 
 def stack_next(weight, index, table, rows, side, sums):
-    memory = (1, 1, 1) + (0,) * 6
+    memory = (1, 1, 1, 0, 0, 0)
     out = (PART, SIDE, KNOWN)
     return call(
-        next_kernel, out, memory, [ROWS], "stack_next", 3 * 10**9, 10**7, weight, index, table, rows, side, *sums
+        next_kernel, out, memory, [ROWS], "stack_next", 3 * 10**9, 10**7, weight, index, table, rows, side, sums
     )
 
 
 def finish(index, table, known, sums):
     out = (shape((8, LANES), F32), shape((2, LANES), F32))
-    return call(last_kernel, out, (1, 1) + (0,) * 5, [], "finish", 10**4, 10**5, index, table, known, *sums)
+    return call(last_kernel, out, (1, 1, 0, 0), [], "finish", 10**4, 10**5, index, table, known, sums)
 
 
 def shift(rows, side):
@@ -353,39 +371,23 @@
     return call(kernel, out, (0,) * 7, scratch, "correlate", 4 * 10**9, 10**7, *parts, shifted, energy, side)
 
 
-def cmp_pairs(move):
-    pairs = []
-    for y in range(4):
-        for x in range(4):
-            for c in range(2):
-                y2, x2, c2 = move(y, x, c)
-                pairs.append(((y * 4 + x) * 2 + c, (y2 * 4 + x2) * 2 + c2))
-    return pairs
-
-
-def ring_sum(value, axis, perms):
-    got = [lax.ppermute(value, axis, perm) for perm in perms]
-    if len(got) == 1:
-        return value + got[0]
-    return (value + got[1]) + (got[0] + got[2])
-
-
 def off_perm(d):
     return [(i, (i + d) % 4) for i in range(4)]
 
 
-def sum_most(value):
-    value = ring_sum(value, "cmp", [cmp_pairs(lambda y, x, c: (y, x, 1 - c))])
-    value = ring_sum(value, "cmp", [cmp_pairs(lambda y, x, c, d=d: (y, (x + d) % 4, c)) for d in (1, 2, 3)])
-    value = ring_sum(value, "cmp", [cmp_pairs(lambda y, x, c, d=d: ((y + d) % 4, x, c)) for d in (1, 2, 3)])
-    return (value, *[lax.ppermute(value, "off", off_perm(d)) for d in (1, 2, 3)])
+def sum_copies(value):
+    other = lax.ppermute(value, "core", [(0, 1), (1, 0)])
+    out = shape((DEVICES // 2, value.shape[0], LANES), BF16)
+    scratch = [pltpu.VMEM(value.shape, F32)]
+    copies = call(spread_kernel, out, (0, 0), scratch, "spread", 10**5, 10**6, value, other)
+    return lax.all_to_all(copies, ("y", "x", "off"), split_axis=0, concat_axis=0, tiled=True)
 
 
 def from_stack(first, part, rows, side):
     others = [lax.ppermute(part, "off", off_perm(d)) for d in (1, 2, 3)]
     shifted, energy = shift(rows, side)
     pilot, sums = correlate(first, (part, *others), shifted, energy, side)
-    return pilot, sum_most(sums)
+    return pilot, sum_copies(sums)
 
 
 def on_device(
@@ -400,7 +402,7 @@
     damping_index,
 ):
     outgoing = pack(traces, shot_id, receiver_id, cmp_bin, offset_class, shift_int, frac_index)
-    slots = lax.all_to_all(outgoing, ("cmp", "off"), split_axis=0, concat_axis=0, tiled=True)
+    slots = lax.all_to_all(outgoing, AXES, split_axis=0, concat_axis=0, tiled=True)
     weight = (1.0 / (1.0 + lax.axis_index("off").astype(F32))).reshape(1, 1)
     part, side, rows = stack_first(weight, slots)
     pilot, sums = from_stack(True, part, rows, side)
@@ -411,17 +413,8 @@
 
 
 def solution(mesh):
-    placed = (
-        P(("cmp", "off"), None),
-        P(("cmp", "off")),
-        P(("cmp", "off")),
-        P(("cmp", "off")),
-        P(("cmp", "off")),
-        P(("cmp", "off")),
-        P(("cmp", "off")),
-        P(),
-        P(),
+    mesh = Mesh(mesh.devices.reshape(4, 4, 2, 4), AXES)
+    placed = (P(AXES, None),) + (P(AXES),) * 6 + (P(), P())
+    return jax.shard_map(
+        on_device, mesh=mesh, in_specs=placed, out_specs=(P(), P(), P(AXES[:3], None)), check_vma=False
     )
-    return jax.shard_map(
-        on_device, mesh=mesh, in_specs=placed, out_specs=(P(), P(), P("cmp", None)), check_vma=False
-    )

time: 135 us -> 126 us (0.933)
  blocking collectives: 0 us -> 38 us
  starting transfers between devices: 41 us -> 16.9 us
  waiting for transfers between devices: 56.4 us -> 33.5 us
    all_to_all x0 -> x2, blocking collectives: none -> 38 us  [sum_copies(): lax.all_to_all(copies, ('y', 'x', 'off'), split_axis=0, concat_axis=0, ti...]
    ppermute x20 -> x2, starting transfers between devices: 23.6 us -> 0.01 us  [sum_copies(): other = lax.ppermute(value, 'core', [(0, 1), (1, 0)])]
    ppermute x20 -> x2, waiting for transfers between devices: 25.3 us -> 2.35 us  [sum_copies(): other = lax.ppermute(value, 'core', [(0, 1), (1, 0)])]
    pallas_call x7 -> x9, Pallas kernels: 30.1 us -> 30.3 us  [call(): pl.pallas_call(kernel, out_shape=out, in_specs=[SMEM if space else VMEM f...]
  transfers between devices with their start and end apart: 27 -> 9, of which waited for: 18 -> 3; matrix products, arithmetic and copies ran while one was open for 0% -> 0% of each run, Pallas kernels for 10% -> 11%
where the time goes in v4:
time: 126 us
  blocking collectives  38 us (30%)
  Pallas kernels  36.5 us (29%)
  waiting for transfers between devices  33.5 us (27%)
  starting transfers between devices  16.9 us (13%)
    all_to_all x2, blocking collectives, sum_copies(): lax.all_to_all(copies, ('y', 'x', 'off'), split_axis=0, concat_axis=0, ti...  38 us
    all_to_all x1, waiting for transfers between devices, on_device(): lax.all_to_all(outgoing, AXES, split_axis=0, concat_axis=0, tiled=True)  31.1 us
    pallas_call x9, Pallas kernels, call(): pl.pallas_call(kernel, out_shape=out, in_specs=[SMEM if space else VMEM f...  30.3 us
    all_to_all x1, starting transfers between devices, on_device(): lax.all_to_all(outgoing, AXES, split_axis=0, concat_axis=0, tiled=True)  11.1 us
    pallas_call x1, Pallas kernels, pack(): pl.pallas_call(pack_kernel, out_shape=shape((DEVICES, TRACE_LIMIT, WIDE),...  6.24 us
    ppermute x6, starting transfers between devices, from_stack(): others = [lax.ppermute(part, 'off', off_perm(d)) for d in (1, 2, 3)]  5.76 us
  transfers between devices with their start and end apart: 9, of which 3 were waited for; matrix products, arithmetic and copies ran while one was open for 0% of the time, Pallas kernels for 11%

profile of v4, /device:TPU:0, one launch (start us, length us, event | category | flops | bytes accessed | tf_op | source)
XLA Modules:
  0.0 125.7 jit_solution(17903540722679216300)
XLA Ops:
  0.6 6.2 %pack.1 = bf16[128,4,2176]{2,1,0:T(4,128)(2,1)} custom-call(s32[1,256]{1,0:T(1,128)} %bitcast.9, s32[1,256]{1,0:T(1,128)} %bitcast.10, s32[1,256]{1,0:T(1,128)} %bitcast.11, s32[1,256]{1,0:T(1,128)} %bitcast.12, s32[1,256]{1,0:T(1,128)} %bitcast.13, s32[1,256]{1,0:T(1,128)} %bitcast.14, bf16[256,2048]{1,0:T(8,128)(2,1)} %refs_6_.1), custom_call_target="tpu_custom_call" | custom-call | tf_op jit(solution)/shard_map/pack/pallas_call | solution.py:324
  6.9 11.1 %all-to-all-start = ((bf16[128,4,2176]{2,1,0:T(4,128)(2,1)}), bf16[128,4,2176]{2,1,0:T(4,128)(2,1)S(1)}, u32[]{:S(2)}, u32[]{:S(2)}) async-start(bf16[128,4,2176]{2,1,0:T(4,128)(2,1)} %pack.1), calls=%async_computation | async-start | bytes 4456448 | tf_op jit(solution)/shard_map/all_to_all | solution.py:405
  18.1 31.1 %all-to-all-done.slots_ref = bf16[128,4,2176]{2,1,0:T(4,128)(2,1)S(1)} async-done(((bf16[128,4,2176]{2,1,0:T(4,128)(2,1)}), bf16[128,4,2176]{2,1,0:T(4,128)(2,1)S(1)}, u32[]{:S(2)}, u32[]{:S(2)}) %all-to-all-start) | async-done | bytes 2228256 | tf_op jit(solution)/shard_map/all_to_all | solution.py:405
  49.2 1.9 %stack_first.1 = (bf16[16,2176]{1,0:T(8,128)(2,1)S(1)}, f32[32,512]{1,0:T(8,128)S(1)}, bf16[512,2176]{1,0:T(8,128)(2,1)S(1)}) custom-call(f32[1,1]{1,0:T(1,128)} %bitcast.weight_ref, bf16[128,4,2176]{2,1,0:T(4,128)(2,1)S(1)} %all-to-all-done.slots_ref), custom_call_target="tpu_custom_call" | custom-call | flops 3000000000 | bytes 10000000 | tf_op jit(solution)/shard_map/stack_first/pallas_call | solution.py:303
  51.2 1.2 collective-permute-start.2
  52.3 1.8 %collective-permute-start.1 = (bf16[16,2176]{1,0:T(8,128)(2,1)S(1)}, bf16[16,2176]{1,0:T(8,128)(2,1)S(1)}, u32[]{:S(2)}, u32[]{:S(2)}) collective-permute-start(bf16[16,2176]{1,0:T(8,128)(2,1)S(1)} %get-tuple-element.20.p0_ref), channel_id=1, source_target_pairs={{0,2},{1,3},{2,0},{3,1},{4,6},{5,7},{6,4},{7,5},{8,10},{9,11},{10,... | collective-permute-start | bytes 208904 | tf_op jit(solution)/shard_map/ppermute | solution.py:387
  54.1 0.0 collective-permute-start
  54.1 7.0 %shift.2 = (bf16[2048,512]{1,0:T(8,128)(2,1)S(1)}, f32[8,512]{1,0:T(8,128)S(1)}) custom-call(bf16[512,2176]{1,0:T(8,128)(2,1)S(1)} %get-tuple-element.18.y_ref, f32[32,512]{1,0:T(8,128)S(1)} %get-tuple-element.19.side_ref.head_ref), custom_call_target="tpu_custom_call" | custom-call | flops 6000000000 | bytes 20000000 | tf_op jit(solution)/shard_map/shift/pallas_call | solution.py:303
  61.1 0.0 collective-permute-done.2.p3_ref
  61.2 0.0 copy-start
  61.2 0.0 copy-start.1
  61.2 5.1 %correlate.2 = (bf16[16,2048]{1,0:T(8,128)(2,1)}, f32[32,128]{1,0:T(8,128)S(1)}) custom-call(bf16[16,2176]{1,0:T(8,128)(2,1)S(1)} %get-tuple-element.20.p0_ref, bf16[16,2176]{1,0:T(8,128)(2,1)S(1)} %collective-permute-done.p1_ref, bf16[16,2176]{1,0:T(8,128)(2,1)S(1)} %collective-permute-done.1.p2_ref, bf16[16,2176]{1,0:T(8,128)(2,1)S(1)} %collective-permute-done.2.p3_ref, ...), custom_call_target="tpu_custom_call" | custom-call | flops 4000000000 | bytes 10000000 | tf_op jit(solution)/shard_map/correlate/pallas_call | solution.py:303
  66.3 0.0 collective-permute-start.3
  66.4 1.2 collective-permute-done.3.other_ref
  67.6 20.4 %all_to_all.15.sums_ref = bf16[64,32,128]{2,1,0:T(8,128)(2,1)S(1)} all-to-all(bf16[64,32,128]{2,1,0:T(8,128)(2,1)S(1)} %spread.2), channel_id=1, replica_groups=mesh['y'=4,'x'=4,'core'=2,'off'=4] {'y','x','off'}, dimensions={0} | all-to-all | bytes 1048576 | tf_op jit(solution)/shard_map/all_to_all | solution.py:383
  88.0 2.8 %stack_next.1 = (bf16[16,2176]{1,0:T(8,128)(2,1)S(1)}, f32[32,512]{1,0:T(8,128)S(1)}, f32[32,128]{1,0:T(8,128)S(1)}) custom-call(f32[1,1]{1,0:T(1,128)} %bitcast.weight_ref, s32[2]{0:T(128)S(1)} %copy-done, f32[8]{0:T(128)S(1)} %copy-done.1, bf16[512,2176]{1,0:T(8,128)(2,1)S(1)} %get-tuple-element.18.y_ref, ...), custom_call_target="tpu_custom_call" | custom-call | flops 3000000000 | bytes 10000000 | tf_op jit(solution)/shard_map/stack_next/pallas_call | solution.py:303
  90.7 0.7 collective-permute-start.6
  91.4 2.1 %collective-permute-start.5 = (bf16[16,2176]{1,0:T(8,128)(2,1)S(1)}, bf16[16,2176]{1,0:T(8,128)(2,1)S(1)}, u32[]{:S(2)}, u32[]{:S(2)}) collective-permute-start(bf16[16,2176]{1,0:T(8,128)(2,1)S(1)} %get-tuple-element.25.p0_ref), channel_id=1, source_target_pairs={{0,2},{1,3},{2,0},{3,1},{4,6},{5,7},{6,4},{7,5},{8,10},{9,11},{10,... | collective-permute-start | bytes 208904 | tf_op jit(solution)/shard_map/ppermute | solution.py:387
  93.5 0.0 collective-permute-start.4
  93.5 7.0 %shift.3 = (bf16[2048,512]{1,0:T(8,128)(2,1)S(1)}, f32[8,512]{1,0:T(8,128)S(1)}) custom-call(bf16[512,2176]{1,0:T(8,128)(2,1)S(1)} %get-tuple-element.18.y_ref, f32[32,512]{1,0:T(8,128)S(1)} %get-tuple-element.26.side_ref), custom_call_target="tpu_custom_call" | custom-call | flops 6000000000 | bytes 20000000 | tf_op jit(solution)/shard_map/shift/pallas_call | solution.py:303
  100.6 5.1 %correlate.3 = (bf16[16,2048]{1,0:T(8,128)(2,1)}, f32[16,128]{1,0:T(8,128)S(1)}) custom-call(bf16[16,2176]{1,0:T(8,128)(2,1)S(1)} %get-tuple-element.25.p0_ref, bf16[16,2176]{1,0:T(8,128)(2,1)S(1)} %collective-permute-done.4.p1_ref, bf16[16,2176]{1,0:T(8,128)(2,1)S(1)} %collective-permute-done.5.p2_ref, bf16[16,2176]{1,0:T(8,128)(2,1)S(1)} %collective-permute-done.6.p3_ref, ...), custom_call_target="tpu_custom_call" | custom-call | flops 4000000000 | bytes 10000000 | tf_op jit(solution)/shard_map/correlate/pallas_call | solution.py:303
  105.7 1.2 collective-permute-done.7.other_ref
  106.9 17.6 %all_to_all.16.sums_ref = bf16[64,16,128]{2,1,0:T(8,128)(2,1)S(1)} all-to-all(bf16[64,16,128]{2,1,0:T(8,128)(2,1)S(1)} %spread.3), channel_id=1, replica_groups=mesh['y'=4,'x'=4,'core'=2,'off'=4] {'y','x','off'}, dimensions={0} | all-to-all | bytes 524288 | tf_op jit(solution)/shard_map/all_to_all | solution.py:383
  124.5 1.2 finish.1
  (10 shorter events, 0.1 us)
Async XLA Ops:
  6.9 42.3 %all-to-all-start = ((bf16[128,4,2176]{2,1,0:T(4,128)(2,1)}), bf16[128,4,2176]{2,1,0:T(4,128)(2,1)S(1)}, u32[]{:S(2)}, u32[]{:S(2)}) async-start(bf16[128,4,2176]{2,1,0:T(4,128)(2,1)} %pack.1), calls=%async_computation | async-start | bytes 4456448 | tf_op jit(solution)/shard_map/all_to_all | solution.py:405
  51.2 10.0 %collective-permute-start.2 = (bf16[16,2176]{1,0:T(8,128)(2,1)S(1)}, bf16[16,2176]{1,0:T(8,128)(2,1)S(1)}, u32[]{:S(2)}, u32[]{:S(2)}) collective-permute-start(bf16[16,2176]{1,0:T(8,128)(2,1)S(1)} %get-tuple-element.20.p0_ref), channel_id=1, source_target_pairs={{0,3},{1,0},{2,1},{3,2},{4,7},{5,4},{6,5},{7,6},{8,11},{9,8},{10,9... | collective-permute-start | bytes 208904 | tf_op jit(solution)/shard_map/ppermute | solution.py:387
  52.3 8.8 %collective-permute-start.1 = (bf16[16,2176]{1,0:T(8,128)(2,1)S(1)}, bf16[16,2176]{1,0:T(8,128)(2,1)S(1)}, u32[]{:S(2)}, u32[]{:S(2)}) collective-permute-start(bf16[16,2176]{1,0:T(8,128)(2,1)S(1)} %get-tuple-element.20.p0_ref), channel_id=1, source_target_pairs={{0,2},{1,3},{2,0},{3,1},{4,6},{5,7},{6,4},{7,5},{8,10},{9,11},{10,... | collective-permute-start | bytes 208904 | tf_op jit(solution)/shard_map/ppermute | solution.py:387
  54.1 7.0 %collective-permute-start = (bf16[16,2176]{1,0:T(8,128)(2,1)S(1)}, bf16[16,2176]{1,0:T(8,128)(2,1)S(1)}, u32[]{:S(2)}, u32[]{:S(2)}) collective-permute-start(bf16[16,2176]{1,0:T(8,128)(2,1)S(1)} %get-tuple-element.20.p0_ref), channel_id=1, source_target_pairs={{0,1},{1,2},{2,3},{3,0},{4,5},{5,6},{6,7},{7,4},{8,9},{9,10},{10,1... | collective-permute-start | bytes 208904 | tf_op jit(solution)/shard_map/ppermute | solution.py:387
  61.2 26.8 %copy-start = (s32[2]{0:T(128)S(1)}, s32[2]{0:T(128)}, u32[]{:S(2)}) copy-start(s32[2]{0:T(128)} %index_ref.3) | copy-start | bytes 28
  61.2 26.8 %copy-start.1 = (f32[8]{0:T(128)S(1)}, f32[8]{0:T(128)}, u32[]{:S(2)}) copy-start(f32[8]{0:T(128)} %table_ref.3) | copy-start | bytes 100
  66.3 1.2 collective-permute-start.3
  90.7 9.8 %collective-permute-start.6 = (bf16[16,2176]{1,0:T(8,128)(2,1)S(1)}, bf16[16,2176]{1,0:T(8,128)(2,1)S(1)}, u32[]{:S(2)}, u32[]{:S(2)}) collective-permute-start(bf16[16,2176]{1,0:T(8,128)(2,1)S(1)} %get-tuple-element.25.p0_ref), channel_id=1, source_target_pairs={{0,3},{1,0},{2,1},{3,2},{4,7},{5,4},{6,5},{7,6},{8,11},{9,8},{10,9... | collective-permute-start | bytes 208904 | tf_op jit(solution)/shard_map/ppermute | solution.py:387
  91.4 9.1 %collective-permute-start.5 = (bf16[16,2176]{1,0:T(8,128)(2,1)S(1)}, bf16[16,2176]{1,0:T(8,128)(2,1)S(1)}, u32[]{:S(2)}, u32[]{:S(2)}) collective-permute-start(bf16[16,2176]{1,0:T(8,128)(2,1)S(1)} %get-tuple-element.25.p0_ref), channel_id=1, source_target_pairs={{0,2},{1,3},{2,0},{3,1},{4,6},{5,7},{6,4},{7,5},{8,10},{9,11},{10,... | collective-permute-start | bytes 208904 | tf_op jit(solution)/shard_map/ppermute | solution.py:387
  93.5 7.0 %collective-permute-start.4 = (bf16[16,2176]{1,0:T(8,128)(2,1)S(1)}, bf16[16,2176]{1,0:T(8,128)(2,1)S(1)}, u32[]{:S(2)}, u32[]{:S(2)}) collective-permute-start(bf16[16,2176]{1,0:T(8,128)(2,1)S(1)} %get-tuple-element.25.p0_ref), channel_id=1, source_target_pairs={{0,1},{1,2},{2,3},{3,0},{4,5},{5,6},{6,7},{7,4},{8,9},{9,10},{10,1... | collective-permute-start | bytes 208904 | tf_op jit(solution)/shard_map/ppermute | solution.py:387
  105.7 1.2 collective-permute-start.7

commit v5 on v4

--- a/solution.py
+++ b/solution.py
@@ -88,18 +88,28 @@
     rank = jnp.sum(jnp.where(same, 1.0, 0.0), axis=0, keepdims=True).astype(jnp.int32)
     slot = dest * TRACE_LIMIT + rank
     onehot = (iota((SLOTS, TR_DEV), 0) == slot).astype(F32).astype(BF16)
-    on = [((amount >> bit) & 1).astype(F32).astype(BF16) > 0 for bit in range(5)]
-    cols = cols.astype(BF16)
+    amount = amount - SHIFT_MAX
+    tail = cols.astype(BF16)
     step = 32
+    lane = iota((step, LANES), 1)
+    blocks = WIDE // LANES
     for r in range(0, TR_DEV, step):
         if r % PACK_ROWS == 0:
             x_copies[r // PACK_ROWS].wait()
-        y = jnp.concatenate([x_ref[r : r + step, :], jnp.zeros((step, LANES), BF16)], axis=1)
-        y = pltpu.roll(y, SHIFT_MAX, 1)
-        for bit in range(5):
-            y = jnp.where(on[bit][r : r + step, :], pltpu.roll(y, WIDE - (1 << bit), 1), y)
-        y_ref[r : r + step, :NS] = y[:, :NS]
-        y_ref[r : r + step, NS:] = y[:, NS:] + cols[r : r + step, :]
+        source = lane + amount[r : r + step, :]
+        index = source & (LANES - 1)
+        turned = [
+            jnp.take_along_axis(
+                x_ref[r : r + step, c * LANES : (c + 1) * LANES].astype(F32), index, axis=1, mode="promise_in_bounds"
+            )
+            for c in range(blocks - 1)
+        ] + [jnp.zeros((step, LANES), F32)]
+        for c in range(blocks):
+            before, after = turned[c - 1], turned[(c + 1) % blocks]
+            y = jnp.where(source < 0, before, jnp.where(source >= LANES, after, turned[c])).astype(BF16)
+            if c == blocks - 1:
+                y = y + tail[r : r + step, :]
+            y_ref[r : r + step, c * LANES : (c + 1) * LANES] = y
     out_copies = []
     group = DEVICES // PACK_OUT
     for i in range(PACK_OUT):
@@ -117,6 +127,22 @@
 
 def one_hot_rows(row, count):
     return (iota((count, SLOTS), 0) == row.astype(jnp.int32)).astype(F32)
+
+
+def one_hot_half(row, count):
+    return one_hot_rows(row, count).astype(BF16)
+
+
+def parts_of(value):
+    top = value.astype(BF16)
+    rest = value - top.astype(F32)
+    middle = rest.astype(BF16)
+    return jnp.concatenate([top, middle, (rest - middle.astype(F32)).astype(BF16)], axis=0)
+
+
+def joined(sums):
+    rows = sums.shape[0] // 3
+    return (sums[0:rows, :] + sums[rows : 2 * rows, :]) + sums[2 * rows :, :]
 
 
 def unit(size):
@@ -169,9 +195,9 @@
     head = head_ref[0:16, :]
     frac = head[5:6, :] * (1.0 / NPHASE)
     for base, at in ((8, 0), (0, 2)):
-        low = one_hot_rows(head[at + 1 : at + 2, :], 128)
+        low = one_hot_half(head[at + 1 : at + 2, :], 128)
         high = one_hot_rows(head[at : at + 1, :], 8)
-        found = dot(known_ref[base : base + 8, :], low, NN, lax.Precision.HIGHEST)
+        found = joined(dot(parts_of(known_ref[base : base + 8, :]), low, NN))
         frac = frac + jnp.sum(found * high, axis=0, keepdims=True)
     stack_rows(weight_ref[0, 0], y_ref, head, frac, side_ref, part_ref, sum_ref)
 
@@ -184,7 +210,7 @@
     shot_ref[...] = total[8:10, :]
 
 
-def shift_kernel(y_ref, side_ref, st_ref, energy_ref, xt_ref):
+def turn_kernel(y_ref, side_ref, st_ref, energy_ref, xt_ref):
     eye = unit(LANES)
     groups = SLOTS // LANES
     for c in range(NS // LANES):
@@ -196,6 +222,11 @@
         part = block[:, q * LANES : (q + 1) * LANES]
         xt_ref[q, 0:8, :] = part[120:128, :]
         xt_ref[q, 8 + NS : 16 + NS, :] = part[0:8, :]
+    shift_kernel(xt_ref, side_ref, st_ref, energy_ref)
+
+
+def shift_kernel(xt_ref, side_ref, st_ref, energy_ref):
+    groups = SLOTS // LANES
     chunk = 32
     energies = []
     for q in range(groups):
@@ -216,11 +247,10 @@
             for h in range(0, chunk // 8, 2):
                 rounded = jnp.concatenate(totals[h : h + 2], axis=0).astype(BF16)
                 st_ref[pl.ds(base + 8 * h, 16), q * LANES : (q + 1) * LANES] = rounded
-                wide = rounded.astype(F32)
-                energy = energy + wide[0:8, :] * wide[0:8, :] + wide[8:16, :] * wide[8:16, :]
+                energy = energy + (totals[h] * totals[h] + totals[h + 1] * totals[h + 1])
             return energy
 
-        energy = lax.fori_loop(0, NS // chunk, body, jnp.zeros((8, LANES), F32), unroll=2)
+        energy = lax.fori_loop(0, NS // chunk, body, jnp.zeros((8, LANES), F32), unroll=4)
         energies.append(jnp.sum(energy, axis=0, keepdims=True))
     energy_ref[...] = jnp.broadcast_to(jnp.concatenate(energies, axis=1), (8, SLOTS))
 
@@ -262,12 +292,12 @@
     misfit = -delay * live
     grad_ref[...] = jnp.zeros_like(grad_ref)
     for at, out, rows in ((2, 0, 8), (0, 8, 2)):
-        low = one_hot_rows(head[at + 1 : at + 2, :], 128)
+        low = one_hot_half(head[at + 1 : at + 2, :], 128)
         high = one_hot_rows(head[at : at + 1, :], 8)
         values = high * misfit
         if first:
             values = jnp.concatenate([values, high * live], axis=0)
-        sums = dot(values, low, NT, lax.Precision.HIGHEST)
+        sums = joined(dot(parts_of(values), low, NT))
         grad_ref[out : out + rows, :] = sums[0:rows, :]
         if first:
             grad_ref[16 + out : 16 + out + rows, :] = sums[8 : 8 + rows, :]
@@ -358,10 +388,16 @@
     return call(last_kernel, out, (1, 1, 0, 0), [], "finish", 10**4, 10**5, index, table, known, sums)
 
 
-def shift(rows, side):
-    out = (shape((NS, SLOTS), BF16), shape((8, SLOTS), F32))
-    scratch = [pltpu.VMEM((SLOTS // LANES, NS + 16, LANES), F32)]
-    return call(shift_kernel, out, (0, 0), scratch, "shift", 6 * 10**9, 2 * 10**7, rows, side)
+SHIFTED = (shape((NS, SLOTS), BF16), shape((8, SLOTS), F32))
+TURNED = shape((SLOTS // LANES, NS + 16, LANES), F32)
+
+
+def shift_first(rows, side):
+    return call(turn_kernel, (*SHIFTED, TURNED), (0, 0), [], "shift_first", 6 * 10**9, 2 * 10**7, rows, side)
+
+
+def shift_next(turned, side):
+    return call(shift_kernel, SHIFTED, (0, 0), [], "shift_next", 6 * 10**9, 2 * 10**7, turned, side)
 
 
 def correlate(first, parts, shifted, energy, side):
@@ -383,11 +419,8 @@
     return lax.all_to_all(copies, ("y", "x", "off"), split_axis=0, concat_axis=0, tiled=True)
 
 
-def from_stack(first, part, rows, side):
-    others = [lax.ppermute(part, "off", off_perm(d)) for d in (1, 2, 3)]
-    shifted, energy = shift(rows, side)
-    pilot, sums = correlate(first, (part, *others), shifted, energy, side)
-    return pilot, sum_copies(sums)
+def exchange(part):
+    return part, *[lax.ppermute(part, "off", off_perm(d)) for d in (1, 2, 3)]
 
 
 def on_device(
@@ -405,9 +438,15 @@
     slots = lax.all_to_all(outgoing, AXES, split_axis=0, concat_axis=0, tiled=True)
     weight = (1.0 / (1.0 + lax.axis_index("off").astype(F32))).reshape(1, 1)
     part, side, rows = stack_first(weight, slots)
-    pilot, sums = from_stack(True, part, rows, side)
+    parts = exchange(part)
+    shifted, energy, turned = shift_first(rows, side)
+    pilot, sums = correlate(True, parts, shifted, energy, side)
+    sums = sum_copies(sums)
     part, side, known = stack_next(weight, damping_index, damping_table, rows, side, sums)
-    pilot, sums = from_stack(False, part, rows, side)
+    parts = exchange(part)
+    shifted, energy = shift_next(turned, side)
+    pilot, sums = correlate(False, parts, shifted, energy, side)
+    sums = sum_copies(sums)
     rec, shot = finish(damping_index, damping_table, known, sums)
     return (shot.reshape(-1), rec.reshape(-1), pilot)
 

time: 126 us -> 121 us (0.960)
  Pallas kernels: 36.5 us -> 31.6 us
    pallas_call x9, Pallas kernels: 30.3 us -> 27.2 us  [call(): pl.pallas_call(kernel, out_shape=out, in_specs=[SMEM if space else VMEM f...]
    pallas_call x1, Pallas kernels: 6.24 us -> 4.43 us  [pack(): pl.pallas_call(pack_kernel, out_shape=shape((DEVICES, TRACE_LIMIT, WIDE),...]
  transfers between devices with their start and end apart: 9 -> 9, of which waited for: 3 -> 4; matrix products, arithmetic and copies ran while one was open for 0% -> 0% of each run, Pallas kernels for 11% -> 9%
where the time goes in v5:
time: 121 us
  blocking collectives  37.7 us (31%)
  waiting for transfers between devices  33.8 us (28%)
  Pallas kernels  31.6 us (26%)
  starting transfers between devices  16.9 us (14%)
    all_to_all x2, blocking collectives, sum_copies(): lax.all_to_all(copies, ('y', 'x', 'off'), split_axis=0, concat_axis=0, ti...  37.7 us
    all_to_all x1, waiting for transfers between devices, on_device(): lax.all_to_all(outgoing, AXES, split_axis=0, concat_axis=0, tiled=True)  31.1 us
    pallas_call x9, Pallas kernels, call(): pl.pallas_call(kernel, out_shape=out, in_specs=[SMEM if space else VMEM f...  27.2 us
    all_to_all x1, starting transfers between devices, on_device(): lax.all_to_all(outgoing, AXES, split_axis=0, concat_axis=0, tiled=True)  11.2 us
    ppermute x6, starting transfers between devices, exchange(): return (part, *[lax.ppermute(part, 'off', off_perm(d)) for d in (1, 2, 3)])  5.77 us
    pallas_call x1, Pallas kernels, pack(): pl.pallas_call(pack_kernel, out_shape=shape((DEVICES, TRACE_LIMIT, WIDE),...  4.43 us
  transfers between devices with their start and end apart: 9, of which 4 were waited for; matrix products, arithmetic and copies ran while one was open for 0% of the time, Pallas kernels for 9%

profile of v5, /device:TPU:0, one launch (start us, length us, event | category | flops | bytes accessed | tf_op | source)
XLA Modules:
  0.0 120.8 jit_solution(5744584978470665986)
XLA Ops:
  0.6 4.4 %pack.1 = bf16[128,4,2176]{2,1,0:T(4,128)(2,1)} custom-call(s32[1,256]{1,0:T(1,128)} %bitcast.9, s32[1,256]{1,0:T(1,128)} %bitcast.10, s32[1,256]{1,0:T(1,128)} %bitcast.11, s32[1,256]{1,0:T(1,128)} %bitcast.12, s32[1,256]{1,0:T(1,128)} %bitcast.13, s32[1,256]{1,0:T(1,128)} %bitcast.14, bf16[256,2048]{1,0:T(8,128)(2,1)} %refs_6_.1), custom_call_target="tpu_custom_call" | custom-call | tf_op jit(solution)/shard_map/pack/pallas_call | solution.py:354
  5.1 11.2 %all-to-all-start = ((bf16[128,4,2176]{2,1,0:T(4,128)(2,1)}), bf16[128,4,2176]{2,1,0:T(4,128)(2,1)S(1)}, u32[]{:S(2)}, u32[]{:S(2)}) async-start(bf16[128,4,2176]{2,1,0:T(4,128)(2,1)} %pack.1), calls=%async_computation | async-start | bytes 4456448 | tf_op jit(solution)/shard_map/all_to_all | solution.py:438
  16.3 31.1 %all-to-all-done.slots_ref = bf16[128,4,2176]{2,1,0:T(4,128)(2,1)S(1)} async-done(((bf16[128,4,2176]{2,1,0:T(4,128)(2,1)}), bf16[128,4,2176]{2,1,0:T(4,128)(2,1)S(1)}, u32[]{:S(2)}, u32[]{:S(2)}) %all-to-all-start) | async-done | bytes 2228256 | tf_op jit(solution)/shard_map/all_to_all | solution.py:438
  47.4 2.0 %stack_first.1 = (bf16[16,2176]{1,0:T(8,128)(2,1)S(1)}, f32[32,512]{1,0:T(8,128)S(1)}, bf16[512,2176]{1,0:T(8,128)(2,1)S(1)}) custom-call(f32[1,1]{1,0:T(1,128)} %bitcast.weight_ref, bf16[128,4,2176]{2,1,0:T(4,128)(2,1)S(1)} %all-to-all-done.slots_ref), custom_call_target="tpu_custom_call" | custom-call | flops 3000000000 | bytes 10000000 | tf_op jit(solution)/shard_map/stack_first/pallas_call | solution.py:333
  49.4 1.2 collective-permute-start.2
  50.6 1.8 %collective-permute-start.1 = (bf16[16,2176]{1,0:T(8,128)(2,1)S(1)}, bf16[16,2176]{1,0:T(8,128)(2,1)S(1)}, u32[]{:S(2)}, u32[]{:S(2)}) collective-permute-start(bf16[16,2176]{1,0:T(8,128)(2,1)S(1)} %get-tuple-element.21.p0_ref), channel_id=1, source_target_pairs={{0,2},{1,3},{2,0},{3,1},{4,6},{5,7},{6,4},{7,5},{8,10},{9,11},{10,... | collective-permute-start | bytes 208904 | tf_op jit(solution)/shard_map/ppermute | solution.py:423
  52.4 6.0 %shift_first.1 = (bf16[2048,512]{1,0:T(8,128)(2,1)S(1)}, f32[8,512]{1,0:T(8,128)S(1)}, f32[4,2064,128]{2,1,0:T(8,128)S(1)}) custom-call(bf16[512,2176]{1,0:T(8,128)(2,1)S(1)} %get-tuple-element.19.y_ref, f32[32,512]{1,0:T(8,128)S(1)} %get-tuple-element.20.side_ref.head_ref), custom_call_target="tpu_custom_call" | custom-call | flops 6000000000 | bytes 20000000 | tf_op jit(solution)/shard_map/shift_first/pallas_call | solution.py:333
  58.4 0.0 collective-permute-done.2.p3_ref
  58.5 0.0 collective-permute-done.p1_ref
  58.5 0.0 copy-start
  58.5 0.0 copy-start.1
  58.5 5.0 %correlate.2 = (bf16[16,2048]{1,0:T(8,128)(2,1)}, f32[32,128]{1,0:T(8,128)S(1)}) custom-call(bf16[16,2176]{1,0:T(8,128)(2,1)S(1)} %get-tuple-element.21.p0_ref, bf16[16,2176]{1,0:T(8,128)(2,1)S(1)} %collective-permute-done.p1_ref, bf16[16,2176]{1,0:T(8,128)(2,1)S(1)} %collective-permute-done.1.p2_ref, bf16[16,2176]{1,0:T(8,128)(2,1)S(1)} %collective-permute-done.2.p3_ref, ...), custom_call_target="tpu_custom_call" | custom-call | flops 4000000000 | bytes 10000000 | tf_op jit(solution)/shard_map/correlate/pallas_call | solution.py:333
  63.5 1.2 collective-permute-done.3.other_ref
  64.7 20.4 %all_to_all.15.sums_ref = bf16[64,32,128]{2,1,0:T(8,128)(2,1)S(1)} all-to-all(bf16[64,32,128]{2,1,0:T(8,128)(2,1)S(1)} %spread.2), channel_id=1, replica_groups=mesh['y'=4,'x'=4,'core'=2,'off'=4] {'y','x','off'}, dimensions={0} | all-to-all | bytes 1048576 | tf_op jit(solution)/shard_map/all_to_all | solution.py:419
  85.1 2.5 %stack_next.1 = (bf16[16,2176]{1,0:T(8,128)(2,1)S(1)}, f32[32,512]{1,0:T(8,128)S(1)}, f32[32,128]{1,0:T(8,128)S(1)}) custom-call(f32[1,1]{1,0:T(1,128)} %bitcast.weight_ref, s32[2]{0:T(128)S(1)} %copy-done, f32[8]{0:T(128)S(1)} %copy-done.1, bf16[512,2176]{1,0:T(8,128)(2,1)S(1)} %get-tuple-element.19.y_ref, ...), custom_call_target="tpu_custom_call" | custom-call | flops 3000000000 | bytes 10000000 | tf_op jit(solution)/shard_map/stack_next/pallas_call | solution.py:333
  87.6 0.7 collective-permute-start.6
  88.3 2.1 %collective-permute-start.5 = (bf16[16,2176]{1,0:T(8,128)(2,1)S(1)}, bf16[16,2176]{1,0:T(8,128)(2,1)S(1)}, u32[]{:S(2)}, u32[]{:S(2)}) collective-permute-start(bf16[16,2176]{1,0:T(8,128)(2,1)S(1)} %get-tuple-element.26.p0_ref), channel_id=1, source_target_pairs={{0,2},{1,3},{2,0},{3,1},{4,6},{5,7},{6,4},{7,5},{8,10},{9,11},{10,... | collective-permute-start | bytes 208904 | tf_op jit(solution)/shard_map/ppermute | solution.py:423
  90.4 0.0 collective-permute-start.4
  90.4 5.2 %shift_next.1 = (bf16[2048,512]{1,0:T(8,128)(2,1)S(1)}, f32[8,512]{1,0:T(8,128)S(1)}) custom-call(f32[4,2064,128]{2,1,0:T(8,128)S(1)} %get-tuple-element.27.xt_ref, f32[32,512]{1,0:T(8,128)S(1)} %get-tuple-element.28.side_ref), custom_call_target="tpu_custom_call" | custom-call | flops 6000000000 | bytes 20000000 | tf_op jit(solution)/shard_map/shift_next/pallas_call | solution.py:333
  95.7 0.3 collective-permute-done.4.p1_ref
  95.9 5.1 %correlate.3 = (bf16[16,2048]{1,0:T(8,128)(2,1)}, f32[16,128]{1,0:T(8,128)S(1)}) custom-call(bf16[16,2176]{1,0:T(8,128)(2,1)S(1)} %get-tuple-element.26.p0_ref, bf16[16,2176]{1,0:T(8,128)(2,1)S(1)} %collective-permute-done.4.p1_ref, bf16[16,2176]{1,0:T(8,128)(2,1)S(1)} %collective-permute-done.5.p2_ref, bf16[16,2176]{1,0:T(8,128)(2,1)S(1)} %collective-permute-done.6.p3_ref, ...), custom_call_target="tpu_custom_call" | custom-call | flops 4000000000 | bytes 10000000 | tf_op jit(solution)/shard_map/correlate/pallas_call | solution.py:333
  101.0 1.2 collective-permute-done.7.other_ref
  102.2 17.4 %all_to_all.16.sums_ref = bf16[64,16,128]{2,1,0:T(8,128)(2,1)S(1)} all-to-all(bf16[64,16,128]{2,1,0:T(8,128)(2,1)S(1)} %spread.3), channel_id=1, replica_groups=mesh['y'=4,'x'=4,'core'=2,'off'=4] {'y','x','off'}, dimensions={0} | all-to-all | bytes 524288 | tf_op jit(solution)/shard_map/all_to_all | solution.py:419
  119.6 1.2 finish.1
  (10 shorter events, 0.1 us)
Async XLA Ops:
  5.1 42.4 %all-to-all-start = ((bf16[128,4,2176]{2,1,0:T(4,128)(2,1)}), bf16[128,4,2176]{2,1,0:T(4,128)(2,1)S(1)}, u32[]{:S(2)}, u32[]{:S(2)}) async-start(bf16[128,4,2176]{2,1,0:T(4,128)(2,1)} %pack.1), calls=%async_computation | async-start | bytes 4456448 | tf_op jit(solution)/shard_map/all_to_all | solution.py:438
  49.4 9.0 %collective-permute-start.2 = (bf16[16,2176]{1,0:T(8,128)(2,1)S(1)}, bf16[16,2176]{1,0:T(8,128)(2,1)S(1)}, u32[]{:S(2)}, u32[]{:S(2)}) collective-permute-start(bf16[16,2176]{1,0:T(8,128)(2,1)S(1)} %get-tuple-element.21.p0_ref), channel_id=1, source_target_pairs={{0,3},{1,0},{2,1},{3,2},{4,7},{5,4},{6,5},{7,6},{8,11},{9,8},{10,9... | collective-permute-start | bytes 208904 | tf_op jit(solution)/shard_map/ppermute | solution.py:423
  50.6 7.8 %collective-permute-start.1 = (bf16[16,2176]{1,0:T(8,128)(2,1)S(1)}, bf16[16,2176]{1,0:T(8,128)(2,1)S(1)}, u32[]{:S(2)}, u32[]{:S(2)}) collective-permute-start(bf16[16,2176]{1,0:T(8,128)(2,1)S(1)} %get-tuple-element.21.p0_ref), channel_id=1, source_target_pairs={{0,2},{1,3},{2,0},{3,1},{4,6},{5,7},{6,4},{7,5},{8,10},{9,11},{10,... | collective-permute-start | bytes 208904 | tf_op jit(solution)/shard_map/ppermute | solution.py:423
  52.4 6.0 %collective-permute-start = (bf16[16,2176]{1,0:T(8,128)(2,1)S(1)}, bf16[16,2176]{1,0:T(8,128)(2,1)S(1)}, u32[]{:S(2)}, u32[]{:S(2)}) collective-permute-start(bf16[16,2176]{1,0:T(8,128)(2,1)S(1)} %get-tuple-element.21.p0_ref), channel_id=1, source_target_pairs={{0,1},{1,2},{2,3},{3,0},{4,5},{5,6},{6,7},{7,4},{8,9},{9,10},{10,1... | collective-permute-start | bytes 208904 | tf_op jit(solution)/shard_map/ppermute | solution.py:423
  58.5 26.6 %copy-start = (s32[2]{0:T(128)S(1)}, s32[2]{0:T(128)}, u32[]{:S(2)}) copy-start(s32[2]{0:T(128)} %index_ref.3) | copy-start | bytes 28
  58.5 26.6 %copy-start.1 = (f32[8]{0:T(128)S(1)}, f32[8]{0:T(128)}, u32[]{:S(2)}) copy-start(f32[8]{0:T(128)} %table_ref.3) | copy-start | bytes 100
  63.5 1.2 collective-permute-start.3
  87.6 8.0 %collective-permute-start.6 = (bf16[16,2176]{1,0:T(8,128)(2,1)S(1)}, bf16[16,2176]{1,0:T(8,128)(2,1)S(1)}, u32[]{:S(2)}, u32[]{:S(2)}) collective-permute-start(bf16[16,2176]{1,0:T(8,128)(2,1)S(1)} %get-tuple-element.26.p0_ref), channel_id=1, source_target_pairs={{0,3},{1,0},{2,1},{3,2},{4,7},{5,4},{6,5},{7,6},{8,11},{9,8},{10,9... | collective-permute-start | bytes 208904 | tf_op jit(solution)/shard_map/ppermute | solution.py:423
  88.3 7.4 %collective-permute-start.5 = (bf16[16,2176]{1,0:T(8,128)(2,1)S(1)}, bf16[16,2176]{1,0:T(8,128)(2,1)S(1)}, u32[]{:S(2)}, u32[]{:S(2)}) collective-permute-start(bf16[16,2176]{1,0:T(8,128)(2,1)S(1)} %get-tuple-element.26.p0_ref), channel_id=1, source_target_pairs={{0,2},{1,3},{2,0},{3,1},{4,6},{5,7},{6,4},{7,5},{8,10},{9,11},{10,... | collective-permute-start | bytes 208904 | tf_op jit(solution)/shard_map/ppermute | solution.py:423
  90.4 5.5 %collective-permute-start.4 = (bf16[16,2176]{1,0:T(8,128)(2,1)S(1)}, bf16[16,2176]{1,0:T(8,128)(2,1)S(1)}, u32[]{:S(2)}, u32[]{:S(2)}) collective-permute-start(bf16[16,2176]{1,0:T(8,128)(2,1)S(1)} %get-tuple-element.26.p0_ref), channel_id=1, source_target_pairs={{0,1},{1,2},{2,3},{3,0},{4,5},{5,6},{6,7},{7,4},{8,9},{9,10},{10,1... | collective-permute-start | bytes 208904 | tf_op jit(solution)/shard_map/ppermute | solution.py:423
  101.0 1.2 collective-permute-start.7

commit v6 on v5

--- a/solution.py
+++ b/solution.py
@@ -149,7 +149,7 @@
     return (iota((size, size), 0) == iota((size, size), 1)).astype(F32).astype(BF16)
 
 
-def stack_rows(weight, y_ref, head, frac, side_ref, part_ref, sum_ref):
+def stack_rows(y_ref, head, frac, side_ref, part_ref, sum_ref):
     live = head[6:7, :]
     u = (iota((TAPS, SLOTS), 0) - (TAPS // 2 - 1)).astype(F32) - frac
     angle = jnp.pi * u
@@ -158,7 +158,9 @@
     taps = sinc * (0.5 + 0.5 * jnp.cos(angle * (1.0 / (TAPS // 2))))
     side_ref[0:16, :] = head
     side_ref[16:32, :] = taps
-    member = one_hot_rows(head[4:5, :], BIN_DEV) * live
+    owner = head[8:9, :]
+    offset = owner - CLASSES * jnp.floor(owner * (1.0 / CLASSES))
+    member = one_hot_rows(head[4:5, :], BIN_DEV) * (live / (1.0 + offset))
     rows = [member * taps[k : k + 1, :] for k in range(TAPS)]
     high = [row.astype(BF16) for row in rows]
     low = [(row - top.astype(F32)).astype(BF16) for row, top in zip(rows, high)]
@@ -167,8 +169,8 @@
     total = jnp.zeros((BIN_DEV, WIDE), F32)
     for k in range(TAPS):
         total = total + pltpu.roll(sum_ref[k * BIN_DEV : (k + 1) * BIN_DEV, :], (TAPS // 2 - 1 - k) % WIDE, 1)
-    part_ref[:, :NS] = (weight * total[:, :NS]).astype(BF16)
-    mass = weight * jnp.sum(member, axis=1, keepdims=True)
+    part_ref[:, :NS] = total[:, :NS].astype(BF16)
+    mass = jnp.sum(member, axis=1, keepdims=True)
     m0 = mass.astype(BF16).astype(F32)
     m1 = (mass - m0).astype(BF16).astype(F32)
     m2 = mass - m0 - m1
@@ -177,18 +179,16 @@
     part_ref[:, NS:] = tail.astype(BF16)
 
 
-def first_kernel(weight_ref, slots_ref, part_ref, side_ref, y_ref, sum_ref):
+def first_kernel(slots_ref, part_ref, side_ref, y_ref, sum_ref):
     y_ref[...] = slots_ref[...].reshape(SLOTS, WIDE)
     head = dot(unit(LANES), y_ref[:, NS:], NT)[HEAD : HEAD + 16, :]
-    stack_rows(weight_ref[0, 0], y_ref, head, head[5:6, :] * (1.0 / NPHASE), side_ref, part_ref, sum_ref)
-
-
-def next_kernel(
-    weight_ref, index_ref, table_ref, y_ref, head_ref, sums_ref, part_ref, side_ref, known_ref, sum_ref
-):
-    damp = table_ref[index_ref[0]]
+    stack_rows(y_ref, head, head[5:6, :] * (1.0 / NPHASE), side_ref, part_ref, sum_ref)
+
+
+def next_kernel(damp_ref, y_ref, head_ref, sums_ref, part_ref, side_ref, known_ref, sum_ref):
+    damp = damp_ref[0:1, :]
     sums = gathered(sums_ref)
-    count = 256.0 * sums[10:20, :] + sums[20:30, :]
+    count = sums[10:20, :]
     known_ref[...] = jnp.zeros_like(known_ref)
     known_ref[0:10, :] = sums[0:10, :] / ((1.0 + damp) * count + damp)
     known_ref[16:26, :] = count
@@ -199,11 +199,11 @@
         high = one_hot_rows(head[at : at + 1, :], 8)
         found = joined(dot(parts_of(known_ref[base : base + 8, :]), low, NN))
         frac = frac + jnp.sum(found * high, axis=0, keepdims=True)
-    stack_rows(weight_ref[0, 0], y_ref, head, frac, side_ref, part_ref, sum_ref)
-
-
-def last_kernel(index_ref, table_ref, known_ref, sums_ref, rec_ref, shot_ref):
-    damp = table_ref[index_ref[1]]
+    stack_rows(y_ref, head, frac, side_ref, part_ref, sum_ref)
+
+
+def last_kernel(damp_ref, known_ref, sums_ref, rec_ref, shot_ref):
+    damp = damp_ref[8:9, :]
     step = gathered(sums_ref) / ((1.0 + damp) * known_ref[16:32, :] + damp)
     total = known_ref[0:16, :] + step
     rec_ref[...] = total[0:8, :]
@@ -308,10 +308,7 @@
     rows_ref[...] = jnp.zeros_like(rows_ref)
     rows_ref[0:10, :] = total[0:10, :]
     if total.shape[0] > 16:
-        count = total[16:26, :]
-        large = jnp.floor(count * (1.0 / 256.0))
-        rows_ref[10:20, :] = large
-        rows_ref[20:30, :] = count - 256.0 * large
+        rows_ref[10:20, :] = total[16:26, :]
     out_ref[...] = jnp.broadcast_to(rows_ref[...].astype(BF16)[None], out_ref.shape)
 
 
@@ -367,25 +364,22 @@
 ROWS = pltpu.VMEM((TAPS * BIN_DEV, WIDE), F32)
 
 
-def stack_first(weight, slots):
+def stack_first(slots):
     out = (PART, SIDE, shape((SLOTS, WIDE), BF16))
-    return call(first_kernel, out, (1, 0), [ROWS], "stack_first", 3 * 10**9, 10**7, weight, slots)
+    return call(first_kernel, out, (0,), [ROWS], "stack_first", 3 * 10**9, 10**7, slots)
 
 
 KNOWN = shape((32, LANES), F32)
 
 
-def stack_next(weight, index, table, rows, side, sums):
-    memory = (1, 1, 1, 0, 0, 0)
+def stack_next(damps, rows, side, sums):
     out = (PART, SIDE, KNOWN)
-    return call(
-        next_kernel, out, memory, [ROWS], "stack_next", 3 * 10**9, 10**7, weight, index, table, rows, side, sums
-    )
-
-
-def finish(index, table, known, sums):
+    return call(next_kernel, out, (0,) * 4, [ROWS], "stack_next", 3 * 10**9, 10**7, damps, rows, side, sums)
+
+
+def finish(damps, known, sums):
     out = (shape((8, LANES), F32), shape((2, LANES), F32))
-    return call(last_kernel, out, (1, 1, 0, 0), [], "finish", 10**4, 10**5, index, table, known, sums)
+    return call(last_kernel, out, (0,) * 3, [], "finish", 10**4, 10**5, damps, known, sums)
 
 
 SHIFTED = (shape((NS, SLOTS), BF16), shape((8, SLOTS), F32))
@@ -413,8 +407,9 @@
 
 def sum_copies(value):
     other = lax.ppermute(value, "core", [(0, 1), (1, 0)])
-    out = shape((DEVICES // 2, value.shape[0], LANES), BF16)
-    scratch = [pltpu.VMEM(value.shape, F32)]
+    rows = 16 if value.shape[0] == 16 else 24
+    out = shape((DEVICES // 2, rows, LANES), BF16)
+    scratch = [pltpu.VMEM((rows, LANES), F32)]
     copies = call(spread_kernel, out, (0, 0), scratch, "spread", 10**5, 10**6, value, other)
     return lax.all_to_all(copies, ("y", "x", "off"), split_axis=0, concat_axis=0, tiled=True)
 
@@ -436,18 +431,20 @@
 ):
     outgoing = pack(traces, shot_id, receiver_id, cmp_bin, offset_class, shift_int, frac_index)
     slots = lax.all_to_all(outgoing, AXES, split_axis=0, concat_axis=0, tiled=True)
-    weight = (1.0 / (1.0 + lax.axis_index("off").astype(F32))).reshape(1, 1)
-    part, side, rows = stack_first(weight, slots)
+    entries = jnp.arange(damping_table.shape[0], dtype=jnp.int32)
+    chosen = jnp.sum(jnp.where(entries == damping_index[:, None], damping_table, 0.0), axis=1)
+    damps = jnp.broadcast_to(chosen[:, None, None], (2, 8, LANES)).reshape(16, LANES)
+    part, side, rows = stack_first(slots)
     parts = exchange(part)
     shifted, energy, turned = shift_first(rows, side)
     pilot, sums = correlate(True, parts, shifted, energy, side)
     sums = sum_copies(sums)
-    part, side, known = stack_next(weight, damping_index, damping_table, rows, side, sums)
+    part, side, known = stack_next(damps, rows, side, sums)
     parts = exchange(part)
     shifted, energy = shift_next(turned, side)
     pilot, sums = correlate(False, parts, shifted, energy, side)
     sums = sum_copies(sums)
-    rec, shot = finish(damping_index, damping_table, known, sums)
+    rec, shot = finish(damps, known, sums)
     return (shot.reshape(-1), rec.reshape(-1), pilot)
 
 

time: 121 us -> 122 us (level)
  blocking collectives: 37.7 us -> 59.2 us
  waiting for transfers between devices: 33.8 us -> 14.2 us
  starting transfers between devices: 16.9 us -> 13.4 us
  local copies, waits for them, and re-layouts: 0.01 us -> 2.44 us
    all_to_all x0 -> x1, blocking collectives: none -> 42.4 us  [on_device(): lax.all_to_all(outgoing, AXES, split_axis=0, concat_axis=0, tiled=True)]
    all_to_all x2 -> x1, blocking collectives: 37.7 us -> 16.9 us  [sum_copies(): lax.all_to_all(copies, ('y', 'x', 'off'), split_axis=0, concat_axis=0, ti...]
    all_to_all x1, waiting for transfers between devices: 31.1 us -> 11.9 us  [sum_copies(): lax.all_to_all(copies, ('y', 'x', 'off'), split_axis=0, concat_axis=0, ti...]
    all_to_all x1, starting transfers between devices: 11.2 us -> 6.17 us  [sum_copies(): lax.all_to_all(copies, ('y', 'x', 'off'), split_axis=0, concat_axis=0, ti...]
    unnamed x4 -> x8, local copies, waits for them, and re-layouts: 0.01 us -> 2.21 us
    ppermute x6, starting transfers between devices: 5.77 us -> 7.27 us  [exchange(): return (part, *[lax.ppermute(part, 'off', off_perm(d)) for d in (1, 2, 3)])]
  transfers between devices with their start and end apart: 9 -> 9, of which waited for: 4 -> 3; matrix products, arithmetic and copies ran while one was open for 0% -> 0% of each run, Pallas kernels for 9% -> 9%
where the time goes in v6:
time: 122 us; the launch traced here: 121 us
  blocking collectives  59.2 us (49%)
  Pallas kernels  31.1 us (25%)
  waiting for transfers between devices  14.2 us (12%)
  starting transfers between devices  13.4 us (11%)
  local copies, waits for them, and re-layouts  2.44 us (2%)
    all_to_all x1, blocking collectives, on_device(): lax.all_to_all(outgoing, AXES, split_axis=0, concat_axis=0, tiled=True)  42.4 us
    pallas_call x9, Pallas kernels, call(): pl.pallas_call(kernel, out_shape=out, in_specs=[SMEM if space else VMEM f...  26.6 us
    all_to_all x1, blocking collectives, sum_copies(): lax.all_to_all(copies, ('y', 'x', 'off'), split_axis=0, concat_axis=0, ti...  16.9 us
    all_to_all x1, waiting for transfers between devices, sum_copies(): lax.all_to_all(copies, ('y', 'x', 'off'), split_axis=0, concat_axis=0, ti...  11.9 us
    ppermute x6, starting transfers between devices, exchange(): return (part, *[lax.ppermute(part, 'off', off_perm(d)) for d in (1, 2, 3)])  7.27 us
    all_to_all x1, starting transfers between devices, sum_copies(): lax.all_to_all(copies, ('y', 'x', 'off'), split_axis=0, concat_axis=0, ti...  6.17 us
    pallas_call x1, Pallas kernels, pack(): pl.pallas_call(pack_kernel, out_shape=shape((DEVICES, TRACE_LIMIT, WIDE),...  4.43 us
  transfers between devices with their start and end apart: 9, of which 3 were waited for; matrix products, arithmetic and copies ran while one was open for 0% of the time, Pallas kernels for 9%

profile of v6, /device:TPU:0, one launch (start us, length us, event | category | flops | bytes accessed | tf_op | source)
XLA Modules:
  0.0 121.3 jit_solution(11484306952568855413)
XLA Ops:
  0.6 4.4 %pack.1 = bf16[128,4,2176]{2,1,0:T(4,128)(2,1)} custom-call(s32[1,256]{1,0:T(1,128)} %bitcast.8, s32[1,256]{1,0:T(1,128)} %bitcast.9, s32[1,256]{1,0:T(1,128)} %bitcast.10, s32[1,256]{1,0:T(1,128)} %bitcast.11, s32[1,256]{1,0:T(1,128)} %bitcast.12, s32[1,256]{1,0:T(1,128)} %bitcast.13, bf16[256,2048]{1,0:T(8,128)(2,1)} %refs_6_.1), custom_call_target="tpu_custom_call" | custom-call | tf_op jit(solution)/shard_map/pack/pallas_call | solution.py:351
  5.1 42.4 %all_to_all.15.slots_ref = bf16[128,4,2176]{2,1,0:T(4,128)(2,1)S(1)} all-to-all(bf16[128,4,2176]{2,1,0:T(4,128)(2,1)} %pack.1), channel_id=1, replica_groups=mesh['y'=4,'x'=4,'core'=2,'off'=4] {'y','x','core','off'}, dimensions={0} | all-to-all | bytes 4456448 | tf_op jit(solution)/shard_map/all_to_all | solution.py:433
  47.4 2.0 %stack_first.1 = (bf16[16,2176]{1,0:T(8,128)(2,1)S(1)}, f32[32,512]{1,0:T(8,128)S(1)}, bf16[512,2176]{1,0:T(8,128)(2,1)S(1)}) custom-call(bf16[128,4,2176]{2,1,0:T(4,128)(2,1)S(1)} %all_to_all.15.slots_ref), custom_call_target="tpu_custom_call" | custom-call | flops 3000000000 | bytes 10000000 | tf_op jit(solution)/shard_map/stack_first/pallas_call | solution.py:330
  49.4 0.9 collective-permute-start
  50.3 1.7 %collective-permute-start.1 = (bf16[16,2176]{1,0:T(8,128)(2,1)S(1)}, bf16[16,2176]{1,0:T(8,128)(2,1)S(1)}, u32[]{:S(2)}, u32[]{:S(2)}) collective-permute-start(bf16[16,2176]{1,0:T(8,128)(2,1)S(1)} %get-tuple-element.21.p0_ref), channel_id=1, source_target_pairs={{0,2},{1,3},{2,0},{3,1},{4,6},{5,7},{6,4},{7,5},{8,10},{9,11},{10,... | collective-permute-start | bytes 208904 | tf_op jit(solution)/shard_map/ppermute | solution.py:418
  52.0 1.0 collective-permute-start.2
  53.1 6.0 %shift_first.1 = (bf16[2048,512]{1,0:T(8,128)(2,1)S(1)}, f32[8,512]{1,0:T(8,128)S(1)}, f32[4,2064,128]{2,1,0:T(8,128)S(1)}) custom-call(bf16[512,2176]{1,0:T(8,128)(2,1)S(1)} %get-tuple-element.19.y_ref, f32[32,512]{1,0:T(8,128)S(1)} %get-tuple-element.20.side_ref.head_ref), custom_call_target="tpu_custom_call" | custom-call | flops 6000000000 | bytes 20000000 | tf_op jit(solution)/shard_map/shift_first/pallas_call | solution.py:330
  59.2 5.0 %correlate.2 = (bf16[16,2048]{1,0:T(8,128)(2,1)}, f32[32,128]{1,0:T(8,128)S(1)}) custom-call(bf16[16,2176]{1,0:T(8,128)(2,1)S(1)} %get-tuple-element.21.p0_ref, bf16[16,2176]{1,0:T(8,128)(2,1)S(1)} %collective-permute-done.p1_ref, bf16[16,2176]{1,0:T(8,128)(2,1)S(1)} %collective-permute-done.1.p2_ref, bf16[16,2176]{1,0:T(8,128)(2,1)S(1)} %collective-permute-done.2.p3_ref, ...), custom_call_target="tpu_custom_call" | custom-call | flops 4000000000 | bytes 10000000 | tf_op jit(solution)/shard_map/correlate/pallas_call | solution.py:330
  64.2 1.2 collective-permute-done.3.other_ref
  65.3 0.8 spread.2
  66.1 6.2 %all-to-all-start.1 = ((bf16[64,24,128]{2,1,0:T(8,128)(2,1)}), bf16[64,24,128]{2,1,0:T(8,128)(2,1)S(1)}, u32[]{:S(2)}, u32[]{:S(2)}) async-start(bf16[64,24,128]{2,1,0:T(8,128)(2,1)} %spread.2), calls=%async_computation.1 | async-start | bytes 786432 | tf_op jit(solution)/shard_map/all_to_all | solution.py:414
  72.3 0.2 fusion
  72.6 0.1 broadcast_in_dim.23
  72.7 11.9 %all-to-all-done.1.sums_ref = bf16[64,24,128]{2,1,0:T(8,128)(2,1)S(1)} async-done(((bf16[64,24,128]{2,1,0:T(8,128)(2,1)}), bf16[64,24,128]{2,1,0:T(8,128)(2,1)S(1)}, u32[]{:S(2)}, u32[]{:S(2)}) %all-to-all-start.1) | async-done | bytes 393248 | tf_op jit(solution)/shard_map/all_to_all | solution.py:414
  84.6 2.0 %stack_next.1 = (bf16[16,2176]{1,0:T(8,128)(2,1)S(1)}, f32[32,512]{1,0:T(8,128)S(1)}, f32[32,128]{1,0:T(8,128)S(1)}) custom-call(f32[16,128]{1,0:T(8,128)S(1)} %broadcast_in_dim.24.damp_ref, bf16[512,2176]{1,0:T(8,128)(2,1)S(1)} %get-tuple-element.19.y_ref, f32[32,512]{1,0:T(8,128)S(1)} %get-tuple-element.20.side_ref.head_ref, ...), custom_call_target="tpu_custom_call" | custom-call | flops 3000000000 | bytes 10000000 | tf_op jit(solution)/shard_map/stack_next/pallas_call | solution.py:330
  86.6 0.7 collective-permute-start.4
  87.3 1.5 %collective-permute-start.5 = (bf16[16,2176]{1,0:T(8,128)(2,1)S(1)}, bf16[16,2176]{1,0:T(8,128)(2,1)S(1)}, u32[]{:S(2)}, u32[]{:S(2)}) collective-permute-start(bf16[16,2176]{1,0:T(8,128)(2,1)S(1)} %get-tuple-element.26.p0_ref), channel_id=1, source_target_pairs={{0,2},{1,3},{2,0},{3,1},{4,6},{5,7},{6,4},{7,5},{8,10},{9,11},{10,... | collective-permute-start | bytes 208904 | tf_op jit(solution)/shard_map/ppermute | solution.py:418
  88.7 1.4 %collective-permute-start.6 = (bf16[16,2176]{1,0:T(8,128)(2,1)S(1)}, bf16[16,2176]{1,0:T(8,128)(2,1)S(1)}, u32[]{:S(2)}, u32[]{:S(2)}) collective-permute-start(bf16[16,2176]{1,0:T(8,128)(2,1)S(1)} %get-tuple-element.26.p0_ref), channel_id=1, source_target_pairs={{0,3},{1,0},{2,1},{3,2},{4,7},{5,4},{6,5},{7,6},{8,11},{9,8},{10,9... | collective-permute-start | bytes 208904 | tf_op jit(solution)/shard_map/ppermute | solution.py:418
  90.2 2.2 %copy-done.1 = f32[4,2064,128]{2,1,0:T(8,128)S(1)} copy-done((f32[4,2064,128]{2,1,0:T(8,128)S(1)}, f32[4,2064,128]{2,1,0:T(8,128)}, u32[]{:S(2)}) %copy-start.1) | copy-done | bytes 4227096
  92.4 5.2 %shift_next.1 = (bf16[2048,512]{1,0:T(8,128)(2,1)S(1)}, f32[8,512]{1,0:T(8,128)S(1)}) custom-call(f32[4,2064,128]{2,1,0:T(8,128)S(1)} %copy-done.1, f32[32,512]{1,0:T(8,128)S(1)} %get-tuple-element.28.side_ref), custom_call_target="tpu_custom_call" | custom-call | flops 6000000000 | bytes 20000000 | tf_op jit(solution)/shard_map/shift_next/pallas_call | solution.py:330
  97.6 5.0 %correlate.3 = (bf16[16,2048]{1,0:T(8,128)(2,1)}, f32[16,128]{1,0:T(8,128)S(1)}) custom-call(bf16[16,2176]{1,0:T(8,128)(2,1)S(1)} %get-tuple-element.26.p0_ref, bf16[16,2176]{1,0:T(8,128)(2,1)S(1)} %collective-permute-done.4.p1_ref, bf16[16,2176]{1,0:T(8,128)(2,1)S(1)} %collective-permute-done.5.p2_ref, bf16[16,2176]{1,0:T(8,128)(2,1)S(1)} %collective-permute-done.6.p3_ref, ...), custom_call_target="tpu_custom_call" | custom-call | flops 4000000000 | bytes 10000000 | tf_op jit(solution)/shard_map/correlate/pallas_call | solution.py:330
  102.6 1.2 collective-permute-done.7.other_ref
  103.8 16.9 %all_to_all.16.sums_ref = bf16[64,16,128]{2,1,0:T(8,128)(2,1)S(1)} all-to-all(bf16[64,16,128]{2,1,0:T(8,128)(2,1)S(1)} %spread.3), channel_id=1, replica_groups=mesh['y'=4,'x'=4,'core'=2,'off'=4] {'y','x','off'}, dimensions={0} | all-to-all | bytes 524288 | tf_op jit(solution)/shard_map/all_to_all | solution.py:414
  120.7 0.7 finish.1
  (18 shorter events, 0.2 us)
Async XLA Ops:
  49.4 9.7 %collective-permute-start = (bf16[16,2176]{1,0:T(8,128)(2,1)S(1)}, bf16[16,2176]{1,0:T(8,128)(2,1)S(1)}, u32[]{:S(2)}, u32[]{:S(2)}) collective-permute-start(bf16[16,2176]{1,0:T(8,128)(2,1)S(1)} %get-tuple-element.21.p0_ref), channel_id=1, source_target_pairs={{0,1},{1,2},{2,3},{3,0},{4,5},{5,6},{6,7},{7,4},{8,9},{9,10},{10,1... | collective-permute-start | bytes 208904 | tf_op jit(solution)/shard_map/ppermute | solution.py:418
  50.3 8.8 %collective-permute-start.1 = (bf16[16,2176]{1,0:T(8,128)(2,1)S(1)}, bf16[16,2176]{1,0:T(8,128)(2,1)S(1)}, u32[]{:S(2)}, u32[]{:S(2)}) collective-permute-start(bf16[16,2176]{1,0:T(8,128)(2,1)S(1)} %get-tuple-element.21.p0_ref), channel_id=1, source_target_pairs={{0,2},{1,3},{2,0},{3,1},{4,6},{5,7},{6,4},{7,5},{8,10},{9,11},{10,... | collective-permute-start | bytes 208904 | tf_op jit(solution)/shard_map/ppermute | solution.py:418
  52.0 7.1 %collective-permute-start.2 = (bf16[16,2176]{1,0:T(8,128)(2,1)S(1)}, bf16[16,2176]{1,0:T(8,128)(2,1)S(1)}, u32[]{:S(2)}, u32[]{:S(2)}) collective-permute-start(bf16[16,2176]{1,0:T(8,128)(2,1)S(1)} %get-tuple-element.21.p0_ref), channel_id=1, source_target_pairs={{0,3},{1,0},{2,1},{3,2},{4,7},{5,4},{6,5},{7,6},{8,11},{9,8},{10,9... | collective-permute-start | bytes 208904 | tf_op jit(solution)/shard_map/ppermute | solution.py:418
  59.1 5.1 %copy-start = (f32[4,2064,128]{2,1,0:T(8,128)}, f32[4,2064,128]{2,1,0:T(8,128)S(1)}, u32[]{:S(2)}) copy-start(f32[4,2064,128]{2,1,0:T(8,128)S(1)} %get-tuple-element.27.xt_ref) | copy-start | bytes 12681220
  59.1 13.2 %copy-start.2 = (f32[8]{0:T(128)S(1)}, f32[8]{0:T(128)}, u32[]{:S(2)}) copy-start(f32[8]{0:T(128)} %param.16) | copy-start | bytes 100
  59.1 13.2 %copy-start.3 = (s32[2]{0:T(128)S(1)}, s32[2]{0:T(128)}, u32[]{:S(2)}) copy-start(s32[2]{0:T(128)} %param.17) | copy-start | bytes 28
  64.2 1.2 collective-permute-start.3
  66.1 18.4 %all-to-all-start.1 = ((bf16[64,24,128]{2,1,0:T(8,128)(2,1)}), bf16[64,24,128]{2,1,0:T(8,128)(2,1)S(1)}, u32[]{:S(2)}, u32[]{:S(2)}) async-start(bf16[64,24,128]{2,1,0:T(8,128)(2,1)} %spread.2), calls=%async_computation.1 | async-start | bytes 786432 | tf_op jit(solution)/shard_map/all_to_all | solution.py:414
  86.6 11.0 %collective-permute-start.4 = (bf16[16,2176]{1,0:T(8,128)(2,1)S(1)}, bf16[16,2176]{1,0:T(8,128)(2,1)S(1)}, u32[]{:S(2)}, u32[]{:S(2)}) collective-permute-start(bf16[16,2176]{1,0:T(8,128)(2,1)S(1)} %get-tuple-element.26.p0_ref), channel_id=1, source_target_pairs={{0,1},{1,2},{2,3},{3,0},{4,5},{5,6},{6,7},{7,4},{8,9},{9,10},{10,1... | collective-permute-start | bytes 208904 | tf_op jit(solution)/shard_map/ppermute | solution.py:418
  87.3 10.3 %collective-permute-start.5 = (bf16[16,2176]{1,0:T(8,128)(2,1)S(1)}, bf16[16,2176]{1,0:T(8,128)(2,1)S(1)}, u32[]{:S(2)}, u32[]{:S(2)}) collective-permute-start(bf16[16,2176]{1,0:T(8,128)(2,1)S(1)} %get-tuple-element.26.p0_ref), channel_id=1, source_target_pairs={{0,2},{1,3},{2,0},{3,1},{4,6},{5,7},{6,4},{7,5},{8,10},{9,11},{10,... | collective-permute-start | bytes 208904 | tf_op jit(solution)/shard_map/ppermute | solution.py:418
  88.7 8.9 %collective-permute-start.6 = (bf16[16,2176]{1,0:T(8,128)(2,1)S(1)}, bf16[16,2176]{1,0:T(8,128)(2,1)S(1)}, u32[]{:S(2)}, u32[]{:S(2)}) collective-permute-start(bf16[16,2176]{1,0:T(8,128)(2,1)S(1)} %get-tuple-element.26.p0_ref), channel_id=1, source_target_pairs={{0,3},{1,0},{2,1},{3,2},{4,7},{5,4},{6,5},{7,6},{8,11},{9,8},{10,9... | collective-permute-start | bytes 208904 | tf_op jit(solution)/shard_map/ppermute | solution.py:418
  90.2 2.2 %copy-start.1 = (f32[4,2064,128]{2,1,0:T(8,128)S(1)}, f32[4,2064,128]{2,1,0:T(8,128)}, u32[]{:S(2)}) copy-start(f32[4,2064,128]{2,1,0:T(8,128)} %copy-done) | copy-start | bytes 12681220
  102.6 1.2 collective-permute-start.7

commit v7 on v6

--- a/solution.py
+++ b/solution.py
@@ -22,8 +22,9 @@
 SLOTS = DEVICES * TRACE_LIMIT
 LANES = 128
 WIDE = NS + LANES
-LROWS = 112
-LAG_TOP = 106
+LROWS = 104
+LAG_TOP = 102
+LAG_PAD = 4
 BINS_STEP = 4
 PACK_ROWS = 64
 PACK_OUT = 4
@@ -263,23 +264,23 @@
     pilot = (total[:, :NS] * lax.rsqrt(mass + 1.0)).astype(BF16)
     pilot_ref[...] = pilot
     wide = pilot.astype(F32)
-    wide_ref[:, :NS] = wide
-    wide_ref[:, NS:] = jnp.zeros((BIN_DEV, LANES), F32)
+    wide_ref[...] = pltpu.roll(jnp.concatenate([wide, jnp.zeros((BIN_DEV, LANES), F32)], axis=1), LAG_PAD, 1)
     pilot_scale = lax.rsqrt(jnp.sum(wide * wide, axis=1, keepdims=True) + EPS)
     head = side_ref[0:16, :]
     live = head[6:7, :]
     member = one_hot_rows(head[4:5, :], BIN_DEV) * live
     corr = jnp.zeros((LROWS, SLOTS), F32)
     for b0 in range(0, BIN_DEV, BINS_STEP):
-        for bb in range(BINS_STEP):
-            row = jnp.broadcast_to(wide_ref[b0 + bb : b0 + bb + 1, :], (8, WIDE))
-            for g in range(0, LROWS, 16):
-                two = [
-                    pltpu.roll(row, (WIDE - (LAG_TOP - HALF) + g + h) % WIDE, 1, stride=1, stride_axis=0)[:, :NS]
-                    for h in (0, 8)
-                ]
-                at = (b0 + bb) * LROWS + g
-                lag_ref[at : at + 16, :] = jnp.concatenate(two, axis=0).astype(BF16)
+        for bb in range(0, BINS_STEP, 2):
+            eights = []
+            for b in (b0 + bb, b0 + bb + 1):
+                row = jnp.broadcast_to(wide_ref[b : b + 1, :], (8, WIDE))
+                for g in range(0, LROWS, 8):
+                    amount = (WIDE - (LAG_TOP - HALF) - LAG_PAD + g) % WIDE
+                    eights.append(pltpu.roll(row, amount, 1, stride=1, stride_axis=0)[:, :NS])
+                    if len(eights) % 2 == 0:
+                        at = (b0 + bb) * LROWS + 8 * (len(eights) - 2)
+                        lag_ref[at : at + 16, :] = jnp.concatenate(eights[-2:], axis=0).astype(BF16)
         every = dot(lag_ref[b0 * LROWS : (b0 + BINS_STEP) * LROWS, :], st_ref[...], NN)
         for bb in range(BINS_STEP):
             corr = corr + member[b0 + bb : b0 + bb + 1, :] * every[bb * LROWS : (bb + 1) * LROWS, :]
@@ -319,7 +320,7 @@
 VMEM = pl.BlockSpec(memory_space=pltpu.VMEM)
 HBM = pl.BlockSpec(memory_space=pl.ANY)
 SMEM = pl.BlockSpec(memory_space=pltpu.SMEM)
-PARAMS = pltpu.CompilerParams(vmem_limit_bytes=40 * 1024 * 1024)
+PARAMS = pltpu.CompilerParams(vmem_limit_bytes=24 * 1024 * 1024)
 
 
 def shape(dims, dtype):

time: 122 us -> 121 us (level)
  no operation moved by 1% of the time
where the time goes in v7:
time: 121 us
  blocking collectives  59.2 us (49%)
  Pallas kernels  30.5 us (25%)
  waiting for transfers between devices  14.1 us (12%)
  starting transfers between devices  13.6 us (11%)
  local copies, waits for them, and re-layouts  2.44 us (2%)
    all_to_all x1, blocking collectives, on_device(): lax.all_to_all(outgoing, AXES, split_axis=0, concat_axis=0, tiled=True)  42.4 us
    pallas_call x9, Pallas kernels, call(): pl.pallas_call(kernel, out_shape=out, in_specs=[SMEM if space else VMEM f...  26.1 us
    all_to_all x1, blocking collectives, sum_copies(): lax.all_to_all(copies, ('y', 'x', 'off'), split_axis=0, concat_axis=0, ti...  16.9 us
    all_to_all x1, waiting for transfers between devices, sum_copies(): lax.all_to_all(copies, ('y', 'x', 'off'), split_axis=0, concat_axis=0, ti...  11.7 us
    ppermute x6, starting transfers between devices, exchange(): return (part, *[lax.ppermute(part, 'off', off_perm(d)) for d in (1, 2, 3)])  7.27 us
    all_to_all x1, starting transfers between devices, sum_copies(): lax.all_to_all(copies, ('y', 'x', 'off'), split_axis=0, concat_axis=0, ti...  6.37 us
    pallas_call x1, Pallas kernels, pack(): pl.pallas_call(pack_kernel, out_shape=shape((DEVICES, TRACE_LIMIT, WIDE),...  4.43 us
  transfers between devices with their start and end apart: 9, of which 3 were waited for; matrix products, arithmetic and copies ran while one was open for 0% of the time, Pallas kernels for 9%

profile of v7, /device:TPU:0, one launch (start us, length us, event | category | flops | bytes accessed | tf_op | source)
XLA Modules:
  0.0 120.9 jit_solution(8989612658085786496)
XLA Ops:
  0.6 4.4 %pack.1 = bf16[128,4,2176]{2,1,0:T(4,128)(2,1)} custom-call(s32[1,256]{1,0:T(1,128)} %bitcast.8, s32[1,256]{1,0:T(1,128)} %bitcast.9, s32[1,256]{1,0:T(1,128)} %bitcast.10, s32[1,256]{1,0:T(1,128)} %bitcast.11, s32[1,256]{1,0:T(1,128)} %bitcast.12, s32[1,256]{1,0:T(1,128)} %bitcast.13, bf16[256,2048]{1,0:T(8,128)(2,1)} %refs_6_.1), custom_call_target="tpu_custom_call" | custom-call | tf_op jit(solution)/shard_map/pack/pallas_call | solution.py:352
  5.1 42.4 %all_to_all.15.slots_ref = bf16[128,4,2176]{2,1,0:T(4,128)(2,1)S(1)} all-to-all(bf16[128,4,2176]{2,1,0:T(4,128)(2,1)} %pack.1), channel_id=1, replica_groups=mesh['y'=4,'x'=4,'core'=2,'off'=4] {'y','x','core','off'}, dimensions={0} | all-to-all | bytes 4456448 | tf_op jit(solution)/shard_map/all_to_all | solution.py:434
  47.4 2.0 %stack_first.1 = (bf16[16,2176]{1,0:T(8,128)(2,1)S(1)}, f32[32,512]{1,0:T(8,128)S(1)}, bf16[512,2176]{1,0:T(8,128)(2,1)S(1)}) custom-call(bf16[128,4,2176]{2,1,0:T(4,128)(2,1)S(1)} %all_to_all.15.slots_ref), custom_call_target="tpu_custom_call" | custom-call | flops 3000000000 | bytes 10000000 | tf_op jit(solution)/shard_map/stack_first/pallas_call | solution.py:331
  49.4 0.9 collective-permute-start
  50.3 1.7 %collective-permute-start.1 = (bf16[16,2176]{1,0:T(8,128)(2,1)S(1)}, bf16[16,2176]{1,0:T(8,128)(2,1)S(1)}, u32[]{:S(2)}, u32[]{:S(2)}) collective-permute-start(bf16[16,2176]{1,0:T(8,128)(2,1)S(1)} %get-tuple-element.21.p0_ref), channel_id=1, source_target_pairs={{0,2},{1,3},{2,0},{3,1},{4,6},{5,7},{6,4},{7,5},{8,10},{9,11},{10,... | collective-permute-start | bytes 208904 | tf_op jit(solution)/shard_map/ppermute | solution.py:419
  52.0 1.0 collective-permute-start.2
  53.1 6.0 %shift_first.1 = (bf16[2048,512]{1,0:T(8,128)(2,1)S(1)}, f32[8,512]{1,0:T(8,128)S(1)}, f32[4,2064,128]{2,1,0:T(8,128)S(1)}) custom-call(bf16[512,2176]{1,0:T(8,128)(2,1)S(1)} %get-tuple-element.19.y_ref, f32[32,512]{1,0:T(8,128)S(1)} %get-tuple-element.20.side_ref.head_ref), custom_call_target="tpu_custom_call" | custom-call | flops 6000000000 | bytes 20000000 | tf_op jit(solution)/shard_map/shift_first/pallas_call | solution.py:331
  59.2 4.7 %correlate.2 = (bf16[16,2048]{1,0:T(8,128)(2,1)}, f32[32,128]{1,0:T(8,128)S(1)}) custom-call(bf16[16,2176]{1,0:T(8,128)(2,1)S(1)} %get-tuple-element.21.p0_ref, bf16[16,2176]{1,0:T(8,128)(2,1)S(1)} %collective-permute-done.p1_ref, bf16[16,2176]{1,0:T(8,128)(2,1)S(1)} %collective-permute-done.1.p2_ref, bf16[16,2176]{1,0:T(8,128)(2,1)S(1)} %collective-permute-done.2.p3_ref, ...), custom_call_target="tpu_custom_call" | custom-call | flops 4000000000 | bytes 10000000 | tf_op jit(solution)/shard_map/correlate/pallas_call | solution.py:331
  63.9 1.2 collective-permute-done.3.other_ref
  65.1 0.8 spread.2
  65.9 6.4 %all-to-all-start.1 = ((bf16[64,24,128]{2,1,0:T(8,128)(2,1)}), bf16[64,24,128]{2,1,0:T(8,128)(2,1)S(1)}, u32[]{:S(2)}, u32[]{:S(2)}) async-start(bf16[64,24,128]{2,1,0:T(8,128)(2,1)} %spread.2), calls=%async_computation.1 | async-start | bytes 786432 | tf_op jit(solution)/shard_map/all_to_all | solution.py:415
  72.3 0.2 fusion
  72.5 0.1 broadcast_in_dim.23
  72.6 11.7 %all-to-all-done.1.sums_ref = bf16[64,24,128]{2,1,0:T(8,128)(2,1)S(1)} async-done(((bf16[64,24,128]{2,1,0:T(8,128)(2,1)}), bf16[64,24,128]{2,1,0:T(8,128)(2,1)S(1)}, u32[]{:S(2)}, u32[]{:S(2)}) %all-to-all-start.1) | async-done | bytes 393248 | tf_op jit(solution)/shard_map/all_to_all | solution.py:415
  84.4 2.0 %stack_next.1 = (bf16[16,2176]{1,0:T(8,128)(2,1)S(1)}, f32[32,512]{1,0:T(8,128)S(1)}, f32[32,128]{1,0:T(8,128)S(1)}) custom-call(f32[16,128]{1,0:T(8,128)S(1)} %broadcast_in_dim.24.damp_ref, bf16[512,2176]{1,0:T(8,128)(2,1)S(1)} %get-tuple-element.19.y_ref, f32[32,512]{1,0:T(8,128)S(1)} %get-tuple-element.20.side_ref.head_ref, ...), custom_call_target="tpu_custom_call" | custom-call | flops 3000000000 | bytes 10000000 | tf_op jit(solution)/shard_map/stack_next/pallas_call | solution.py:331
  86.3 0.7 collective-permute-start.4
  87.0 1.5 %collective-permute-start.5 = (bf16[16,2176]{1,0:T(8,128)(2,1)S(1)}, bf16[16,2176]{1,0:T(8,128)(2,1)S(1)}, u32[]{:S(2)}, u32[]{:S(2)}) collective-permute-start(bf16[16,2176]{1,0:T(8,128)(2,1)S(1)} %get-tuple-element.26.p0_ref), channel_id=1, source_target_pairs={{0,2},{1,3},{2,0},{3,1},{4,6},{5,7},{6,4},{7,5},{8,10},{9,11},{10,... | collective-permute-start | bytes 208904 | tf_op jit(solution)/shard_map/ppermute | solution.py:419
  88.5 1.4 %collective-permute-start.6 = (bf16[16,2176]{1,0:T(8,128)(2,1)S(1)}, bf16[16,2176]{1,0:T(8,128)(2,1)S(1)}, u32[]{:S(2)}, u32[]{:S(2)}) collective-permute-start(bf16[16,2176]{1,0:T(8,128)(2,1)S(1)} %get-tuple-element.26.p0_ref), channel_id=1, source_target_pairs={{0,3},{1,0},{2,1},{3,2},{4,7},{5,4},{6,5},{7,6},{8,11},{9,8},{10,9... | collective-permute-start | bytes 208904 | tf_op jit(solution)/shard_map/ppermute | solution.py:419
  89.9 2.2 %copy-done.1 = f32[4,2064,128]{2,1,0:T(8,128)S(1)} copy-done((f32[4,2064,128]{2,1,0:T(8,128)S(1)}, f32[4,2064,128]{2,1,0:T(8,128)}, u32[]{:S(2)}) %copy-start.1) | copy-done | bytes 4227096
  92.1 5.2 %shift_next.1 = (bf16[2048,512]{1,0:T(8,128)(2,1)S(1)}, f32[8,512]{1,0:T(8,128)S(1)}) custom-call(f32[4,2064,128]{2,1,0:T(8,128)S(1)} %copy-done.1, f32[32,512]{1,0:T(8,128)S(1)} %get-tuple-element.28.side_ref), custom_call_target="tpu_custom_call" | custom-call | flops 6000000000 | bytes 20000000 | tf_op jit(solution)/shard_map/shift_next/pallas_call | solution.py:331
  97.4 4.7 %correlate.3 = (bf16[16,2048]{1,0:T(8,128)(2,1)}, f32[16,128]{1,0:T(8,128)S(1)}) custom-call(bf16[16,2176]{1,0:T(8,128)(2,1)S(1)} %get-tuple-element.26.p0_ref, bf16[16,2176]{1,0:T(8,128)(2,1)S(1)} %collective-permute-done.4.p1_ref, bf16[16,2176]{1,0:T(8,128)(2,1)S(1)} %collective-permute-done.5.p2_ref, bf16[16,2176]{1,0:T(8,128)(2,1)S(1)} %collective-permute-done.6.p3_ref, ...), custom_call_target="tpu_custom_call" | custom-call | flops 4000000000 | bytes 10000000 | tf_op jit(solution)/shard_map/correlate/pallas_call | solution.py:331
  102.1 1.2 collective-permute-done.7.other_ref
  103.3 16.9 %all_to_all.16.sums_ref = bf16[64,16,128]{2,1,0:T(8,128)(2,1)S(1)} all-to-all(bf16[64,16,128]{2,1,0:T(8,128)(2,1)S(1)} %spread.3), channel_id=1, replica_groups=mesh['y'=4,'x'=4,'core'=2,'off'=4] {'y','x','off'}, dimensions={0} | all-to-all | bytes 524288 | tf_op jit(solution)/shard_map/all_to_all | solution.py:415
  120.2 0.7 finish.1
  (18 shorter events, 0.2 us)
Async XLA Ops:
  49.4 9.7 %collective-permute-start = (bf16[16,2176]{1,0:T(8,128)(2,1)S(1)}, bf16[16,2176]{1,0:T(8,128)(2,1)S(1)}, u32[]{:S(2)}, u32[]{:S(2)}) collective-permute-start(bf16[16,2176]{1,0:T(8,128)(2,1)S(1)} %get-tuple-element.21.p0_ref), channel_id=1, source_target_pairs={{0,1},{1,2},{2,3},{3,0},{4,5},{5,6},{6,7},{7,4},{8,9},{9,10},{10,1... | collective-permute-start | bytes 208904 | tf_op jit(solution)/shard_map/ppermute | solution.py:419
  50.3 8.8 %collective-permute-start.1 = (bf16[16,2176]{1,0:T(8,128)(2,1)S(1)}, bf16[16,2176]{1,0:T(8,128)(2,1)S(1)}, u32[]{:S(2)}, u32[]{:S(2)}) collective-permute-start(bf16[16,2176]{1,0:T(8,128)(2,1)S(1)} %get-tuple-element.21.p0_ref), channel_id=1, source_target_pairs={{0,2},{1,3},{2,0},{3,1},{4,6},{5,7},{6,4},{7,5},{8,10},{9,11},{10,... | collective-permute-start | bytes 208904 | tf_op jit(solution)/shard_map/ppermute | solution.py:419
  52.0 7.1 %collective-permute-start.2 = (bf16[16,2176]{1,0:T(8,128)(2,1)S(1)}, bf16[16,2176]{1,0:T(8,128)(2,1)S(1)}, u32[]{:S(2)}, u32[]{:S(2)}) collective-permute-start(bf16[16,2176]{1,0:T(8,128)(2,1)S(1)} %get-tuple-element.21.p0_ref), channel_id=1, source_target_pairs={{0,3},{1,0},{2,1},{3,2},{4,7},{5,4},{6,5},{7,6},{8,11},{9,8},{10,9... | collective-permute-start | bytes 208904 | tf_op jit(solution)/shard_map/ppermute | solution.py:419
  59.1 4.8 %copy-start = (f32[4,2064,128]{2,1,0:T(8,128)}, f32[4,2064,128]{2,1,0:T(8,128)S(1)}, u32[]{:S(2)}) copy-start(f32[4,2064,128]{2,1,0:T(8,128)S(1)} %get-tuple-element.27.xt_ref) | copy-start | bytes 12681220
  59.1 13.1 %copy-start.2 = (f32[8]{0:T(128)S(1)}, f32[8]{0:T(128)}, u32[]{:S(2)}) copy-start(f32[8]{0:T(128)} %param.16) | copy-start | bytes 100
  59.1 13.1 %copy-start.3 = (s32[2]{0:T(128)S(1)}, s32[2]{0:T(128)}, u32[]{:S(2)}) copy-start(s32[2]{0:T(128)} %param.17) | copy-start | bytes 28
  63.9 1.2 collective-permute-start.3
  65.9 18.4 %all-to-all-start.1 = ((bf16[64,24,128]{2,1,0:T(8,128)(2,1)}), bf16[64,24,128]{2,1,0:T(8,128)(2,1)S(1)}, u32[]{:S(2)}, u32[]{:S(2)}) async-start(bf16[64,24,128]{2,1,0:T(8,128)(2,1)} %spread.2), calls=%async_computation.1 | async-start | bytes 786432 | tf_op jit(solution)/shard_map/all_to_all | solution.py:415
  86.3 11.0 %collective-permute-start.4 = (bf16[16,2176]{1,0:T(8,128)(2,1)S(1)}, bf16[16,2176]{1,0:T(8,128)(2,1)S(1)}, u32[]{:S(2)}, u32[]{:S(2)}) collective-permute-start(bf16[16,2176]{1,0:T(8,128)(2,1)S(1)} %get-tuple-element.26.p0_ref), channel_id=1, source_target_pairs={{0,1},{1,2},{2,3},{3,0},{4,5},{5,6},{6,7},{7,4},{8,9},{9,10},{10,1... | collective-permute-start | bytes 208904 | tf_op jit(solution)/shard_map/ppermute | solution.py:419
  87.0 10.3 %collective-permute-start.5 = (bf16[16,2176]{1,0:T(8,128)(2,1)S(1)}, bf16[16,2176]{1,0:T(8,128)(2,1)S(1)}, u32[]{:S(2)}, u32[]{:S(2)}) collective-permute-start(bf16[16,2176]{1,0:T(8,128)(2,1)S(1)} %get-tuple-element.26.p0_ref), channel_id=1, source_target_pairs={{0,2},{1,3},{2,0},{3,1},{4,6},{5,7},{6,4},{7,5},{8,10},{9,11},{10,... | collective-permute-start | bytes 208904 | tf_op jit(solution)/shard_map/ppermute | solution.py:419
  88.5 8.9 %collective-permute-start.6 = (bf16[16,2176]{1,0:T(8,128)(2,1)S(1)}, bf16[16,2176]{1,0:T(8,128)(2,1)S(1)}, u32[]{:S(2)}, u32[]{:S(2)}) collective-permute-start(bf16[16,2176]{1,0:T(8,128)(2,1)S(1)} %get-tuple-element.26.p0_ref), channel_id=1, source_target_pairs={{0,3},{1,0},{2,1},{3,2},{4,7},{5,4},{6,5},{7,6},{8,11},{9,8},{10,9... | collective-permute-start | bytes 208904 | tf_op jit(solution)/shard_map/ppermute | solution.py:419
  89.9 2.2 %copy-start.1 = (f32[4,2064,128]{2,1,0:T(8,128)S(1)}, f32[4,2064,128]{2,1,0:T(8,128)}, u32[]{:S(2)}) copy-start(f32[4,2064,128]{2,1,0:T(8,128)} %copy-done) | copy-start | bytes 12681220
  102.1 1.2 collective-permute-start.7

commit v8 on v7

--- a/solution.py
+++ b/solution.py
@@ -180,7 +180,8 @@
     part_ref[:, NS:] = tail.astype(BF16)
 
 
-def first_kernel(slots_ref, part_ref, side_ref, y_ref, sum_ref):
+def first_kernel(damp_ref, slots_ref, part_ref, side_ref, y_ref, kept_ref, sum_ref):
+    kept_ref[...] = damp_ref[...]
     y_ref[...] = slots_ref[...].reshape(SLOTS, WIDE)
     head = dot(unit(LANES), y_ref[:, NS:], NT)[HEAD : HEAD + 16, :]
     stack_rows(y_ref, head, head[5:6, :] * (1.0 / NPHASE), side_ref, part_ref, sum_ref)
@@ -365,9 +366,9 @@
 ROWS = pltpu.VMEM((TAPS * BIN_DEV, WIDE), F32)
 
 
-def stack_first(slots):
-    out = (PART, SIDE, shape((SLOTS, WIDE), BF16))
-    return call(first_kernel, out, (0,), [ROWS], "stack_first", 3 * 10**9, 10**7, slots)
+def stack_first(damps, slots):
+    out = (PART, SIDE, shape((SLOTS, WIDE), BF16), shape((16, LANES), F32))
+    return call(first_kernel, out, (0, 0), [ROWS], "stack_first", 3 * 10**9, 10**7, damps, slots)
 
 
 KNOWN = shape((32, LANES), F32)
@@ -435,7 +436,7 @@
     entries = jnp.arange(damping_table.shape[0], dtype=jnp.int32)
     chosen = jnp.sum(jnp.where(entries == damping_index[:, None], damping_table, 0.0), axis=1)
     damps = jnp.broadcast_to(chosen[:, None, None], (2, 8, LANES)).reshape(16, LANES)
-    part, side, rows = stack_first(slots)
+    part, side, rows, damps = stack_first(damps, slots)
     parts = exchange(part)
     shifted, energy, turned = shift_first(rows, side)
     pilot, sums = correlate(True, parts, shifted, energy, side)

time: 121 us -> 118 us (0.975)
  blocking collectives: 59.2 us -> 36.4 us
  waiting for transfers between devices: 14.1 us -> 33.4 us
  starting transfers between devices: 13.6 us -> 16.9 us
  local copies, waits for them, and re-layouts: 2.44 us -> 0.24 us
    all_to_all x1 -> x0, blocking collectives: 42.4 us -> none  [on_device(): lax.all_to_all(outgoing, AXES, split_axis=0, concat_axis=0, tiled=True)]
    all_to_all x1 -> x2, blocking collectives: 16.9 us -> 36.4 us  [sum_copies(): lax.all_to_all(copies, ('y', 'x', 'off'), split_axis=0, concat_axis=0, ti...]
    all_to_all x1, waiting for transfers between devices: 11.7 us -> 30.8 us  [on_device(): lax.all_to_all(outgoing, AXES, split_axis=0, concat_axis=0, tiled=True)]
    all_to_all x1, starting transfers between devices: 6.37 us -> 11.2 us  [on_device(): lax.all_to_all(outgoing, AXES, split_axis=0, concat_axis=0, tiled=True)]
    unnamed x8 -> x4, local copies, waits for them, and re-layouts: 2.21 us -> 0.01 us
    ppermute x6, starting transfers between devices: 7.27 us -> 5.74 us  [exchange(): return (part, *[lax.ppermute(part, 'off', off_perm(d)) for d in (1, 2, 3)])]
  transfers between devices with their start and end apart: 9 -> 9, of which waited for: 3 -> 4; matrix products, arithmetic and copies ran while one was open for 0% -> 0% of each run, Pallas kernels for 9% -> 10%
where the time goes in v8:
time: 118 us
  blocking collectives  36.4 us (31%)
  waiting for transfers between devices  33.4 us (28%)
  Pallas kernels  30.1 us (26%)
  starting transfers between devices  16.9 us (14%)
    all_to_all x2, blocking collectives, sum_copies(): lax.all_to_all(copies, ('y', 'x', 'off'), split_axis=0, concat_axis=0, ti...  36.4 us
    all_to_all x1, waiting for transfers between devices, on_device(): lax.all_to_all(outgoing, AXES, split_axis=0, concat_axis=0, tiled=True)  30.8 us
    pallas_call x9, Pallas kernels, call(): pl.pallas_call(kernel, out_shape=out, in_specs=[SMEM if space else VMEM f...  25.6 us
    all_to_all x1, starting transfers between devices, on_device(): lax.all_to_all(outgoing, AXES, split_axis=0, concat_axis=0, tiled=True)  11.2 us
    ppermute x6, starting transfers between devices, exchange(): return (part, *[lax.ppermute(part, 'off', off_perm(d)) for d in (1, 2, 3)])  5.74 us
    pallas_call x1, Pallas kernels, pack(): pl.pallas_call(pack_kernel, out_shape=shape((DEVICES, TRACE_LIMIT, WIDE),...  4.44 us
  transfers between devices with their start and end apart: 9, of which 4 were waited for; matrix products, arithmetic and copies ran while one was open for 0% of the time, Pallas kernels for 10%

profile of v8, /device:TPU:0, one launch (start us, length us, event | category | flops | bytes accessed | tf_op | source)
XLA Modules:
  0.0 118.0 jit_solution(15944768998276778368)
XLA Ops:
  0.6 4.4 %pack.1 = bf16[128,4,2176]{2,1,0:T(4,128)(2,1)} custom-call(s32[1,256]{1,0:T(1,128)} %bitcast.8, s32[1,256]{1,0:T(1,128)} %bitcast.9, s32[1,256]{1,0:T(1,128)} %bitcast.10, s32[1,256]{1,0:T(1,128)} %bitcast.11, s32[1,256]{1,0:T(1,128)} %bitcast.12, s32[1,256]{1,0:T(1,128)} %bitcast.13, bf16[256,2048]{1,0:T(8,128)(2,1)} %refs_6_.1), custom_call_target="tpu_custom_call" | custom-call | tf_op jit(solution)/shard_map/pack/pallas_call | solution.py:353
  5.1 0.0 copy-start
  5.1 11.2 %all-to-all-start = ((bf16[128,4,2176]{2,1,0:T(4,128)(2,1)}), bf16[128,4,2176]{2,1,0:T(4,128)(2,1)S(1)}, u32[]{:S(2)}, u32[]{:S(2)}) async-start(bf16[128,4,2176]{2,1,0:T(4,128)(2,1)} %pack.1), calls=%async_computation | async-start | bytes 4456448 | tf_op jit(solution)/shard_map/all_to_all | solution.py:435
  16.3 0.2 fusion
  16.5 0.1 broadcast_in_dim.22
  16.5 0.1 broadcast_in_dim.23
  16.6 30.8 %all-to-all-done.slots_ref = bf16[128,4,2176]{2,1,0:T(4,128)(2,1)S(1)} async-done(((bf16[128,4,2176]{2,1,0:T(4,128)(2,1)}), bf16[128,4,2176]{2,1,0:T(4,128)(2,1)S(1)}, u32[]{:S(2)}, u32[]{:S(2)}) %all-to-all-start) | async-done | bytes 2228256 | tf_op jit(solution)/shard_map/all_to_all | solution.py:435
  47.5 0.1 broadcast_in_dim.24.damp_ref
  47.5 2.0 %stack_first.1 = (bf16[16,2176]{1,0:T(8,128)(2,1)S(1)}, f32[32,512]{1,0:T(8,128)S(1)}, bf16[512,2176]{1,0:T(8,128)(2,1)S(1)}, f32[16,128]{1,0:T(8,128)S(1)}) custom-call(f32[16,128]{1,0:T(8,128)S(1)} %broadcast_in_dim.24.damp_ref, bf16[128,4,2176]{2,1,0:T(4,128)(2,1)S(1)} %all-to-all-done.slots_ref), custom_call_target="tpu_custom_call" | custom-call | flops 3000000000 | bytes 10000000 | tf_op jit(solution)/shard_map/stack_first/pallas_call | solution.py:332
  49.6 1.2 collective-permute-start.2
  50.7 1.8 %collective-permute-start.1 = (bf16[16,2176]{1,0:T(8,128)(2,1)S(1)}, bf16[16,2176]{1,0:T(8,128)(2,1)S(1)}, u32[]{:S(2)}, u32[]{:S(2)}) collective-permute-start(bf16[16,2176]{1,0:T(8,128)(2,1)S(1)} %get-tuple-element.23.p0_ref), channel_id=1, source_target_pairs={{0,2},{1,3},{2,0},{3,1},{4,6},{5,7},{6,4},{7,5},{8,10},{9,11},{10,... | collective-permute-start | bytes 208904 | tf_op jit(solution)/shard_map/ppermute | solution.py:420
  52.5 6.0 %shift_first.1 = (bf16[2048,512]{1,0:T(8,128)(2,1)S(1)}, f32[8,512]{1,0:T(8,128)S(1)}, f32[4,2064,128]{2,1,0:T(8,128)S(1)}) custom-call(bf16[512,2176]{1,0:T(8,128)(2,1)S(1)} %get-tuple-element.21.y_ref, f32[32,512]{1,0:T(8,128)S(1)} %get-tuple-element.22.side_ref.head_ref), custom_call_target="tpu_custom_call" | custom-call | flops 6000000000 | bytes 20000000 | tf_op jit(solution)/shard_map/shift_first/pallas_call | solution.py:332
  58.6 4.7 %correlate.2 = (bf16[16,2048]{1,0:T(8,128)(2,1)}, f32[32,128]{1,0:T(8,128)S(1)}) custom-call(bf16[16,2176]{1,0:T(8,128)(2,1)S(1)} %get-tuple-element.23.p0_ref, bf16[16,2176]{1,0:T(8,128)(2,1)S(1)} %collective-permute-done.p1_ref, bf16[16,2176]{1,0:T(8,128)(2,1)S(1)} %collective-permute-done.1.p2_ref, bf16[16,2176]{1,0:T(8,128)(2,1)S(1)} %collective-permute-done.2.p3_ref, ...), custom_call_target="tpu_custom_call" | custom-call | flops 4000000000 | bytes 10000000 | tf_op jit(solution)/shard_map/correlate/pallas_call | solution.py:332
  63.3 1.2 %collective-permute-done.3.other_ref = f32[32,128]{1,0:T(8,128)S(1)} collective-permute-done((f32[32,128]{1,0:T(8,128)S(1)}, f32[32,128]{1,0:T(8,128)S(1)}, u32[]{:S(2)}, u32[]{:S(2)}) %collective-permute-start.3) | collective-permute-done | bytes 16416 | tf_op jit(solution)/shard_map/ppermute | solution.py:411
  64.5 19.0 %all_to_all.15.sums_ref = bf16[64,24,128]{2,1,0:T(8,128)(2,1)S(1)} all-to-all(bf16[64,24,128]{2,1,0:T(8,128)(2,1)S(1)} %spread.2), channel_id=1, replica_groups=mesh['y'=4,'x'=4,'core'=2,'off'=4] {'y','x','off'}, dimensions={0} | all-to-all | bytes 786432 | tf_op jit(solution)/shard_map/all_to_all | solution.py:416
  83.5 2.0 %stack_next.1 = (bf16[16,2176]{1,0:T(8,128)(2,1)S(1)}, f32[32,512]{1,0:T(8,128)S(1)}, f32[32,128]{1,0:T(8,128)S(1)}) custom-call(f32[16,128]{1,0:T(8,128)S(1)} %get-tuple-element.20.damp_ref, bf16[512,2176]{1,0:T(8,128)(2,1)S(1)} %get-tuple-element.21.y_ref, f32[32,512]{1,0:T(8,128)S(1)} %get-tuple-element.22.side_ref.head_ref, ...), custom_call_target="tpu_custom_call" | custom-call | flops 3000000000 | bytes 10000000 | tf_op jit(solution)/shard_map/stack_next/pallas_call | solution.py:332
  85.5 0.7 collective-permute-start.6
  86.2 2.1 %collective-permute-start.5 = (bf16[16,2176]{1,0:T(8,128)(2,1)S(1)}, bf16[16,2176]{1,0:T(8,128)(2,1)S(1)}, u32[]{:S(2)}, u32[]{:S(2)}) collective-permute-start(bf16[16,2176]{1,0:T(8,128)(2,1)S(1)} %get-tuple-element.28.p0_ref), channel_id=1, source_target_pairs={{0,2},{1,3},{2,0},{3,1},{4,6},{5,7},{6,4},{7,5},{8,10},{9,11},{10,... | collective-permute-start | bytes 208904 | tf_op jit(solution)/shard_map/ppermute | solution.py:420
  88.3 5.2 %shift_next.1 = (bf16[2048,512]{1,0:T(8,128)(2,1)S(1)}, f32[8,512]{1,0:T(8,128)S(1)}) custom-call(f32[4,2064,128]{2,1,0:T(8,128)S(1)} %get-tuple-element.29.xt_ref, f32[32,512]{1,0:T(8,128)S(1)} %get-tuple-element.30.side_ref), custom_call_target="tpu_custom_call" | custom-call | flops 6000000000 | bytes 20000000 | tf_op jit(solution)/shard_map/shift_next/pallas_call | solution.py:332
  93.6 0.3 collective-permute-done.4.p1_ref
  93.8 4.9 %correlate.3 = (bf16[16,2048]{1,0:T(8,128)(2,1)}, f32[16,128]{1,0:T(8,128)S(1)}) custom-call(bf16[16,2176]{1,0:T(8,128)(2,1)S(1)} %get-tuple-element.28.p0_ref, bf16[16,2176]{1,0:T(8,128)(2,1)S(1)} %collective-permute-done.4.p1_ref, bf16[16,2176]{1,0:T(8,128)(2,1)S(1)} %collective-permute-done.5.p2_ref, bf16[16,2176]{1,0:T(8,128)(2,1)S(1)} %collective-permute-done.6.p3_ref, ...), custom_call_target="tpu_custom_call" | custom-call | flops 4000000000 | bytes 10000000 | tf_op jit(solution)/shard_map/correlate/pallas_call | solution.py:332
  98.7 1.2 collective-permute-done.7.other_ref
  99.9 17.5 %all_to_all.16.sums_ref = bf16[64,16,128]{2,1,0:T(8,128)(2,1)S(1)} all-to-all(bf16[64,16,128]{2,1,0:T(8,128)(2,1)S(1)} %spread.3), channel_id=1, replica_groups=mesh['y'=4,'x'=4,'core'=2,'off'=4] {'y','x','off'}, dimensions={0} | all-to-all | bytes 524288 | tf_op jit(solution)/shard_map/all_to_all | solution.py:416
  117.4 0.7 finish.1
  (14 shorter events, 0.1 us)
Async XLA Ops:
  5.1 11.2 %copy-start = (f32[8]{0:T(128)S(1)}, f32[8]{0:T(128)}, u32[]{:S(2)}) copy-start(f32[8]{0:T(128)} %param.16) | copy-start | bytes 100
  5.1 11.2 %copy-start.1 = (s32[2]{0:T(128)S(1)}, s32[2]{0:T(128)}, u32[]{:S(2)}) copy-start(s32[2]{0:T(128)} %param.17) | copy-start | bytes 28
  5.1 42.4 %all-to-all-start = ((bf16[128,4,2176]{2,1,0:T(4,128)(2,1)}), bf16[128,4,2176]{2,1,0:T(4,128)(2,1)S(1)}, u32[]{:S(2)}, u32[]{:S(2)}) async-start(bf16[128,4,2176]{2,1,0:T(4,128)(2,1)} %pack.1), calls=%async_computation | async-start | bytes 4456448 | tf_op jit(solution)/shard_map/all_to_all | solution.py:435
  49.6 9.0 %collective-permute-start.2 = (bf16[16,2176]{1,0:T(8,128)(2,1)S(1)}, bf16[16,2176]{1,0:T(8,128)(2,1)S(1)}, u32[]{:S(2)}, u32[]{:S(2)}) collective-permute-start(bf16[16,2176]{1,0:T(8,128)(2,1)S(1)} %get-tuple-element.23.p0_ref), channel_id=1, source_target_pairs={{0,3},{1,0},{2,1},{3,2},{4,7},{5,4},{6,5},{7,6},{8,11},{9,8},{10,9... | collective-permute-start | bytes 208904 | tf_op jit(solution)/shard_map/ppermute | solution.py:420
  50.7 7.8 %collective-permute-start.1 = (bf16[16,2176]{1,0:T(8,128)(2,1)S(1)}, bf16[16,2176]{1,0:T(8,128)(2,1)S(1)}, u32[]{:S(2)}, u32[]{:S(2)}) collective-permute-start(bf16[16,2176]{1,0:T(8,128)(2,1)S(1)} %get-tuple-element.23.p0_ref), channel_id=1, source_target_pairs={{0,2},{1,3},{2,0},{3,1},{4,6},{5,7},{6,4},{7,5},{8,10},{9,11},{10,... | collective-permute-start | bytes 208904 | tf_op jit(solution)/shard_map/ppermute | solution.py:420
  52.5 6.0 %collective-permute-start = (bf16[16,2176]{1,0:T(8,128)(2,1)S(1)}, bf16[16,2176]{1,0:T(8,128)(2,1)S(1)}, u32[]{:S(2)}, u32[]{:S(2)}) collective-permute-start(bf16[16,2176]{1,0:T(8,128)(2,1)S(1)} %get-tuple-element.23.p0_ref), channel_id=1, source_target_pairs={{0,1},{1,2},{2,3},{3,0},{4,5},{5,6},{6,7},{7,4},{8,9},{9,10},{10,1... | collective-permute-start | bytes 208904 | tf_op jit(solution)/shard_map/ppermute | solution.py:420
  63.3 1.2 %collective-permute-start.3 = (f32[32,128]{1,0:T(8,128)S(1)}, f32[32,128]{1,0:T(8,128)S(1)}, u32[]{:S(2)}, u32[]{:S(2)}) collective-permute-start(f32[32,128]{1,0:T(8,128)S(1)} %get-tuple-element.26.own_ref), channel_id=1, source_target_pairs={{0,4},{4,0},{1,5},{5,1},{2,6},{6,2},{3,7},{7,3},{8,12},{12,8},{9,1... | collective-permute-start | bytes 49160 | tf_op jit(solution)/shard_map/ppermute | solution.py:411
  85.5 8.0 %collective-permute-start.6 = (bf16[16,2176]{1,0:T(8,128)(2,1)S(1)}, bf16[16,2176]{1,0:T(8,128)(2,1)S(1)}, u32[]{:S(2)}, u32[]{:S(2)}) collective-permute-start(bf16[16,2176]{1,0:T(8,128)(2,1)S(1)} %get-tuple-element.28.p0_ref), channel_id=1, source_target_pairs={{0,3},{1,0},{2,1},{3,2},{4,7},{5,4},{6,5},{7,6},{8,11},{9,8},{10,9... | collective-permute-start | bytes 208904 | tf_op jit(solution)/shard_map/ppermute | solution.py:420
  86.2 7.3 %collective-permute-start.5 = (bf16[16,2176]{1,0:T(8,128)(2,1)S(1)}, bf16[16,2176]{1,0:T(8,128)(2,1)S(1)}, u32[]{:S(2)}, u32[]{:S(2)}) collective-permute-start(bf16[16,2176]{1,0:T(8,128)(2,1)S(1)} %get-tuple-element.28.p0_ref), channel_id=1, source_target_pairs={{0,2},{1,3},{2,0},{3,1},{4,6},{5,7},{6,4},{7,5},{8,10},{9,11},{10,... | collective-permute-start | bytes 208904 | tf_op jit(solution)/shard_map/ppermute | solution.py:420
  88.3 5.5 %collective-permute-start.4 = (bf16[16,2176]{1,0:T(8,128)(2,1)S(1)}, bf16[16,2176]{1,0:T(8,128)(2,1)S(1)}, u32[]{:S(2)}, u32[]{:S(2)}) collective-permute-start(bf16[16,2176]{1,0:T(8,128)(2,1)S(1)} %get-tuple-element.28.p0_ref), channel_id=1, source_target_pairs={{0,1},{1,2},{2,3},{3,0},{4,5},{5,6},{6,7},{7,4},{8,9},{9,10},{10,1... | collective-permute-start | bytes 208904 | tf_op jit(solution)/shard_map/ppermute | solution.py:420
  98.7 1.2 collective-permute-start.7

commit v9 on v8

--- a/solution.py
+++ b/solution.py
@@ -26,7 +26,7 @@
 LAG_TOP = 102
 LAG_PAD = 4
 BINS_STEP = 4
-PACK_ROWS = 64
+PACK_ROWS = 256
 PACK_OUT = 4
 PACK_VMEM = 63 * 1024 * 1024
 BETA = 24.0
@@ -163,10 +163,8 @@
     offset = owner - CLASSES * jnp.floor(owner * (1.0 / CLASSES))
     member = one_hot_rows(head[4:5, :], BIN_DEV) * (live / (1.0 + offset))
     rows = [member * taps[k : k + 1, :] for k in range(TAPS)]
-    high = [row.astype(BF16) for row in rows]
-    low = [(row - top.astype(F32)).astype(BF16) for row, top in zip(rows, high)]
-    slots = y_ref[...]
-    sum_ref[...] = dot(jnp.concatenate(high, axis=0), slots, NN) + dot(jnp.concatenate(low, axis=0), slots, NN)
+    rows = jnp.concatenate([row.astype(BF16) for row in rows], axis=0)
+    sum_ref[...] = dot(rows, y_ref[...], NN)
     total = jnp.zeros((BIN_DEV, WIDE), F32)
     for k in range(TAPS):
         total = total + pltpu.roll(sum_ref[k * BIN_DEV : (k + 1) * BIN_DEV, :], (TAPS // 2 - 1 - k) % WIDE, 1)
@@ -257,13 +255,15 @@
     energy_ref[...] = jnp.broadcast_to(jnp.concatenate(energies, axis=1), (8, SLOTS))
 
 
-def corr_kernel(first, p0_ref, p1_ref, p2_ref, p3_ref, st_ref, energy_ref, side_ref, pilot_ref, grad_ref, lag_ref, wide_ref):
+def corr_kernel(first, p0_ref, p1_ref, p2_ref, p3_ref, st_ref, energy_ref, side_ref, *refs):
+    grad_ref, lag_ref, wide_ref = refs[-3:]
     total = (p0_ref[...].astype(F32) + p2_ref[...].astype(F32)) + (
         p1_ref[...].astype(F32) + p3_ref[...].astype(F32)
     )
     mass = (total[:, NS : NS + 1] + total[:, NS + 1 : NS + 2]) + total[:, NS + 2 : NS + 3]
     pilot = (total[:, :NS] * lax.rsqrt(mass + 1.0)).astype(BF16)
-    pilot_ref[...] = pilot
+    if not first:
+        refs[0][...] = pilot
     wide = pilot.astype(F32)
     wide_ref[...] = pltpu.roll(jnp.concatenate([wide, jnp.zeros((BIN_DEV, LANES), F32)], axis=1), LAG_PAD, 1)
     pilot_scale = lax.rsqrt(jnp.sum(wide * wide, axis=1, keepdims=True) + EPS)
@@ -293,16 +293,18 @@
     )
     misfit = -delay * live
     grad_ref[...] = jnp.zeros_like(grad_ref)
-    for at, out, rows in ((2, 0, 8), (0, 8, 2)):
-        low = one_hot_half(head[at + 1 : at + 2, :], 128)
-        high = one_hot_rows(head[at : at + 1, :], 8)
-        values = high * misfit
-        if first:
-            values = jnp.concatenate([values, high * live], axis=0)
-        sums = joined(dot(parts_of(values), low, NT))
-        grad_ref[out : out + rows, :] = sums[0:rows, :]
-        if first:
-            grad_ref[16 + out : 16 + out + rows, :] = sums[8 : 8 + rows, :]
+    low = jnp.concatenate([one_hot_half(head[at + 1 : at + 2, :], 128) for at in (2, 0)], axis=0)
+    high = jnp.concatenate([one_hot_rows(head[at : at + 1, :], 8) for at in (2, 0)], axis=0)
+    left = parts_of(high * misfit)
+    if first:
+        left = jnp.concatenate([left, (high * live).astype(BF16)], axis=0)
+    sums = dot(left, low, NT)
+    delays = joined(sums[0:48, :])
+    grad_ref[0:8, :] = delays[0:8, 0:128]
+    grad_ref[8:10, :] = delays[8:10, 128:256]
+    if first:
+        grad_ref[16:24, :] = sums[48:56, 0:128]
+        grad_ref[24:26, :] = sums[56:58, 128:256]
 
 
 def spread_kernel(own_ref, other_ref, out_ref, rows_ref):
@@ -397,7 +399,7 @@
 
 
 def correlate(first, parts, shifted, energy, side):
-    out = (shape((BIN_DEV, NS), BF16), shape((32 if first else 16, LANES), F32))
+    out = (shape((32, LANES), F32),) if first else (shape((BIN_DEV, NS), BF16), shape((16, LANES), F32))
     scratch = [pltpu.VMEM((BIN_DEV * LROWS, NS), BF16), pltpu.VMEM((BIN_DEV, WIDE), F32)]
     kernel = functools.partial(corr_kernel, first)
     return call(kernel, out, (0,) * 7, scratch, "correlate", 4 * 10**9, 10**7, *parts, shifted, energy, side)
@@ -439,7 +441,7 @@
     part, side, rows, damps = stack_first(damps, slots)
     parts = exchange(part)
     shifted, energy, turned = shift_first(rows, side)
-    pilot, sums = correlate(True, parts, shifted, energy, side)
+    (sums,) = correlate(True, parts, shifted, energy, side)
     sums = sum_copies(sums)
     part, side, known = stack_next(damps, rows, side, sums)
     parts = exchange(part)

time: 118 us -> 116 us (0.983)
  Pallas kernels: 30.1 us -> 28 us
    pallas_call x9, Pallas kernels: 25.6 us -> 23.8 us  [call(): pl.pallas_call(kernel, out_shape=out, in_specs=[SMEM if space else VMEM f...]
where the time goes in v9:
time: 116 us
  blocking collectives  36.4 us (31%)
  waiting for transfers between devices  33.4 us (29%)
  Pallas kernels  28 us (24%)
  starting transfers between devices  17 us (15%)
    all_to_all x2, blocking collectives, sum_copies(): lax.all_to_all(copies, ('y', 'x', 'off'), split_axis=0, concat_axis=0, ti...  36.4 us
    all_to_all x1, waiting for transfers between devices, on_device(): lax.all_to_all(outgoing, AXES, split_axis=0, concat_axis=0, tiled=True)  30.8 us
    pallas_call x9, Pallas kernels, call(): pl.pallas_call(kernel, out_shape=out, in_specs=[SMEM if space else VMEM f...  23.8 us
    all_to_all x1, starting transfers between devices, on_device(): lax.all_to_all(outgoing, AXES, split_axis=0, concat_axis=0, tiled=True)  11.2 us
    ppermute x6, starting transfers between devices, exchange(): return (part, *[lax.ppermute(part, 'off', off_perm(d)) for d in (1, 2, 3)])  5.75 us
    pallas_call x1, Pallas kernels, pack(): pl.pallas_call(pack_kernel, out_shape=shape((DEVICES, TRACE_LIMIT, WIDE),...  4.15 us
    ppermute x2, waiting for transfers between devices, sum_copies(): other = lax.ppermute(value, 'core', [(0, 1), (1, 0)])  2.34 us
  transfers between devices with their start and end apart: 9, of which 4 were waited for; matrix products, arithmetic and copies ran while one was open for 0% of the time, Pallas kernels for 10%

profile of v9, /device:TPU:0, one launch (start us, length us, event | category | flops | bytes accessed | tf_op | source)
XLA Modules:
  0.0 116.0 jit_solution(17127115968637519834)
XLA Ops:
  0.6 4.2 %pack.1 = bf16[128,4,2176]{2,1,0:T(4,128)(2,1)} custom-call(s32[1,256]{1,0:T(1,128)} %bitcast.8, s32[1,256]{1,0:T(1,128)} %bitcast.9, s32[1,256]{1,0:T(1,128)} %bitcast.10, s32[1,256]{1,0:T(1,128)} %bitcast.11, s32[1,256]{1,0:T(1,128)} %bitcast.12, s32[1,256]{1,0:T(1,128)} %bitcast.13, bf16[256,2048]{1,0:T(8,128)(2,1)} %refs_6_.1), custom_call_target="tpu_custom_call" | custom-call | tf_op jit(solution)/shard_map/pack/pallas_call | solution.py:355
  4.8 11.2 %all-to-all-start = ((bf16[128,4,2176]{2,1,0:T(4,128)(2,1)}), bf16[128,4,2176]{2,1,0:T(4,128)(2,1)S(1)}, u32[]{:S(2)}, u32[]{:S(2)}) async-start(bf16[128,4,2176]{2,1,0:T(4,128)(2,1)} %pack.1), calls=%async_computation | async-start | bytes 4456448 | tf_op jit(solution)/shard_map/all_to_all | solution.py:437
  16.0 0.2 fusion
  16.2 0.1 broadcast_in_dim.22
  16.3 0.1 broadcast_in_dim.23
  16.3 30.8 %all-to-all-done.slots_ref = bf16[128,4,2176]{2,1,0:T(4,128)(2,1)S(1)} async-done(((bf16[128,4,2176]{2,1,0:T(4,128)(2,1)}), bf16[128,4,2176]{2,1,0:T(4,128)(2,1)S(1)}, u32[]{:S(2)}, u32[]{:S(2)}) %all-to-all-start) | async-done | bytes 2228256 | tf_op jit(solution)/shard_map/all_to_all | solution.py:437
  47.2 0.1 broadcast_in_dim.24.damp_ref
  47.2 1.4 %stack_first.1 = (bf16[16,2176]{1,0:T(8,128)(2,1)S(1)}, f32[32,512]{1,0:T(8,128)S(1)}, bf16[512,2176]{1,0:T(8,128)(2,1)S(1)}, f32[16,128]{1,0:T(8,128)S(1)}) custom-call(f32[16,128]{1,0:T(8,128)S(1)} %broadcast_in_dim.24.damp_ref, bf16[128,4,2176]{2,1,0:T(4,128)(2,1)S(1)} %all-to-all-done.slots_ref), custom_call_target="tpu_custom_call" | custom-call | flops 3000000000 | bytes 10000000 | tf_op jit(solution)/shard_map/stack_first/pallas_call | solution.py:334
  48.6 1.2 %collective-permute-start.2 = (bf16[16,2176]{1,0:T(8,128)(2,1)S(1)}, bf16[16,2176]{1,0:T(8,128)(2,1)S(1)}, u32[]{:S(2)}, u32[]{:S(2)}) collective-permute-start(bf16[16,2176]{1,0:T(8,128)(2,1)S(1)} %get-tuple-element.22.p0_ref), channel_id=1, source_target_pairs={{0,3},{1,0},{2,1},{3,2},{4,7},{5,4},{6,5},{7,6},{8,11},{9,8},{10,9... | collective-permute-start | bytes 208904 | tf_op jit(solution)/shard_map/ppermute | solution.py:422
  49.8 1.8 %collective-permute-start.1 = (bf16[16,2176]{1,0:T(8,128)(2,1)S(1)}, bf16[16,2176]{1,0:T(8,128)(2,1)S(1)}, u32[]{:S(2)}, u32[]{:S(2)}) collective-permute-start(bf16[16,2176]{1,0:T(8,128)(2,1)S(1)} %get-tuple-element.22.p0_ref), channel_id=1, source_target_pairs={{0,2},{1,3},{2,0},{3,1},{4,6},{5,7},{6,4},{7,5},{8,10},{9,11},{10,... | collective-permute-start | bytes 208904 | tf_op jit(solution)/shard_map/ppermute | solution.py:422
  51.6 6.0 %shift_first.1 = (bf16[2048,512]{1,0:T(8,128)(2,1)S(1)}, f32[8,512]{1,0:T(8,128)S(1)}, f32[4,2064,128]{2,1,0:T(8,128)S(1)}) custom-call(bf16[512,2176]{1,0:T(8,128)(2,1)S(1)} %get-tuple-element.20.y_ref, f32[32,512]{1,0:T(8,128)S(1)} %get-tuple-element.21.side_ref.head_ref), custom_call_target="tpu_custom_call" | custom-call | flops 6000000000 | bytes 20000000 | tf_op jit(solution)/shard_map/shift_first/pallas_call | solution.py:334
  57.7 4.2 %correlate.2.own_ref = f32[32,128]{1,0:T(8,128)S(1)} custom-call(bf16[16,2176]{1,0:T(8,128)(2,1)S(1)} %get-tuple-element.22.p0_ref, bf16[16,2176]{1,0:T(8,128)(2,1)S(1)} %collective-permute-done.p1_ref, bf16[16,2176]{1,0:T(8,128)(2,1)S(1)} %collective-permute-done.1.p2_ref, bf16[16,2176]{1,0:T(8,128)(2,1)S(1)} %collective-permute-done.2.p3_ref, ...), custom_call_target="tpu_custom_call" | custom-call | flops 4000000000 | bytes 10000000 | tf_op jit(solution)/shard_map/correlate/pallas_call | solution.py:334
  61.9 0.1 collective-permute-start.3
  62.0 1.2 %collective-permute-done.3.other_ref = f32[32,128]{1,0:T(8,128)S(1)} collective-permute-done((f32[32,128]{1,0:T(8,128)S(1)}, f32[32,128]{1,0:T(8,128)S(1)}, u32[]{:S(2)}, u32[]{:S(2)}) %collective-permute-start.3) | collective-permute-done | bytes 16416 | tf_op jit(solution)/shard_map/ppermute | solution.py:413
  63.2 19.0 %all_to_all.15.sums_ref = bf16[64,24,128]{2,1,0:T(8,128)(2,1)S(1)} all-to-all(bf16[64,24,128]{2,1,0:T(8,128)(2,1)S(1)} %spread.2), channel_id=1, replica_groups=mesh['y'=4,'x'=4,'core'=2,'off'=4] {'y','x','off'}, dimensions={0} | all-to-all | bytes 786432 | tf_op jit(solution)/shard_map/all_to_all | solution.py:418
  82.2 1.4 %stack_next.1 = (bf16[16,2176]{1,0:T(8,128)(2,1)S(1)}, f32[32,512]{1,0:T(8,128)S(1)}, f32[32,128]{1,0:T(8,128)S(1)}) custom-call(f32[16,128]{1,0:T(8,128)S(1)} %get-tuple-element.19.damp_ref, bf16[512,2176]{1,0:T(8,128)(2,1)S(1)} %get-tuple-element.20.y_ref, f32[32,512]{1,0:T(8,128)S(1)} %get-tuple-element.21.side_ref.head_ref, ...), custom_call_target="tpu_custom_call" | custom-call | flops 3000000000 | bytes 10000000 | tf_op jit(solution)/shard_map/stack_next/pallas_call | solution.py:334
  83.5 0.7 collective-permute-start.6
  84.2 2.1 %collective-permute-start.5 = (bf16[16,2176]{1,0:T(8,128)(2,1)S(1)}, bf16[16,2176]{1,0:T(8,128)(2,1)S(1)}, u32[]{:S(2)}, u32[]{:S(2)}) collective-permute-start(bf16[16,2176]{1,0:T(8,128)(2,1)S(1)} %get-tuple-element.26.p0_ref), channel_id=1, source_target_pairs={{0,2},{1,3},{2,0},{3,1},{4,6},{5,7},{6,4},{7,5},{8,10},{9,11},{10,... | collective-permute-start | bytes 208904 | tf_op jit(solution)/shard_map/ppermute | solution.py:422
  86.3 5.2 %shift_next.1 = (bf16[2048,512]{1,0:T(8,128)(2,1)S(1)}, f32[8,512]{1,0:T(8,128)S(1)}) custom-call(f32[4,2064,128]{2,1,0:T(8,128)S(1)} %get-tuple-element.27.xt_ref, f32[32,512]{1,0:T(8,128)S(1)} %get-tuple-element.28.side_ref), custom_call_target="tpu_custom_call" | custom-call | flops 6000000000 | bytes 20000000 | tf_op jit(solution)/shard_map/shift_next/pallas_call | solution.py:334
  91.6 0.3 collective-permute-done.4.p1_ref
  91.8 4.9 %correlate.3 = (bf16[16,2048]{1,0:T(8,128)(2,1)}, f32[16,128]{1,0:T(8,128)S(1)}) custom-call(bf16[16,2176]{1,0:T(8,128)(2,1)S(1)} %get-tuple-element.26.p0_ref, bf16[16,2176]{1,0:T(8,128)(2,1)S(1)} %collective-permute-done.4.p1_ref, bf16[16,2176]{1,0:T(8,128)(2,1)S(1)} %collective-permute-done.5.p2_ref, bf16[16,2176]{1,0:T(8,128)(2,1)S(1)} %collective-permute-done.6.p3_ref, ...), custom_call_target="tpu_custom_call" | custom-call | flops 4000000000 | bytes 10000000 | tf_op jit(solution)/shard_map/correlate/pallas_call | solution.py:334
  96.7 1.2 %collective-permute-done.7.other_ref = f32[16,128]{1,0:T(8,128)S(1)} collective-permute-done((f32[16,128]{1,0:T(8,128)S(1)}, f32[16,128]{1,0:T(8,128)S(1)}, u32[]{:S(2)}, u32[]{:S(2)}) %collective-permute-start.7) | collective-permute-done | bytes 8224 | tf_op jit(solution)/shard_map/ppermute | solution.py:413
  97.9 17.5 %all_to_all.16.sums_ref = bf16[64,16,128]{2,1,0:T(8,128)(2,1)S(1)} all-to-all(bf16[64,16,128]{2,1,0:T(8,128)(2,1)S(1)} %spread.3), channel_id=1, replica_groups=mesh['y'=4,'x'=4,'core'=2,'off'=4] {'y','x','off'}, dimensions={0} | all-to-all | bytes 524288 | tf_op jit(solution)/shard_map/all_to_all | solution.py:418
  115.4 0.7 finish.1
  (14 shorter events, 0.1 us)
Async XLA Ops:
  4.8 11.2 %copy-start = (f32[8]{0:T(128)S(1)}, f32[8]{0:T(128)}, u32[]{:S(2)}) copy-start(f32[8]{0:T(128)} %param.16) | copy-start | bytes 100
  4.8 11.2 %copy-start.1 = (s32[2]{0:T(128)S(1)}, s32[2]{0:T(128)}, u32[]{:S(2)}) copy-start(s32[2]{0:T(128)} %param.17) | copy-start | bytes 28
  4.8 42.4 %all-to-all-start = ((bf16[128,4,2176]{2,1,0:T(4,128)(2,1)}), bf16[128,4,2176]{2,1,0:T(4,128)(2,1)S(1)}, u32[]{:S(2)}, u32[]{:S(2)}) async-start(bf16[128,4,2176]{2,1,0:T(4,128)(2,1)} %pack.1), calls=%async_computation | async-start | bytes 4456448 | tf_op jit(solution)/shard_map/all_to_all | solution.py:437
  48.6 9.0 %collective-permute-start.2 = (bf16[16,2176]{1,0:T(8,128)(2,1)S(1)}, bf16[16,2176]{1,0:T(8,128)(2,1)S(1)}, u32[]{:S(2)}, u32[]{:S(2)}) collective-permute-start(bf16[16,2176]{1,0:T(8,128)(2,1)S(1)} %get-tuple-element.22.p0_ref), channel_id=1, source_target_pairs={{0,3},{1,0},{2,1},{3,2},{4,7},{5,4},{6,5},{7,6},{8,11},{9,8},{10,9... | collective-permute-start | bytes 208904 | tf_op jit(solution)/shard_map/ppermute | solution.py:422
  49.8 7.8 %collective-permute-start.1 = (bf16[16,2176]{1,0:T(8,128)(2,1)S(1)}, bf16[16,2176]{1,0:T(8,128)(2,1)S(1)}, u32[]{:S(2)}, u32[]{:S(2)}) collective-permute-start(bf16[16,2176]{1,0:T(8,128)(2,1)S(1)} %get-tuple-element.22.p0_ref), channel_id=1, source_target_pairs={{0,2},{1,3},{2,0},{3,1},{4,6},{5,7},{6,4},{7,5},{8,10},{9,11},{10,... | collective-permute-start | bytes 208904 | tf_op jit(solution)/shard_map/ppermute | solution.py:422
  51.6 6.0 %collective-permute-start = (bf16[16,2176]{1,0:T(8,128)(2,1)S(1)}, bf16[16,2176]{1,0:T(8,128)(2,1)S(1)}, u32[]{:S(2)}, u32[]{:S(2)}) collective-permute-start(bf16[16,2176]{1,0:T(8,128)(2,1)S(1)} %get-tuple-element.22.p0_ref), channel_id=1, source_target_pairs={{0,1},{1,2},{2,3},{3,0},{4,5},{5,6},{6,7},{7,4},{8,9},{9,10},{10,1... | collective-permute-start | bytes 208904 | tf_op jit(solution)/shard_map/ppermute | solution.py:422
  61.9 1.3 %collective-permute-start.3 = (f32[32,128]{1,0:T(8,128)S(1)}, f32[32,128]{1,0:T(8,128)S(1)}, u32[]{:S(2)}, u32[]{:S(2)}) collective-permute-start(f32[32,128]{1,0:T(8,128)S(1)} %correlate.2.own_ref), channel_id=1, source_target_pairs={{0,4},{4,0},{1,5},{5,1},{2,6},{6,2},{3,7},{7,3},{8,12},{12,8},{9,1... | collective-permute-start | bytes 49160 | tf_op jit(solution)/shard_map/ppermute | solution.py:413
  83.5 8.0 %collective-permute-start.6 = (bf16[16,2176]{1,0:T(8,128)(2,1)S(1)}, bf16[16,2176]{1,0:T(8,128)(2,1)S(1)}, u32[]{:S(2)}, u32[]{:S(2)}) collective-permute-start(bf16[16,2176]{1,0:T(8,128)(2,1)S(1)} %get-tuple-element.26.p0_ref), channel_id=1, source_target_pairs={{0,3},{1,0},{2,1},{3,2},{4,7},{5,4},{6,5},{7,6},{8,11},{9,8},{10,9... | collective-permute-start | bytes 208904 | tf_op jit(solution)/shard_map/ppermute | solution.py:422
  84.2 7.3 %collective-permute-start.5 = (bf16[16,2176]{1,0:T(8,128)(2,1)S(1)}, bf16[16,2176]{1,0:T(8,128)(2,1)S(1)}, u32[]{:S(2)}, u32[]{:S(2)}) collective-permute-start(bf16[16,2176]{1,0:T(8,128)(2,1)S(1)} %get-tuple-element.26.p0_ref), channel_id=1, source_target_pairs={{0,2},{1,3},{2,0},{3,1},{4,6},{5,7},{6,4},{7,5},{8,10},{9,11},{10,... | collective-permute-start | bytes 208904 | tf_op jit(solution)/shard_map/ppermute | solution.py:422
  86.3 5.5 %collective-permute-start.4 = (bf16[16,2176]{1,0:T(8,128)(2,1)S(1)}, bf16[16,2176]{1,0:T(8,128)(2,1)S(1)}, u32[]{:S(2)}, u32[]{:S(2)}) collective-permute-start(bf16[16,2176]{1,0:T(8,128)(2,1)S(1)} %get-tuple-element.26.p0_ref), channel_id=1, source_target_pairs={{0,1},{1,2},{2,3},{3,0},{4,5},{5,6},{6,7},{7,4},{8,9},{9,10},{10,1... | collective-permute-start | bytes 208904 | tf_op jit(solution)/shard_map/ppermute | solution.py:422
  96.7 1.2 %collective-permute-start.7 = (f32[16,128]{1,0:T(8,128)S(1)}, f32[16,128]{1,0:T(8,128)S(1)}, u32[]{:S(2)}, u32[]{:S(2)}) collective-permute-start(f32[16,128]{1,0:T(8,128)S(1)} %get-tuple-element.31.own_ref), channel_id=1, source_target_pairs={{0,4},{4,0},{1,5},{5,1},{2,6},{6,2},{3,7},{7,3},{8,12},{12,8},{9,1... | collective-permute-start | bytes 24584 | tf_op jit(solution)/shard_map/ppermute | solution.py:413

commit v10 on v9

--- a/solution.py
+++ b/solution.py
@@ -256,14 +256,17 @@
 
 
 def corr_kernel(first, p0_ref, p1_ref, p2_ref, p3_ref, st_ref, energy_ref, side_ref, *refs):
-    grad_ref, lag_ref, wide_ref = refs[-3:]
+    grad_ref, lag_ref, wide_ref = refs[:3] if first else refs[1:4]
     total = (p0_ref[...].astype(F32) + p2_ref[...].astype(F32)) + (
         p1_ref[...].astype(F32) + p3_ref[...].astype(F32)
     )
     mass = (total[:, NS : NS + 1] + total[:, NS + 1 : NS + 2]) + total[:, NS + 2 : NS + 3]
     pilot = (total[:, :NS] * lax.rsqrt(mass + 1.0)).astype(BF16)
     if not first:
-        refs[0][...] = pilot
+        pilot_ref, pilot_sem = refs[4:]
+        pilot_ref[...] = pilot
+        pilot_copy = pltpu.make_async_copy(pilot_ref, refs[0], pilot_sem)
+        pilot_copy.start()
     wide = pilot.astype(F32)
     wide_ref[...] = pltpu.roll(jnp.concatenate([wide, jnp.zeros((BIN_DEV, LANES), F32)], axis=1), LAG_PAD, 1)
     pilot_scale = lax.rsqrt(jnp.sum(wide * wide, axis=1, keepdims=True) + EPS)
@@ -305,6 +308,8 @@
     if first:
         grad_ref[16:24, :] = sums[48:56, 0:128]
         grad_ref[24:26, :] = sums[56:58, 128:256]
+    else:
+        pilot_copy.wait()
 
 
 def spread_kernel(own_ref, other_ref, out_ref, rows_ref):
@@ -399,10 +404,20 @@
 
 
 def correlate(first, parts, shifted, energy, side):
-    out = (shape((32, LANES), F32),) if first else (shape((BIN_DEV, NS), BF16), shape((16, LANES), F32))
+    sums = shape((32 if first else 16, LANES), F32)
     scratch = [pltpu.VMEM((BIN_DEV * LROWS, NS), BF16), pltpu.VMEM((BIN_DEV, WIDE), F32)]
-    kernel = functools.partial(corr_kernel, first)
-    return call(kernel, out, (0,) * 7, scratch, "correlate", 4 * 10**9, 10**7, *parts, shifted, energy, side)
+    if not first:
+        scratch += [pltpu.VMEM((BIN_DEV, NS), BF16), pltpu.SemaphoreType.DMA]
+    return pl.pallas_call(
+        functools.partial(corr_kernel, first),
+        out_shape=(sums,) if first else (shape((BIN_DEV, NS), BF16), sums),
+        in_specs=[VMEM] * 7,
+        out_specs=(VMEM,) if first else (HBM, VMEM),
+        scratch_shapes=scratch,
+        compiler_params=PARAMS,
+        cost_estimate=pl.CostEstimate(flops=4 * 10**9, bytes_accessed=10**7, transcendentals=0),
+        name="correlate",
+    )(*parts, shifted, energy, side)
 
 
 def off_perm(d):

time: 116 us -> 116 us (level)
    pallas_call x9 -> x7, Pallas kernels: 23.8 us -> 14.7 us  [call(): pl.pallas_call(kernel, out_shape=out, in_specs=[SMEM if space else VMEM f...]
    pallas_call x0 -> x2, Pallas kernels: none -> 8.61 us  [correlate(): pl.pallas_call(functools.partial(corr_kernel, first), out_shape=(sums,) i...]
where the time goes in v10:
time: 116 us
  blocking collectives  36.4 us (31%)
  waiting for transfers between devices  33.4 us (29%)
  Pallas kernels  27.5 us (24%)
  starting transfers between devices  17.1 us (15%)
    all_to_all x2, blocking collectives, sum_copies(): lax.all_to_all(copies, ('y', 'x', 'off'), split_axis=0, concat_axis=0, ti...  36.4 us
    all_to_all x1, waiting for transfers between devices, on_device(): lax.all_to_all(outgoing, AXES, split_axis=0, concat_axis=0, tiled=True)  30.8 us
    pallas_call x7, Pallas kernels, call(): pl.pallas_call(kernel, out_shape=out, in_specs=[SMEM if space else VMEM f...  14.7 us
    all_to_all x1, starting transfers between devices, on_device(): lax.all_to_all(outgoing, AXES, split_axis=0, concat_axis=0, tiled=True)  11.2 us
    pallas_call x2, Pallas kernels, correlate(): pl.pallas_call(functools.partial(corr_kernel, first), out_shape=(sums,) i...  8.61 us
    ppermute x6, starting transfers between devices, exchange(): return (part, *[lax.ppermute(part, 'off', off_perm(d)) for d in (1, 2, 3)])  5.75 us
    pallas_call x1, Pallas kernels, pack(): pl.pallas_call(pack_kernel, out_shape=shape((DEVICES, TRACE_LIMIT, WIDE),...  4.15 us
    ppermute x2, waiting for transfers between devices, sum_copies(): other = lax.ppermute(value, 'core', [(0, 1), (1, 0)])  2.33 us
  transfers between devices with their start and end apart: 9, of which 4 were waited for; matrix products, arithmetic and copies ran while one was open for 0% of the time, Pallas kernels for 10%

profile of v10, /device:TPU:0, one launch (start us, length us, event | category | flops | bytes accessed | tf_op | source)
XLA Modules:
  0.0 115.6 jit_solution(8703901467017163409)
XLA Ops:
  0.6 4.2 %pack.1 = bf16[128,4,2176]{2,1,0:T(4,128)(2,1)} custom-call(s32[1,256]{1,0:T(1,128)} %bitcast.8, s32[1,256]{1,0:T(1,128)} %bitcast.9, s32[1,256]{1,0:T(1,128)} %bitcast.10, s32[1,256]{1,0:T(1,128)} %bitcast.11, s32[1,256]{1,0:T(1,128)} %bitcast.12, s32[1,256]{1,0:T(1,128)} %bitcast.13, bf16[256,2048]{1,0:T(8,128)(2,1)} %refs_6_.1), custom_call_target="tpu_custom_call" | custom-call | tf_op jit(solution)/shard_map/pack/pallas_call | solution.py:360
  4.8 11.2 %all-to-all-start = ((bf16[128,4,2176]{2,1,0:T(4,128)(2,1)}), bf16[128,4,2176]{2,1,0:T(4,128)(2,1)S(1)}, u32[]{:S(2)}, u32[]{:S(2)}) async-start(bf16[128,4,2176]{2,1,0:T(4,128)(2,1)} %pack.1), calls=%async_computation | async-start | bytes 4456448 | tf_op jit(solution)/shard_map/all_to_all | solution.py:452
  16.0 0.2 fusion
  16.2 0.1 broadcast_in_dim.22
  16.3 0.1 broadcast_in_dim.23
  16.3 30.8 %all-to-all-done.slots_ref = bf16[128,4,2176]{2,1,0:T(4,128)(2,1)S(1)} async-done(((bf16[128,4,2176]{2,1,0:T(4,128)(2,1)}), bf16[128,4,2176]{2,1,0:T(4,128)(2,1)S(1)}, u32[]{:S(2)}, u32[]{:S(2)}) %all-to-all-start) | async-done | bytes 2228256 | tf_op jit(solution)/shard_map/all_to_all | solution.py:452
  47.2 1.4 %stack_first.1 = (bf16[16,2176]{1,0:T(8,128)(2,1)S(1)}, f32[32,512]{1,0:T(8,128)S(1)}, bf16[512,2176]{1,0:T(8,128)(2,1)S(1)}, f32[16,128]{1,0:T(8,128)S(1)}) custom-call(f32[16,128]{1,0:T(8,128)S(1)} %broadcast_in_dim.24.damp_ref, bf16[128,4,2176]{2,1,0:T(4,128)(2,1)S(1)} %all-to-all-done.slots_ref), custom_call_target="tpu_custom_call" | custom-call | flops 3000000000 | bytes 10000000 | tf_op jit(solution)/shard_map/stack_first/pallas_call | solution.py:339
  48.6 1.2 %collective-permute-start.2 = (bf16[16,2176]{1,0:T(8,128)(2,1)S(1)}, bf16[16,2176]{1,0:T(8,128)(2,1)S(1)}, u32[]{:S(2)}, u32[]{:S(2)}) collective-permute-start(bf16[16,2176]{1,0:T(8,128)(2,1)S(1)} %get-tuple-element.22.p0_ref), channel_id=1, source_target_pairs={{0,3},{1,0},{2,1},{3,2},{4,7},{5,4},{6,5},{7,6},{8,11},{9,8},{10,9... | collective-permute-start | bytes 208904 | tf_op jit(solution)/shard_map/ppermute | solution.py:437
  49.8 1.8 %collective-permute-start.1 = (bf16[16,2176]{1,0:T(8,128)(2,1)S(1)}, bf16[16,2176]{1,0:T(8,128)(2,1)S(1)}, u32[]{:S(2)}, u32[]{:S(2)}) collective-permute-start(bf16[16,2176]{1,0:T(8,128)(2,1)S(1)} %get-tuple-element.22.p0_ref), channel_id=1, source_target_pairs={{0,2},{1,3},{2,0},{3,1},{4,6},{5,7},{6,4},{7,5},{8,10},{9,11},{10,... | collective-permute-start | bytes 208904 | tf_op jit(solution)/shard_map/ppermute | solution.py:437
  51.6 6.0 %shift_first.1 = (bf16[2048,512]{1,0:T(8,128)(2,1)S(1)}, f32[8,512]{1,0:T(8,128)S(1)}, f32[4,2064,128]{2,1,0:T(8,128)S(1)}) custom-call(bf16[512,2176]{1,0:T(8,128)(2,1)S(1)} %get-tuple-element.20.y_ref, f32[32,512]{1,0:T(8,128)S(1)} %get-tuple-element.21.side_ref.head_ref), custom_call_target="tpu_custom_call" | custom-call | flops 6000000000 | bytes 20000000 | tf_op jit(solution)/shard_map/shift_first/pallas_call | solution.py:339
  57.7 4.2 %correlate.2.own_ref = f32[32,128]{1,0:T(8,128)S(1)} custom-call(bf16[16,2176]{1,0:T(8,128)(2,1)S(1)} %get-tuple-element.22.p0_ref, bf16[16,2176]{1,0:T(8,128)(2,1)S(1)} %collective-permute-done.p1_ref, bf16[16,2176]{1,0:T(8,128)(2,1)S(1)} %collective-permute-done.1.p2_ref, bf16[16,2176]{1,0:T(8,128)(2,1)S(1)} %collective-permute-done.2.p3_ref, ...), custom_call_target="tpu_custom_call" | custom-call | flops 4000000000 | bytes 10000000 | tf_op jit(solution)/shard_map/correlate/pallas_call | solution.py:411
  61.9 0.1 collective-permute-start.3
  62.0 1.2 %collective-permute-done.3.other_ref = f32[32,128]{1,0:T(8,128)S(1)} collective-permute-done((f32[32,128]{1,0:T(8,128)S(1)}, f32[32,128]{1,0:T(8,128)S(1)}, u32[]{:S(2)}, u32[]{:S(2)}) %collective-permute-start.3) | collective-permute-done | bytes 16416 | tf_op jit(solution)/shard_map/ppermute | solution.py:428
  63.2 19.0 %all_to_all.15.sums_ref = bf16[64,24,128]{2,1,0:T(8,128)(2,1)S(1)} all-to-all(bf16[64,24,128]{2,1,0:T(8,128)(2,1)S(1)} %spread.2), channel_id=1, replica_groups=mesh['y'=4,'x'=4,'core'=2,'off'=4] {'y','x','off'}, dimensions={0} | all-to-all | bytes 786432 | tf_op jit(solution)/shard_map/all_to_all | solution.py:433
  82.2 1.4 %stack_next.1 = (bf16[16,2176]{1,0:T(8,128)(2,1)S(1)}, f32[32,512]{1,0:T(8,128)S(1)}, f32[32,128]{1,0:T(8,128)S(1)}) custom-call(f32[16,128]{1,0:T(8,128)S(1)} %get-tuple-element.19.damp_ref, bf16[512,2176]{1,0:T(8,128)(2,1)S(1)} %get-tuple-element.20.y_ref, f32[32,512]{1,0:T(8,128)S(1)} %get-tuple-element.21.side_ref.head_ref, ...), custom_call_target="tpu_custom_call" | custom-call | flops 3000000000 | bytes 10000000 | tf_op jit(solution)/shard_map/stack_next/pallas_call | solution.py:339
  83.5 0.7 collective-permute-start.6
  84.2 2.1 %collective-permute-start.5 = (bf16[16,2176]{1,0:T(8,128)(2,1)S(1)}, bf16[16,2176]{1,0:T(8,128)(2,1)S(1)}, u32[]{:S(2)}, u32[]{:S(2)}) collective-permute-start(bf16[16,2176]{1,0:T(8,128)(2,1)S(1)} %get-tuple-element.26.p0_ref), channel_id=1, source_target_pairs={{0,2},{1,3},{2,0},{3,1},{4,6},{5,7},{6,4},{7,5},{8,10},{9,11},{10,... | collective-permute-start | bytes 208904 | tf_op jit(solution)/shard_map/ppermute | solution.py:437
  86.3 5.2 %shift_next.1 = (bf16[2048,512]{1,0:T(8,128)(2,1)S(1)}, f32[8,512]{1,0:T(8,128)S(1)}) custom-call(f32[4,2064,128]{2,1,0:T(8,128)S(1)} %get-tuple-element.27.xt_ref, f32[32,512]{1,0:T(8,128)S(1)} %get-tuple-element.28.side_ref), custom_call_target="tpu_custom_call" | custom-call | flops 6000000000 | bytes 20000000 | tf_op jit(solution)/shard_map/shift_next/pallas_call | solution.py:339
  91.6 0.3 collective-permute-done.4.p1_ref
  91.8 4.4 %correlate.3 = (bf16[16,2048]{1,0:T(8,128)(2,1)}, f32[16,128]{1,0:T(8,128)S(1)}) custom-call(bf16[16,2176]{1,0:T(8,128)(2,1)S(1)} %get-tuple-element.26.p0_ref, bf16[16,2176]{1,0:T(8,128)(2,1)S(1)} %collective-permute-done.4.p1_ref, bf16[16,2176]{1,0:T(8,128)(2,1)S(1)} %collective-permute-done.5.p2_ref, bf16[16,2176]{1,0:T(8,128)(2,1)S(1)} %collective-permute-done.6.p3_ref, ...), custom_call_target="tpu_custom_call" | custom-call | flops 4000000000 | bytes 10000000 | tf_op jit(solution)/shard_map/correlate/pallas_call | solution.py:411
  96.2 0.1 collective-permute-start.7
  96.3 1.2 %collective-permute-done.7.other_ref = f32[16,128]{1,0:T(8,128)S(1)} collective-permute-done((f32[16,128]{1,0:T(8,128)S(1)}, f32[16,128]{1,0:T(8,128)S(1)}, u32[]{:S(2)}, u32[]{:S(2)}) %collective-permute-start.7) | collective-permute-done | bytes 8224 | tf_op jit(solution)/shard_map/ppermute | solution.py:428
  97.5 17.5 %all_to_all.16.sums_ref = bf16[64,16,128]{2,1,0:T(8,128)(2,1)S(1)} all-to-all(bf16[64,16,128]{2,1,0:T(8,128)(2,1)S(1)} %spread.3), channel_id=1, replica_groups=mesh['y'=4,'x'=4,'core'=2,'off'=4] {'y','x','off'}, dimensions={0} | all-to-all | bytes 524288 | tf_op jit(solution)/shard_map/all_to_all | solution.py:433
  115.0 0.7 finish.1
  (14 shorter events, 0.2 us)
Async XLA Ops:
  4.8 11.2 %copy-start = (f32[8]{0:T(128)S(1)}, f32[8]{0:T(128)}, u32[]{:S(2)}) copy-start(f32[8]{0:T(128)} %param.16) | copy-start | bytes 100
  4.8 11.2 %copy-start.1 = (s32[2]{0:T(128)S(1)}, s32[2]{0:T(128)}, u32[]{:S(2)}) copy-start(s32[2]{0:T(128)} %param.17) | copy-start | bytes 28
  4.8 42.4 %all-to-all-start = ((bf16[128,4,2176]{2,1,0:T(4,128)(2,1)}), bf16[128,4,2176]{2,1,0:T(4,128)(2,1)S(1)}, u32[]{:S(2)}, u32[]{:S(2)}) async-start(bf16[128,4,2176]{2,1,0:T(4,128)(2,1)} %pack.1), calls=%async_computation | async-start | bytes 4456448 | tf_op jit(solution)/shard_map/all_to_all | solution.py:452
  48.6 9.0 %collective-permute-start.2 = (bf16[16,2176]{1,0:T(8,128)(2,1)S(1)}, bf16[16,2176]{1,0:T(8,128)(2,1)S(1)}, u32[]{:S(2)}, u32[]{:S(2)}) collective-permute-start(bf16[16,2176]{1,0:T(8,128)(2,1)S(1)} %get-tuple-element.22.p0_ref), channel_id=1, source_target_pairs={{0,3},{1,0},{2,1},{3,2},{4,7},{5,4},{6,5},{7,6},{8,11},{9,8},{10,9... | collective-permute-start | bytes 208904 | tf_op jit(solution)/shard_map/ppermute | solution.py:437
  49.8 7.8 %collective-permute-start.1 = (bf16[16,2176]{1,0:T(8,128)(2,1)S(1)}, bf16[16,2176]{1,0:T(8,128)(2,1)S(1)}, u32[]{:S(2)}, u32[]{:S(2)}) collective-permute-start(bf16[16,2176]{1,0:T(8,128)(2,1)S(1)} %get-tuple-element.22.p0_ref), channel_id=1, source_target_pairs={{0,2},{1,3},{2,0},{3,1},{4,6},{5,7},{6,4},{7,5},{8,10},{9,11},{10,... | collective-permute-start | bytes 208904 | tf_op jit(solution)/shard_map/ppermute | solution.py:437
  51.6 6.0 %collective-permute-start = (bf16[16,2176]{1,0:T(8,128)(2,1)S(1)}, bf16[16,2176]{1,0:T(8,128)(2,1)S(1)}, u32[]{:S(2)}, u32[]{:S(2)}) collective-permute-start(bf16[16,2176]{1,0:T(8,128)(2,1)S(1)} %get-tuple-element.22.p0_ref), channel_id=1, source_target_pairs={{0,1},{1,2},{2,3},{3,0},{4,5},{5,6},{6,7},{7,4},{8,9},{9,10},{10,1... | collective-permute-start | bytes 208904 | tf_op jit(solution)/shard_map/ppermute | solution.py:437
  61.9 1.3 %collective-permute-start.3 = (f32[32,128]{1,0:T(8,128)S(1)}, f32[32,128]{1,0:T(8,128)S(1)}, u32[]{:S(2)}, u32[]{:S(2)}) collective-permute-start(f32[32,128]{1,0:T(8,128)S(1)} %correlate.2.own_ref), channel_id=1, source_target_pairs={{0,4},{4,0},{1,5},{5,1},{2,6},{6,2},{3,7},{7,3},{8,12},{12,8},{9,1... | collective-permute-start | bytes 49160 | tf_op jit(solution)/shard_map/ppermute | solution.py:428
  83.5 8.0 %collective-permute-start.6 = (bf16[16,2176]{1,0:T(8,128)(2,1)S(1)}, bf16[16,2176]{1,0:T(8,128)(2,1)S(1)}, u32[]{:S(2)}, u32[]{:S(2)}) collective-permute-start(bf16[16,2176]{1,0:T(8,128)(2,1)S(1)} %get-tuple-element.26.p0_ref), channel_id=1, source_target_pairs={{0,3},{1,0},{2,1},{3,2},{4,7},{5,4},{6,5},{7,6},{8,11},{9,8},{10,9... | collective-permute-start | bytes 208904 | tf_op jit(solution)/shard_map/ppermute | solution.py:437
  84.2 7.3 %collective-permute-start.5 = (bf16[16,2176]{1,0:T(8,128)(2,1)S(1)}, bf16[16,2176]{1,0:T(8,128)(2,1)S(1)}, u32[]{:S(2)}, u32[]{:S(2)}) collective-permute-start(bf16[16,2176]{1,0:T(8,128)(2,1)S(1)} %get-tuple-element.26.p0_ref), channel_id=1, source_target_pairs={{0,2},{1,3},{2,0},{3,1},{4,6},{5,7},{6,4},{7,5},{8,10},{9,11},{10,... | collective-permute-start | bytes 208904 | tf_op jit(solution)/shard_map/ppermute | solution.py:437
  86.3 5.5 %collective-permute-start.4 = (bf16[16,2176]{1,0:T(8,128)(2,1)S(1)}, bf16[16,2176]{1,0:T(8,128)(2,1)S(1)}, u32[]{:S(2)}, u32[]{:S(2)}) collective-permute-start(bf16[16,2176]{1,0:T(8,128)(2,1)S(1)} %get-tuple-element.26.p0_ref), channel_id=1, source_target_pairs={{0,1},{1,2},{2,3},{3,0},{4,5},{5,6},{6,7},{7,4},{8,9},{9,10},{10,1... | collective-permute-start | bytes 208904 | tf_op jit(solution)/shard_map/ppermute | solution.py:437
  96.2 1.3 %collective-permute-start.7 = (f32[16,128]{1,0:T(8,128)S(1)}, f32[16,128]{1,0:T(8,128)S(1)}, u32[]{:S(2)}, u32[]{:S(2)}) collective-permute-start(f32[16,128]{1,0:T(8,128)S(1)} %get-tuple-element.31.own_ref), channel_id=1, source_target_pairs={{0,4},{4,0},{1,5},{5,1},{2,6},{6,2},{3,7},{7,3},{8,12},{12,8},{9,1... | collective-permute-start | bytes 24584 | tf_op jit(solution)/shard_map/ppermute | solution.py:428

commit v11 on v10

--- a/solution.py
+++ b/solution.py
@@ -250,7 +250,7 @@
                 energy = energy + (totals[h] * totals[h] + totals[h + 1] * totals[h + 1])
             return energy
 
-        energy = lax.fori_loop(0, NS // chunk, body, jnp.zeros((8, LANES), F32), unroll=4)
+        energy = lax.fori_loop(0, NS // chunk, body, jnp.zeros((8, LANES), F32), unroll=8)
         energies.append(jnp.sum(energy, axis=0, keepdims=True))
     energy_ref[...] = jnp.broadcast_to(jnp.concatenate(energies, axis=1), (8, SLOTS))
 

time: 116 us -> 115 us (level)
  transfers between devices with their start and end apart: 9 -> 9, of which waited for: 4 -> 4; matrix products, arithmetic and copies ran while one was open for 0% -> 0% of each run, Pallas kernels for 10% -> 9%
where the time goes in v11:
time: 115 us
  blocking collectives  36.1 us (31%)
  waiting for transfers between devices  33.8 us (29%)
  Pallas kernels  26.8 us (23%)
  starting transfers between devices  17.1 us (15%)
    all_to_all x2, blocking collectives, sum_copies(): lax.all_to_all(copies, ('y', 'x', 'off'), split_axis=0, concat_axis=0, ti...  36.1 us
    all_to_all x1, waiting for transfers between devices, on_device(): lax.all_to_all(outgoing, AXES, split_axis=0, concat_axis=0, tiled=True)  30.8 us
    pallas_call x7, Pallas kernels, call(): pl.pallas_call(kernel, out_shape=out, in_specs=[SMEM if space else VMEM f...  14 us
    all_to_all x1, starting transfers between devices, on_device(): lax.all_to_all(outgoing, AXES, split_axis=0, concat_axis=0, tiled=True)  11.2 us
    pallas_call x2, Pallas kernels, correlate(): pl.pallas_call(functools.partial(corr_kernel, first), out_shape=(sums,) i...  8.61 us
    ppermute x6, starting transfers between devices, exchange(): return (part, *[lax.ppermute(part, 'off', off_perm(d)) for d in (1, 2, 3)])  5.75 us
    pallas_call x1, Pallas kernels, pack(): pl.pallas_call(pack_kernel, out_shape=shape((DEVICES, TRACE_LIMIT, WIDE),...  4.15 us
    ppermute x2, waiting for transfers between devices, sum_copies(): other = lax.ppermute(value, 'core', [(0, 1), (1, 0)])  2.33 us
  transfers between devices with their start and end apart: 9, of which 4 were waited for; matrix products, arithmetic and copies ran while one was open for 0% of the time, Pallas kernels for 9%

profile of v11, /device:TPU:0, one launch (start us, length us, event | category | flops | bytes accessed | tf_op | source)
XLA Modules:
  0.0 114.9 jit_solution(17529638770499204982)
XLA Ops:
  0.6 4.2 %pack.1 = bf16[128,4,2176]{2,1,0:T(4,128)(2,1)} custom-call(s32[1,256]{1,0:T(1,128)} %bitcast.8, s32[1,256]{1,0:T(1,128)} %bitcast.9, s32[1,256]{1,0:T(1,128)} %bitcast.10, s32[1,256]{1,0:T(1,128)} %bitcast.11, s32[1,256]{1,0:T(1,128)} %bitcast.12, s32[1,256]{1,0:T(1,128)} %bitcast.13, bf16[256,2048]{1,0:T(8,128)(2,1)} %refs_6_.1), custom_call_target="tpu_custom_call" | custom-call | tf_op jit(solution)/shard_map/pack/pallas_call | solution.py:360
  4.8 11.2 %all-to-all-start = ((bf16[128,4,2176]{2,1,0:T(4,128)(2,1)}), bf16[128,4,2176]{2,1,0:T(4,128)(2,1)S(1)}, u32[]{:S(2)}, u32[]{:S(2)}) async-start(bf16[128,4,2176]{2,1,0:T(4,128)(2,1)} %pack.1), calls=%async_computation | async-start | bytes 4456448 | tf_op jit(solution)/shard_map/all_to_all | solution.py:452
  16.0 0.2 fusion
  16.2 0.1 broadcast_in_dim.22
  16.3 0.1 broadcast_in_dim.23
  16.3 30.8 %all-to-all-done.slots_ref = bf16[128,4,2176]{2,1,0:T(4,128)(2,1)S(1)} async-done(((bf16[128,4,2176]{2,1,0:T(4,128)(2,1)}), bf16[128,4,2176]{2,1,0:T(4,128)(2,1)S(1)}, u32[]{:S(2)}, u32[]{:S(2)}) %all-to-all-start) | async-done | bytes 2228256 | tf_op jit(solution)/shard_map/all_to_all | solution.py:452
  47.2 1.4 %stack_first.1 = (bf16[16,2176]{1,0:T(8,128)(2,1)S(1)}, f32[32,512]{1,0:T(8,128)S(1)}, bf16[512,2176]{1,0:T(8,128)(2,1)S(1)}, f32[16,128]{1,0:T(8,128)S(1)}) custom-call(f32[16,128]{1,0:T(8,128)S(1)} %broadcast_in_dim.24.damp_ref, bf16[128,4,2176]{2,1,0:T(4,128)(2,1)S(1)} %all-to-all-done.slots_ref), custom_call_target="tpu_custom_call" | custom-call | flops 3000000000 | bytes 10000000 | tf_op jit(solution)/shard_map/stack_first/pallas_call | solution.py:339
  48.6 1.2 %collective-permute-start.2 = (bf16[16,2176]{1,0:T(8,128)(2,1)S(1)}, bf16[16,2176]{1,0:T(8,128)(2,1)S(1)}, u32[]{:S(2)}, u32[]{:S(2)}) collective-permute-start(bf16[16,2176]{1,0:T(8,128)(2,1)S(1)} %get-tuple-element.22.p0_ref), channel_id=1, source_target_pairs={{0,3},{1,0},{2,1},{3,2},{4,7},{5,4},{6,5},{7,6},{8,11},{9,8},{10,9... | collective-permute-start | bytes 208904 | tf_op jit(solution)/shard_map/ppermute | solution.py:437
  49.8 1.8 %collective-permute-start.1 = (bf16[16,2176]{1,0:T(8,128)(2,1)S(1)}, bf16[16,2176]{1,0:T(8,128)(2,1)S(1)}, u32[]{:S(2)}, u32[]{:S(2)}) collective-permute-start(bf16[16,2176]{1,0:T(8,128)(2,1)S(1)} %get-tuple-element.22.p0_ref), channel_id=1, source_target_pairs={{0,2},{1,3},{2,0},{3,1},{4,6},{5,7},{6,4},{7,5},{8,10},{9,11},{10,... | collective-permute-start | bytes 208904 | tf_op jit(solution)/shard_map/ppermute | solution.py:437
  51.6 5.7 %shift_first.1 = (bf16[2048,512]{1,0:T(8,128)(2,1)S(1)}, f32[8,512]{1,0:T(8,128)S(1)}, f32[4,2064,128]{2,1,0:T(8,128)S(1)}) custom-call(bf16[512,2176]{1,0:T(8,128)(2,1)S(1)} %get-tuple-element.20.y_ref, f32[32,512]{1,0:T(8,128)S(1)} %get-tuple-element.21.side_ref.head_ref), custom_call_target="tpu_custom_call" | custom-call | flops 6000000000 | bytes 20000000 | tf_op jit(solution)/shard_map/shift_first/pallas_call | solution.py:339
  57.3 4.2 %correlate.2.own_ref = f32[32,128]{1,0:T(8,128)S(1)} custom-call(bf16[16,2176]{1,0:T(8,128)(2,1)S(1)} %get-tuple-element.22.p0_ref, bf16[16,2176]{1,0:T(8,128)(2,1)S(1)} %collective-permute-done.p1_ref, bf16[16,2176]{1,0:T(8,128)(2,1)S(1)} %collective-permute-done.1.p2_ref, bf16[16,2176]{1,0:T(8,128)(2,1)S(1)} %collective-permute-done.2.p3_ref, ...), custom_call_target="tpu_custom_call" | custom-call | flops 4000000000 | bytes 10000000 | tf_op jit(solution)/shard_map/correlate/pallas_call | solution.py:411
  61.5 0.1 collective-permute-start.3
  61.6 1.2 %collective-permute-done.3.other_ref = f32[32,128]{1,0:T(8,128)S(1)} collective-permute-done((f32[32,128]{1,0:T(8,128)S(1)}, f32[32,128]{1,0:T(8,128)S(1)}, u32[]{:S(2)}, u32[]{:S(2)}) %collective-permute-start.3) | collective-permute-done | bytes 16416 | tf_op jit(solution)/shard_map/ppermute | solution.py:428
  62.8 19.0 %all_to_all.15.sums_ref = bf16[64,24,128]{2,1,0:T(8,128)(2,1)S(1)} all-to-all(bf16[64,24,128]{2,1,0:T(8,128)(2,1)S(1)} %spread.2), channel_id=1, replica_groups=mesh['y'=4,'x'=4,'core'=2,'off'=4] {'y','x','off'}, dimensions={0} | all-to-all | bytes 786432 | tf_op jit(solution)/shard_map/all_to_all | solution.py:433
  81.8 1.4 %stack_next.1 = (bf16[16,2176]{1,0:T(8,128)(2,1)S(1)}, f32[32,512]{1,0:T(8,128)S(1)}, f32[32,128]{1,0:T(8,128)S(1)}) custom-call(f32[16,128]{1,0:T(8,128)S(1)} %get-tuple-element.19.damp_ref, bf16[512,2176]{1,0:T(8,128)(2,1)S(1)} %get-tuple-element.20.y_ref, f32[32,512]{1,0:T(8,128)S(1)} %get-tuple-element.21.side_ref.head_ref, ...), custom_call_target="tpu_custom_call" | custom-call | flops 3000000000 | bytes 10000000 | tf_op jit(solution)/shard_map/stack_next/pallas_call | solution.py:339
  83.2 0.7 collective-permute-start.6
  83.9 2.1 %collective-permute-start.5 = (bf16[16,2176]{1,0:T(8,128)(2,1)S(1)}, bf16[16,2176]{1,0:T(8,128)(2,1)S(1)}, u32[]{:S(2)}, u32[]{:S(2)}) collective-permute-start(bf16[16,2176]{1,0:T(8,128)(2,1)S(1)} %get-tuple-element.26.p0_ref), channel_id=1, source_target_pairs={{0,2},{1,3},{2,0},{3,1},{4,6},{5,7},{6,4},{7,5},{8,10},{9,11},{10,... | collective-permute-start | bytes 208904 | tf_op jit(solution)/shard_map/ppermute | solution.py:437
  85.9 4.9 %shift_next.1 = (bf16[2048,512]{1,0:T(8,128)(2,1)S(1)}, f32[8,512]{1,0:T(8,128)S(1)}) custom-call(f32[4,2064,128]{2,1,0:T(8,128)S(1)} %get-tuple-element.27.xt_ref, f32[32,512]{1,0:T(8,128)S(1)} %get-tuple-element.28.side_ref), custom_call_target="tpu_custom_call" | custom-call | flops 6000000000 | bytes 20000000 | tf_op jit(solution)/shard_map/shift_next/pallas_call | solution.py:339
  90.9 0.6 collective-permute-done.4.p1_ref
  91.4 4.4 %correlate.3 = (bf16[16,2048]{1,0:T(8,128)(2,1)}, f32[16,128]{1,0:T(8,128)S(1)}) custom-call(bf16[16,2176]{1,0:T(8,128)(2,1)S(1)} %get-tuple-element.26.p0_ref, bf16[16,2176]{1,0:T(8,128)(2,1)S(1)} %collective-permute-done.4.p1_ref, bf16[16,2176]{1,0:T(8,128)(2,1)S(1)} %collective-permute-done.5.p2_ref, bf16[16,2176]{1,0:T(8,128)(2,1)S(1)} %collective-permute-done.6.p3_ref, ...), custom_call_target="tpu_custom_call" | custom-call | flops 4000000000 | bytes 10000000 | tf_op jit(solution)/shard_map/correlate/pallas_call | solution.py:411
  95.9 0.1 collective-permute-start.7
  96.0 1.2 %collective-permute-done.7.other_ref = f32[16,128]{1,0:T(8,128)S(1)} collective-permute-done((f32[16,128]{1,0:T(8,128)S(1)}, f32[16,128]{1,0:T(8,128)S(1)}, u32[]{:S(2)}, u32[]{:S(2)}) %collective-permute-start.7) | collective-permute-done | bytes 8224 | tf_op jit(solution)/shard_map/ppermute | solution.py:428
  97.2 17.1 %all_to_all.16.sums_ref = bf16[64,16,128]{2,1,0:T(8,128)(2,1)S(1)} all-to-all(bf16[64,16,128]{2,1,0:T(8,128)(2,1)S(1)} %spread.3), channel_id=1, replica_groups=mesh['y'=4,'x'=4,'core'=2,'off'=4] {'y','x','off'}, dimensions={0} | all-to-all | bytes 524288 | tf_op jit(solution)/shard_map/all_to_all | solution.py:433
  114.3 0.7 finish.1
  (14 shorter events, 0.2 us)
Async XLA Ops:
  4.8 11.2 %copy-start = (f32[8]{0:T(128)S(1)}, f32[8]{0:T(128)}, u32[]{:S(2)}) copy-start(f32[8]{0:T(128)} %param.16) | copy-start | bytes 100
  4.8 11.2 %copy-start.1 = (s32[2]{0:T(128)S(1)}, s32[2]{0:T(128)}, u32[]{:S(2)}) copy-start(s32[2]{0:T(128)} %param.17) | copy-start | bytes 28
  4.8 42.4 %all-to-all-start = ((bf16[128,4,2176]{2,1,0:T(4,128)(2,1)}), bf16[128,4,2176]{2,1,0:T(4,128)(2,1)S(1)}, u32[]{:S(2)}, u32[]{:S(2)}) async-start(bf16[128,4,2176]{2,1,0:T(4,128)(2,1)} %pack.1), calls=%async_computation | async-start | bytes 4456448 | tf_op jit(solution)/shard_map/all_to_all | solution.py:452
  48.6 8.6 %collective-permute-start.2 = (bf16[16,2176]{1,0:T(8,128)(2,1)S(1)}, bf16[16,2176]{1,0:T(8,128)(2,1)S(1)}, u32[]{:S(2)}, u32[]{:S(2)}) collective-permute-start(bf16[16,2176]{1,0:T(8,128)(2,1)S(1)} %get-tuple-element.22.p0_ref), channel_id=1, source_target_pairs={{0,3},{1,0},{2,1},{3,2},{4,7},{5,4},{6,5},{7,6},{8,11},{9,8},{10,9... | collective-permute-start | bytes 208904 | tf_op jit(solution)/shard_map/ppermute | solution.py:437
  49.8 7.5 %collective-permute-start.1 = (bf16[16,2176]{1,0:T(8,128)(2,1)S(1)}, bf16[16,2176]{1,0:T(8,128)(2,1)S(1)}, u32[]{:S(2)}, u32[]{:S(2)}) collective-permute-start(bf16[16,2176]{1,0:T(8,128)(2,1)S(1)} %get-tuple-element.22.p0_ref), channel_id=1, source_target_pairs={{0,2},{1,3},{2,0},{3,1},{4,6},{5,7},{6,4},{7,5},{8,10},{9,11},{10,... | collective-permute-start | bytes 208904 | tf_op jit(solution)/shard_map/ppermute | solution.py:437
  51.6 5.7 %collective-permute-start = (bf16[16,2176]{1,0:T(8,128)(2,1)S(1)}, bf16[16,2176]{1,0:T(8,128)(2,1)S(1)}, u32[]{:S(2)}, u32[]{:S(2)}) collective-permute-start(bf16[16,2176]{1,0:T(8,128)(2,1)S(1)} %get-tuple-element.22.p0_ref), channel_id=1, source_target_pairs={{0,1},{1,2},{2,3},{3,0},{4,5},{5,6},{6,7},{7,4},{8,9},{9,10},{10,1... | collective-permute-start | bytes 208904 | tf_op jit(solution)/shard_map/ppermute | solution.py:437
  61.5 1.3 %collective-permute-start.3 = (f32[32,128]{1,0:T(8,128)S(1)}, f32[32,128]{1,0:T(8,128)S(1)}, u32[]{:S(2)}, u32[]{:S(2)}) collective-permute-start(f32[32,128]{1,0:T(8,128)S(1)} %correlate.2.own_ref), channel_id=1, source_target_pairs={{0,4},{4,0},{1,5},{5,1},{2,6},{6,2},{3,7},{7,3},{8,12},{12,8},{9,1... | collective-permute-start | bytes 49160 | tf_op jit(solution)/shard_map/ppermute | solution.py:428
  83.2 7.7 %collective-permute-start.6 = (bf16[16,2176]{1,0:T(8,128)(2,1)S(1)}, bf16[16,2176]{1,0:T(8,128)(2,1)S(1)}, u32[]{:S(2)}, u32[]{:S(2)}) collective-permute-start(bf16[16,2176]{1,0:T(8,128)(2,1)S(1)} %get-tuple-element.26.p0_ref), channel_id=1, source_target_pairs={{0,3},{1,0},{2,1},{3,2},{4,7},{5,4},{6,5},{7,6},{8,11},{9,8},{10,9... | collective-permute-start | bytes 208904 | tf_op jit(solution)/shard_map/ppermute | solution.py:437
  83.9 7.0 %collective-permute-start.5 = (bf16[16,2176]{1,0:T(8,128)(2,1)S(1)}, bf16[16,2176]{1,0:T(8,128)(2,1)S(1)}, u32[]{:S(2)}, u32[]{:S(2)}) collective-permute-start(bf16[16,2176]{1,0:T(8,128)(2,1)S(1)} %get-tuple-element.26.p0_ref), channel_id=1, source_target_pairs={{0,2},{1,3},{2,0},{3,1},{4,6},{5,7},{6,4},{7,5},{8,10},{9,11},{10,... | collective-permute-start | bytes 208904 | tf_op jit(solution)/shard_map/ppermute | solution.py:437
  85.9 5.5 %collective-permute-start.4 = (bf16[16,2176]{1,0:T(8,128)(2,1)S(1)}, bf16[16,2176]{1,0:T(8,128)(2,1)S(1)}, u32[]{:S(2)}, u32[]{:S(2)}) collective-permute-start(bf16[16,2176]{1,0:T(8,128)(2,1)S(1)} %get-tuple-element.26.p0_ref), channel_id=1, source_target_pairs={{0,1},{1,2},{2,3},{3,0},{4,5},{5,6},{6,7},{7,4},{8,9},{9,10},{10,1... | collective-permute-start | bytes 208904 | tf_op jit(solution)/shard_map/ppermute | solution.py:437
  95.9 1.3 %collective-permute-start.7 = (f32[16,128]{1,0:T(8,128)S(1)}, f32[16,128]{1,0:T(8,128)S(1)}, u32[]{:S(2)}, u32[]{:S(2)}) collective-permute-start(f32[16,128]{1,0:T(8,128)S(1)} %get-tuple-element.31.own_ref), channel_id=1, source_target_pairs={{0,4},{4,0},{1,5},{5,1},{2,6},{6,2},{3,7},{7,3},{8,12},{12,8},{9,1... | collective-permute-start | bytes 24584 | tf_op jit(solution)/shard_map/ppermute | solution.py:428

commit v12 on v11

--- a/solution.py
+++ b/solution.py
@@ -250,7 +250,7 @@
                 energy = energy + (totals[h] * totals[h] + totals[h + 1] * totals[h + 1])
             return energy
 
-        energy = lax.fori_loop(0, NS // chunk, body, jnp.zeros((8, LANES), F32), unroll=8)
+        energy = lax.fori_loop(0, NS // chunk, body, jnp.zeros((8, LANES), F32), unroll=16)
         energies.append(jnp.sum(energy, axis=0, keepdims=True))
     energy_ref[...] = jnp.broadcast_to(jnp.concatenate(energies, axis=1), (8, SLOTS))
 

time: 115 us -> 115 us (level)
  no operation moved by 1% of the time
where the time goes in v12:
time: 115 us
  blocking collectives  36.2 us (31%)
  waiting for transfers between devices  33.6 us (29%)
  Pallas kernels  27 us (23%)
  starting transfers between devices  17.1 us (15%)
    all_to_all x2, blocking collectives, sum_copies(): lax.all_to_all(copies, ('y', 'x', 'off'), split_axis=0, concat_axis=0, ti...  36.2 us
    all_to_all x1, waiting for transfers between devices, on_device(): lax.all_to_all(outgoing, AXES, split_axis=0, concat_axis=0, tiled=True)  30.8 us
    pallas_call x7, Pallas kernels, call(): pl.pallas_call(kernel, out_shape=out, in_specs=[SMEM if space else VMEM f...  14.3 us
    all_to_all x1, starting transfers between devices, on_device(): lax.all_to_all(outgoing, AXES, split_axis=0, concat_axis=0, tiled=True)  11.2 us
    pallas_call x2, Pallas kernels, correlate(): pl.pallas_call(functools.partial(corr_kernel, first), out_shape=(sums,) i...  8.61 us
    ppermute x6, starting transfers between devices, exchange(): return (part, *[lax.ppermute(part, 'off', off_perm(d)) for d in (1, 2, 3)])  5.75 us
    pallas_call x1, Pallas kernels, pack(): pl.pallas_call(pack_kernel, out_shape=shape((DEVICES, TRACE_LIMIT, WIDE),...  4.15 us
    ppermute x2, waiting for transfers between devices, sum_copies(): other = lax.ppermute(value, 'core', [(0, 1), (1, 0)])  2.33 us
  transfers between devices with their start and end apart: 9, of which 4 were waited for; matrix products, arithmetic and copies ran while one was open for 0% of the time, Pallas kernels for 9%

profile of v12, /device:TPU:0, one launch (start us, length us, event | category | flops | bytes accessed | tf_op | source)
XLA Modules:
  0.0 115.2 jit_solution(8293099160218052660)
XLA Ops:
  0.6 4.2 %pack.1 = bf16[128,4,2176]{2,1,0:T(4,128)(2,1)} custom-call(s32[1,256]{1,0:T(1,128)} %bitcast.8, s32[1,256]{1,0:T(1,128)} %bitcast.9, s32[1,256]{1,0:T(1,128)} %bitcast.10, s32[1,256]{1,0:T(1,128)} %bitcast.11, s32[1,256]{1,0:T(1,128)} %bitcast.12, s32[1,256]{1,0:T(1,128)} %bitcast.13, bf16[256,2048]{1,0:T(8,128)(2,1)} %refs_6_.1), custom_call_target="tpu_custom_call" | custom-call | tf_op jit(solution)/shard_map/pack/pallas_call | solution.py:360
  4.8 11.2 %all-to-all-start = ((bf16[128,4,2176]{2,1,0:T(4,128)(2,1)}), bf16[128,4,2176]{2,1,0:T(4,128)(2,1)S(1)}, u32[]{:S(2)}, u32[]{:S(2)}) async-start(bf16[128,4,2176]{2,1,0:T(4,128)(2,1)} %pack.1), calls=%async_computation | async-start | bytes 4456448 | tf_op jit(solution)/shard_map/all_to_all | solution.py:452
  16.0 0.2 fusion
  16.2 0.1 broadcast_in_dim.22
  16.3 0.1 broadcast_in_dim.23
  16.3 30.8 %all-to-all-done.slots_ref = bf16[128,4,2176]{2,1,0:T(4,128)(2,1)S(1)} async-done(((bf16[128,4,2176]{2,1,0:T(4,128)(2,1)}), bf16[128,4,2176]{2,1,0:T(4,128)(2,1)S(1)}, u32[]{:S(2)}, u32[]{:S(2)}) %all-to-all-start) | async-done | bytes 2228256 | tf_op jit(solution)/shard_map/all_to_all | solution.py:452
  47.2 1.4 %stack_first.1 = (bf16[16,2176]{1,0:T(8,128)(2,1)S(1)}, f32[32,512]{1,0:T(8,128)S(1)}, bf16[512,2176]{1,0:T(8,128)(2,1)S(1)}, f32[16,128]{1,0:T(8,128)S(1)}) custom-call(f32[16,128]{1,0:T(8,128)S(1)} %broadcast_in_dim.24.damp_ref, bf16[128,4,2176]{2,1,0:T(4,128)(2,1)S(1)} %all-to-all-done.slots_ref), custom_call_target="tpu_custom_call" | custom-call | flops 3000000000 | bytes 10000000 | tf_op jit(solution)/shard_map/stack_first/pallas_call | solution.py:339
  48.6 1.2 %collective-permute-start.2 = (bf16[16,2176]{1,0:T(8,128)(2,1)S(1)}, bf16[16,2176]{1,0:T(8,128)(2,1)S(1)}, u32[]{:S(2)}, u32[]{:S(2)}) collective-permute-start(bf16[16,2176]{1,0:T(8,128)(2,1)S(1)} %get-tuple-element.22.p0_ref), channel_id=1, source_target_pairs={{0,3},{1,0},{2,1},{3,2},{4,7},{5,4},{6,5},{7,6},{8,11},{9,8},{10,9... | collective-permute-start | bytes 208904 | tf_op jit(solution)/shard_map/ppermute | solution.py:437
  49.8 1.8 %collective-permute-start.1 = (bf16[16,2176]{1,0:T(8,128)(2,1)S(1)}, bf16[16,2176]{1,0:T(8,128)(2,1)S(1)}, u32[]{:S(2)}, u32[]{:S(2)}) collective-permute-start(bf16[16,2176]{1,0:T(8,128)(2,1)S(1)} %get-tuple-element.22.p0_ref), channel_id=1, source_target_pairs={{0,2},{1,3},{2,0},{3,1},{4,6},{5,7},{6,4},{7,5},{8,10},{9,11},{10,... | collective-permute-start | bytes 208904 | tf_op jit(solution)/shard_map/ppermute | solution.py:437
  51.6 5.8 %shift_first.1 = (bf16[2048,512]{1,0:T(8,128)(2,1)S(1)}, f32[8,512]{1,0:T(8,128)S(1)}, f32[4,2064,128]{2,1,0:T(8,128)S(1)}) custom-call(bf16[512,2176]{1,0:T(8,128)(2,1)S(1)} %get-tuple-element.20.y_ref, f32[32,512]{1,0:T(8,128)S(1)} %get-tuple-element.21.side_ref.head_ref), custom_call_target="tpu_custom_call" | custom-call | flops 6000000000 | bytes 20000000 | tf_op jit(solution)/shard_map/shift_first/pallas_call | solution.py:339
  57.4 4.2 %correlate.2.own_ref = f32[32,128]{1,0:T(8,128)S(1)} custom-call(bf16[16,2176]{1,0:T(8,128)(2,1)S(1)} %get-tuple-element.22.p0_ref, bf16[16,2176]{1,0:T(8,128)(2,1)S(1)} %collective-permute-done.p1_ref, bf16[16,2176]{1,0:T(8,128)(2,1)S(1)} %collective-permute-done.1.p2_ref, bf16[16,2176]{1,0:T(8,128)(2,1)S(1)} %collective-permute-done.2.p3_ref, ...), custom_call_target="tpu_custom_call" | custom-call | flops 4000000000 | bytes 10000000 | tf_op jit(solution)/shard_map/correlate/pallas_call | solution.py:411
  61.6 0.1 collective-permute-start.3
  61.7 1.2 %collective-permute-done.3.other_ref = f32[32,128]{1,0:T(8,128)S(1)} collective-permute-done((f32[32,128]{1,0:T(8,128)S(1)}, f32[32,128]{1,0:T(8,128)S(1)}, u32[]{:S(2)}, u32[]{:S(2)}) %collective-permute-start.3) | collective-permute-done | bytes 16416 | tf_op jit(solution)/shard_map/ppermute | solution.py:428
  62.9 19.0 %all_to_all.15.sums_ref = bf16[64,24,128]{2,1,0:T(8,128)(2,1)S(1)} all-to-all(bf16[64,24,128]{2,1,0:T(8,128)(2,1)S(1)} %spread.2), channel_id=1, replica_groups=mesh['y'=4,'x'=4,'core'=2,'off'=4] {'y','x','off'}, dimensions={0} | all-to-all | bytes 786432 | tf_op jit(solution)/shard_map/all_to_all | solution.py:433
  81.9 1.4 %stack_next.1 = (bf16[16,2176]{1,0:T(8,128)(2,1)S(1)}, f32[32,512]{1,0:T(8,128)S(1)}, f32[32,128]{1,0:T(8,128)S(1)}) custom-call(f32[16,128]{1,0:T(8,128)S(1)} %get-tuple-element.19.damp_ref, bf16[512,2176]{1,0:T(8,128)(2,1)S(1)} %get-tuple-element.20.y_ref, f32[32,512]{1,0:T(8,128)S(1)} %get-tuple-element.21.side_ref.head_ref, ...), custom_call_target="tpu_custom_call" | custom-call | flops 3000000000 | bytes 10000000 | tf_op jit(solution)/shard_map/stack_next/pallas_call | solution.py:339
  83.3 0.7 collective-permute-start.6
  84.0 2.1 %collective-permute-start.5 = (bf16[16,2176]{1,0:T(8,128)(2,1)S(1)}, bf16[16,2176]{1,0:T(8,128)(2,1)S(1)}, u32[]{:S(2)}, u32[]{:S(2)}) collective-permute-start(bf16[16,2176]{1,0:T(8,128)(2,1)S(1)} %get-tuple-element.26.p0_ref), channel_id=1, source_target_pairs={{0,2},{1,3},{2,0},{3,1},{4,6},{5,7},{6,4},{7,5},{8,10},{9,11},{10,... | collective-permute-start | bytes 208904 | tf_op jit(solution)/shard_map/ppermute | solution.py:437
  86.0 5.0 %shift_next.1 = (bf16[2048,512]{1,0:T(8,128)(2,1)S(1)}, f32[8,512]{1,0:T(8,128)S(1)}) custom-call(f32[4,2064,128]{2,1,0:T(8,128)S(1)} %get-tuple-element.27.xt_ref, f32[32,512]{1,0:T(8,128)S(1)} %get-tuple-element.28.side_ref), custom_call_target="tpu_custom_call" | custom-call | flops 6000000000 | bytes 20000000 | tf_op jit(solution)/shard_map/shift_next/pallas_call | solution.py:339
  91.1 0.5 collective-permute-done.4.p1_ref
  91.6 4.4 %correlate.3 = (bf16[16,2048]{1,0:T(8,128)(2,1)}, f32[16,128]{1,0:T(8,128)S(1)}) custom-call(bf16[16,2176]{1,0:T(8,128)(2,1)S(1)} %get-tuple-element.26.p0_ref, bf16[16,2176]{1,0:T(8,128)(2,1)S(1)} %collective-permute-done.4.p1_ref, bf16[16,2176]{1,0:T(8,128)(2,1)S(1)} %collective-permute-done.5.p2_ref, bf16[16,2176]{1,0:T(8,128)(2,1)S(1)} %collective-permute-done.6.p3_ref, ...), custom_call_target="tpu_custom_call" | custom-call | flops 4000000000 | bytes 10000000 | tf_op jit(solution)/shard_map/correlate/pallas_call | solution.py:411
  96.0 0.1 collective-permute-start.7
  96.1 1.2 %collective-permute-done.7.other_ref = f32[16,128]{1,0:T(8,128)S(1)} collective-permute-done((f32[16,128]{1,0:T(8,128)S(1)}, f32[16,128]{1,0:T(8,128)S(1)}, u32[]{:S(2)}, u32[]{:S(2)}) %collective-permute-start.7) | collective-permute-done | bytes 8224 | tf_op jit(solution)/shard_map/ppermute | solution.py:428
  97.3 17.2 %all_to_all.16.sums_ref = bf16[64,16,128]{2,1,0:T(8,128)(2,1)S(1)} all-to-all(bf16[64,16,128]{2,1,0:T(8,128)(2,1)S(1)} %spread.3), channel_id=1, replica_groups=mesh['y'=4,'x'=4,'core'=2,'off'=4] {'y','x','off'}, dimensions={0} | all-to-all | bytes 524288 | tf_op jit(solution)/shard_map/all_to_all | solution.py:433
  114.5 0.7 finish.1
  (14 shorter events, 0.2 us)
Async XLA Ops:
  4.8 11.2 %copy-start = (f32[8]{0:T(128)S(1)}, f32[8]{0:T(128)}, u32[]{:S(2)}) copy-start(f32[8]{0:T(128)} %param.16) | copy-start | bytes 100
  4.8 11.2 %copy-start.1 = (s32[2]{0:T(128)S(1)}, s32[2]{0:T(128)}, u32[]{:S(2)}) copy-start(s32[2]{0:T(128)} %param.17) | copy-start | bytes 28
  4.8 42.4 %all-to-all-start = ((bf16[128,4,2176]{2,1,0:T(4,128)(2,1)}), bf16[128,4,2176]{2,1,0:T(4,128)(2,1)S(1)}, u32[]{:S(2)}, u32[]{:S(2)}) async-start(bf16[128,4,2176]{2,1,0:T(4,128)(2,1)} %pack.1), calls=%async_computation | async-start | bytes 4456448 | tf_op jit(solution)/shard_map/all_to_all | solution.py:452
  48.6 8.7 %collective-permute-start.2 = (bf16[16,2176]{1,0:T(8,128)(2,1)S(1)}, bf16[16,2176]{1,0:T(8,128)(2,1)S(1)}, u32[]{:S(2)}, u32[]{:S(2)}) collective-permute-start(bf16[16,2176]{1,0:T(8,128)(2,1)S(1)} %get-tuple-element.22.p0_ref), channel_id=1, source_target_pairs={{0,3},{1,0},{2,1},{3,2},{4,7},{5,4},{6,5},{7,6},{8,11},{9,8},{10,9... | collective-permute-start | bytes 208904 | tf_op jit(solution)/shard_map/ppermute | solution.py:437
  49.8 7.6 %collective-permute-start.1 = (bf16[16,2176]{1,0:T(8,128)(2,1)S(1)}, bf16[16,2176]{1,0:T(8,128)(2,1)S(1)}, u32[]{:S(2)}, u32[]{:S(2)}) collective-permute-start(bf16[16,2176]{1,0:T(8,128)(2,1)S(1)} %get-tuple-element.22.p0_ref), channel_id=1, source_target_pairs={{0,2},{1,3},{2,0},{3,1},{4,6},{5,7},{6,4},{7,5},{8,10},{9,11},{10,... | collective-permute-start | bytes 208904 | tf_op jit(solution)/shard_map/ppermute | solution.py:437
  51.6 5.8 %collective-permute-start = (bf16[16,2176]{1,0:T(8,128)(2,1)S(1)}, bf16[16,2176]{1,0:T(8,128)(2,1)S(1)}, u32[]{:S(2)}, u32[]{:S(2)}) collective-permute-start(bf16[16,2176]{1,0:T(8,128)(2,1)S(1)} %get-tuple-element.22.p0_ref), channel_id=1, source_target_pairs={{0,1},{1,2},{2,3},{3,0},{4,5},{5,6},{6,7},{7,4},{8,9},{9,10},{10,1... | collective-permute-start | bytes 208904 | tf_op jit(solution)/shard_map/ppermute | solution.py:437
  61.6 1.3 %collective-permute-start.3 = (f32[32,128]{1,0:T(8,128)S(1)}, f32[32,128]{1,0:T(8,128)S(1)}, u32[]{:S(2)}, u32[]{:S(2)}) collective-permute-start(f32[32,128]{1,0:T(8,128)S(1)} %correlate.2.own_ref), channel_id=1, source_target_pairs={{0,4},{4,0},{1,5},{5,1},{2,6},{6,2},{3,7},{7,3},{8,12},{12,8},{9,1... | collective-permute-start | bytes 49160 | tf_op jit(solution)/shard_map/ppermute | solution.py:428
  83.3 7.8 %collective-permute-start.6 = (bf16[16,2176]{1,0:T(8,128)(2,1)S(1)}, bf16[16,2176]{1,0:T(8,128)(2,1)S(1)}, u32[]{:S(2)}, u32[]{:S(2)}) collective-permute-start(bf16[16,2176]{1,0:T(8,128)(2,1)S(1)} %get-tuple-element.26.p0_ref), channel_id=1, source_target_pairs={{0,3},{1,0},{2,1},{3,2},{4,7},{5,4},{6,5},{7,6},{8,11},{9,8},{10,9... | collective-permute-start | bytes 208904 | tf_op jit(solution)/shard_map/ppermute | solution.py:437
  84.0 7.1 %collective-permute-start.5 = (bf16[16,2176]{1,0:T(8,128)(2,1)S(1)}, bf16[16,2176]{1,0:T(8,128)(2,1)S(1)}, u32[]{:S(2)}, u32[]{:S(2)}) collective-permute-start(bf16[16,2176]{1,0:T(8,128)(2,1)S(1)} %get-tuple-element.26.p0_ref), channel_id=1, source_target_pairs={{0,2},{1,3},{2,0},{3,1},{4,6},{5,7},{6,4},{7,5},{8,10},{9,11},{10,... | collective-permute-start | bytes 208904 | tf_op jit(solution)/shard_map/ppermute | solution.py:437
  86.0 5.5 %collective-permute-start.4 = (bf16[16,2176]{1,0:T(8,128)(2,1)S(1)}, bf16[16,2176]{1,0:T(8,128)(2,1)S(1)}, u32[]{:S(2)}, u32[]{:S(2)}) collective-permute-start(bf16[16,2176]{1,0:T(8,128)(2,1)S(1)} %get-tuple-element.26.p0_ref), channel_id=1, source_target_pairs={{0,1},{1,2},{2,3},{3,0},{4,5},{5,6},{6,7},{7,4},{8,9},{9,10},{10,1... | collective-permute-start | bytes 208904 | tf_op jit(solution)/shard_map/ppermute | solution.py:437
  96.0 1.3 %collective-permute-start.7 = (f32[16,128]{1,0:T(8,128)S(1)}, f32[16,128]{1,0:T(8,128)S(1)}, u32[]{:S(2)}, u32[]{:S(2)}) collective-permute-start(f32[16,128]{1,0:T(8,128)S(1)} %get-tuple-element.31.own_ref), channel_id=1, source_target_pairs={{0,4},{4,0},{1,5},{5,1},{2,6},{6,2},{3,7},{7,3},{8,12},{12,8},{9,1... | collective-permute-start | bytes 24584 | tf_op jit(solution)/shard_map/ppermute | solution.py:428
